TPU v7x, 512 devices: a whole 4x4x16 slice. The times are simulated.
512 devices in a mesh: dp: 64 (over y_hi, z, core), tensor: 8 (over x, y_lo).
Axes of the slice: x: 4, y: 4 (y_hi: 2, y_lo: 2; y = y_hi * 2 + y_lo), z: 16, core: 2. Of those that a mesh axis runs over, the one named last changes fastest.
Arguments:
- hidden: bfloat16 [8192, 5120], P('dp'), may hold values from -6 to 6
- qkv_weight: bfloat16 [5120, 6144], P(('dp', 'tensor')), may hold values from -0.078125 to 0.078125
- query_gain: float32 [128], replicated, may hold values from 0.1 to 1.9
- key_gain: float32 [128], replicated, may hold values from 0.1 to 1.9
- positions: int32 [8192], replicated, may hold values from 0 to 32767, as said below
- block_mask: int32 [64, 64], replicated, may hold values from 0 to 1, as said below
Outputs:
- keys: bfloat16 [8192, 1024], P('dp', 'tensor')
- values: bfloat16 [8192, 1024], P('dp', 'tensor')
- context: bfloat16 [8192, 4096], P('dp', 'tensor')
Inputs may be any that keep to these rules, and one draw needn't show every extreme that they name: `positions`: strictly increasing; position 4 i + r with 0 <= r < 4 for the i-th surviving token; the first is 0 and the last 32767. `block_mask`: 1 on the diagonal, 0 above it.
All inputs are finite; a program needn't handle non-finite values.
Results may differ from a plain program's by a relative error of at most 0.0069.
Values may be sent and summed in bfloat16 or wider, within the bound.
No kernel may reach another device: no remote copies, remote signals or barrier semaphores. Data moves between devices by JAX's collectives and lax.ppermute only.
A program may use at most 64 MiB of HBM per device.

v0:
```python
import math

import jax
import jax.numpy as jnp
from jax import lax
from jax.sharding import PartitionSpec as P

HD = 128
BLOCK = 128
GQ = 4


def head_norm(inputs, gain):
    meansq = jnp.mean(inputs * inputs, axis=-1, keepdims=True)
    return inputs * lax.rsqrt(meansq + 1e-06) * gain


def rotate(inputs, token_pos):
    halfway = inputs.shape[-1] // 2
    inverse = 1000000.0 ** (-(jnp.arange(halfway, dtype=jnp.float32) * 2.0) / inputs.shape[-1])
    angles = token_pos.astype(jnp.float32)[:, None] * inverse[None, :]
    angles = angles.reshape((angles.shape[0],) + (1,) * (inputs.ndim - 2) + (halfway,))
    cosine = jnp.cos(angles)
    sine = jnp.sin(angles)
    first = inputs[..., :halfway]
    second = inputs[..., halfway:]
    return jnp.concatenate(
        [first * cosine - second * sine, second * cosine + first * sine], axis=-1
    )


def local(hidden, qkv_weight, query_gain, key_gain, positions, block_mask):
    tensor_count = lax.axis_size("tensor")
    dp_count = lax.axis_size("dp")
    tensor_idx = lax.axis_index("tensor")
    dp_idx = lax.axis_index("dp")
    tok_rows = hidden.shape[0]
    feat_width = hidden.shape[1]
    all_cols = qkv_weight.shape[1]
    local_cols = all_cols // tensor_count
    row_share = feat_width // (dp_count * tensor_count)
    strided = lax.dynamic_index_in_dim(
        hidden.reshape(tok_rows, dp_count, tensor_count, row_share), tensor_idx, 2, keepdims=False
    )
    strided = strided.reshape(tok_rows, dp_count * row_share)
    partial_sums = jnp.dot(
        strided,
        lax.all_gather(qkv_weight, "dp", axis=0, tiled=True),
        preferred_element_type=jnp.float32,
    )
    project = lax.psum_scatter(partial_sums, "tensor", scatter_dimension=1, tiled=True)
    groups = local_cols // ((GQ + 2) * HD)
    project = project.reshape(tok_rows, groups, GQ + 2, HD)
    first_row = dp_idx * tok_rows
    own_pos = lax.dynamic_slice_in_dim(positions, first_row, tok_rows, 0)
    queries = rotate(head_norm(project[:, :, :GQ], query_gain), own_pos).astype(jnp.bfloat16)
    keys = rotate(head_norm(project[:, :, GQ], key_gain), own_pos).astype(jnp.bfloat16)
    values = project[:, :, GQ + 1].astype(jnp.bfloat16)
    own_blocks = tok_rows // BLOCK
    mask_rows = lax.dynamic_slice_in_dim(block_mask, dp_idx * own_blocks, own_blocks, 0)
    mask_rows = jnp.repeat(mask_rows, BLOCK, axis=0)
    scaling = 1.0 / math.sqrt(HD)
    key_part = lax.all_gather(keys, "dp", axis=0, tiled=True)
    value_part = lax.all_gather(values, "dp", axis=0, tiled=True)
    block_live = mask_rows
    block_live = jnp.repeat(block_live, BLOCK, axis=1) == 1
    live = block_live & (positions[None, :] <= own_pos[:, None])
    scores = (
        jnp.einsum("qgjd,kgd->qgjk", queries, key_part, preferred_element_type=jnp.float32)
        * scaling
    )
    weights = jnp.where(live[:, None, None, :], jnp.exp(scores), 0.0)
    numer = jnp.einsum(
        "qgjk,kgd->qgjd",
        weights.astype(jnp.bfloat16),
        value_part,
        preferred_element_type=jnp.float32,
    )
    denom = jnp.sum(weights, axis=-1)
    numer, denom = (numer, denom)
    context = (numer / denom[..., None]).astype(jnp.bfloat16).reshape(tok_rows, groups * GQ * HD)
    return (keys.reshape(tok_rows, groups * HD), values.reshape(tok_rows, groups * HD), context)


def solution(mesh):
    return jax.shard_map(
        local,
        mesh=mesh,
        in_specs=(P("dp", None), P(("dp", "tensor"), None), P(), P(), P(), P()),
        out_specs=(P("dp", "tensor"), P("dp", "tensor"), P("dp", "tensor")),
        check_vma=False,
    )
```

profile of v0, /device:TPU:1, one launch (start us, length us, event | category | flops | bytes accessed | tf_op | source)
XLA Modules:
  0.0 590.5 jit_solution(178004589857050419)
XLA Ops:
  7.2 0.7 all-gather.10.cloned.1.call-update
  7.9 1.8 copy.22
  9.7 0.4 reshape.378
  10.2 0.1 reshape.379
  10.3 187.0 %all-gather.10.cloned.1.call-done = bf16[64,10,6144]{2,1,0:T(8,128)(2,1)} async-done(((bf16[1,10,6144]{2,1,0:T(8,128)(2,1)}), bf16[64,10,6144]{2,1,0:T(8,128)(2,1)}) %all-gather.10.cloned.1.call-update) | async-done | bytes 7864336 | tf_op jit(solution)/shard_map/all_gather | solution.py:48
  197.3 13.8 %reshape.388 = bf16[640,6144]{1,0:T(8,128)(2,1)} reshape(bf16[64,10,6144]{2,1,0:T(8,128)(2,1)} %all-gather.10.cloned.1.call-done) | data formatting | bytes 15728640
  211.1 6.3 %fusion.43 = f32[128,6144]{1,0:T(8,128)} fusion(bf16[128,640]{0,1:T(8,128)(2,1)S(1)} %reshape.379, bf16[640,6144]{1,0:T(8,128)(2,1)} %reshape.388), kind=kOutput, calls=%fused_computation.52 | convolution fusion | flops 1006632960 | bytes 11173888 | tf_op jit(solution)/shard_map/dot_general | solution.py:46
  217.4 0.0 all-gather.6.cloned.1.call-start
  217.5 0.1 fusion.42
  217.6 72.3 %reduce-scatter.2.cloned.1.call-done = f32[128,768]{1,0:T(8,128)} async-done(((f32[128,6144]{1,0:T(8,128)}), f32[128,768]{1,0:T(8,128)}) %reduce-scatter.2.cloned.1.call-update) | async-done | bytes 393232 | tf_op jit(solution)/shard_map/reduce_scatter | solution.py:51
  289.9 1.1 copy.23
  291.0 0.1 copy.30
  291.1 0.1 fusion.37
  291.3 0.1 fusion.38
  291.4 0.3 fusion.34
  291.7 0.7 pad_maximum_fusion.1
  292.5 0.7 compare_bitcast_fusion
  293.2 0.6 slice.52
  293.8 0.1 broadcast_bitcast_fusion
  293.9 0.3 multiply_cosine_fusion
  294.2 2.8 compare_and_fusion
  297.0 0.1 copy.31
  297.1 0.7 copy.27
  297.8 0.7 pad_maximum_fusion
  298.5 0.1 multiply_reduce_fusion
  298.7 0.1 multiply_multiply_fusion
  298.9 0.1 fusion.24
  299.0 140.6 %all-gather.6.cloned.1.call-done = bf16[8192,1,128]{2,0,1:T(8,128)(2,1)} async-done(((bf16[128,1,128]{2,0,1:T(8,128)(2,1)}), bf16[8192,1,128]{2,0,1:T(8,128)(2,1)}) %all-gather.6.cloned.1.call-update) | async-done | bytes 2097168 | tf_op jit(solution)/shard_map/all_gather | solution.py:63
  439.6 9.6 %fusion = (f32[128,4]{0,1:T(4,128)S(1)}, f32[8192,128,4]{1,0,2:T(8,128)}) fusion(pred[128,8192]{0,1:T(8,128)(4,1)S(1)} %compare_and_fusion, bf16[128,4,64]{2,0,1:T(8,128)(2,1)S(1)} %get-tuple-element.15, bf16[128,4,64]{2,0,1:T(8,128)(2,1)S(1)} %get-tuple-element.14, bf16[8192,1,128]{2,0,1:T(8,128)(2,1)} %all-gather.6.cloned.1.call-done), kind=kOutput, calls=%fused_computation.1 | convolution fusion | flops 1086586368 | bytes 20056064 | tf_op jit(solution)/shard_map/qgjd,kgd->qgjk/dot_general | solution.py:69
  449.2 125.0 %all-gather.8.cloned.1.call-done = bf16[8192,1,1,128]{0,3,2,1:T(8,128)(2,1)} async-done(((bf16[128,1,1,128]{0,3,2,1:T(8,128)(2,1)}), bf16[8192,1,1,128]{0,3,2,1:T(8,128)(2,1)}) %all-gather.8.cloned.1.call-update) | async-done | bytes 2097168 | tf_op jit(solution)/shard_map/all_gather | solution.py:64
  574.2 9.0 %fusion.19 = bf16[1,128,128,4]{2,1,3,0:T(8,128)(2,1)S(1)} fusion(f32[8192,128,4]{1,0,2:T(8,128)} %get-tuple-element.21, pred[128,8192]{0,1:T(8,128)(4,1)S(1)} %compare_and_fusion, bf16[8192,1,1,128]{0,3,2,1:T(8,128)(2,1)} %all-gather.8.cloned.1.call-done, f32[128,4]{0,1:T(4,128)S(1)} %get-tuple-element.20), kind=kOutput, calls=%fused_computation.12 | convolution fusion | flops 1086455808 | bytes 20056064 | tf_op jit(solution)/shard_map/qgjk,kgd->qgjd/dot_general | solution.py:73
  583.2 0.8 copy.28
  (19 shorter events, 0.3 us)
Async XLA Ops:
  7.2 190.1 %all-gather.10.cloned.1.call-start = ((), (), s32[]{:S(2)}) async-start(), calls=%async_computation.4 | async-start | bytes 12779520 | tf_op jit(solution)/shard_map/all_gather | solution.py:48
  7.9 282.0 %reduce-scatter.2.cloned.1.call-start = ((), (), s32[]{:S(2)}) async-start(), calls=%async_computation.1 | async-start | bytes 3538944 | tf_op jit(solution)/shard_map/reduce_scatter | solution.py:51
  211.1 6.5 %copy-start = (s32[8192]{0:T(1024)S(1)}, s32[8192]{0:T(1024)}, u32[]{:S(2)}) copy-start(s32[8192]{0:T(1024)} %param.10) | copy-start | bytes 98308
  211.1 80.2 %copy-start.1 = (f32[128]{0:T(128)S(1)}, f32[128]{0:T(128)}, u32[]{:S(2)}) copy-start(f32[128]{0:T(128)} %param.9) | copy-start | bytes 1540
  211.1 87.6 %copy-start.2 = (f32[128]{0:T(128)S(1)}, f32[128]{0:T(128)}, u32[]{:S(2)}) copy-start(f32[128]{0:T(128)} %param.8) | copy-start | bytes 1540
  217.4 222.2 %all-gather.6.cloned.1.call-start = ((), (), s32[]{:S(2)}) async-start(), calls=%async_computation.2 | async-start | bytes 2129920 | tf_op jit(solution)/shard_map/all_gather | solution.py:63
  292.4 281.7 %all-gather.8.cloned.1.call-start = ((), (), s32[]{:S(2)}) async-start(), calls=%async_computation.3 | async-start | bytes 2129920 | tf_op jit(solution)/shard_map/all_gather | solution.py:64
Sparse Core Ops, SparseCore 0:
  11.3 185.9 all-gather.9
  217.6 72.2 reduce-scatter.1
  293.7 145.8 all-gather.5
  442.5 131.6 all-gather.7
where the time goes:
time: 591 us; the launch traced here: 590 us
  waiting for transfers between devices  526 us (89%)
  matrix products  24.9 us (4%)
  local copies, waits for them, and re-layouts  19.7 us (3%)
  between operations  13.9 us (2%)
  other arithmetic  6.2 us (1%)
    all_gather x1, waiting for transfers between devices, local(): lax.all_gather(qkv_weight, 'dp', axis=0, tiled=True)  187 us
    all_gather x1, waiting for transfers between devices, local(): key_part = lax.all_gather(keys, 'dp', axis=0, tiled=True)  141 us
    all_gather x1, waiting for transfers between devices, local(): value_part = lax.all_gather(values, 'dp', axis=0, tiled=True)  125 us
    reduce_scatter x1, waiting for transfers between devices, local(): lax.psum_scatter(partial_sums, 'tensor', scatter_dimension=1, tiled=True)  72.3 us
    unnamed x12, local copies, waits for them, and re-layouts  17.3 us
  transfers between devices with their start and end apart: 4, of which 4 were waited for; matrix products, arithmetic and copies ran while one was open for 3% of the time, Pallas kernels for 0%

commit v1 on v0

v1 whole, which is shorter than its diff:
```python
import functools
import math

import jax
import jax.numpy as jnp
from jax import lax
from jax.experimental import pallas as pl
from jax.experimental.pallas import tpu as pltpu
from jax.sharding import Mesh, PartitionSpec as P

HD = 128
BLOCK = 128
GQ = 4
KV = 8
YH, ZH, ZL, CORE, X, YL = 2, 4, 4, 2, 4, 2
NZ = ZH * ZL
GROUP = YH * CORE
DP = ("yh", "zh", "zl", "c")
TENSOR = ("x", "yl")
Z = ("zh", "zl")
bf16 = jnp.bfloat16
f32 = jnp.float32


def params():
    return pltpu.CompilerParams(vmem_limit_bytes=40 * 1024 * 1024)


def swap(inputs, axis):
    return lax.ppermute(inputs, axis, [(0, 1), (1, 0)])


def from_z(inputs, offset):
    return lax.ppermute(inputs, Z, [(i, (i - offset) % NZ) for i in range(NZ)])


def norm_rope(inputs, gain, cosine, sine):
    meansq = jnp.mean(inputs * inputs, axis=-1, keepdims=True)
    normed = inputs * lax.rsqrt(meansq + 1e-06) * gain
    return normed * cosine + pltpu.roll(normed, HD // 2, 1) * sine


def kv_partial_kernel(place, h0, h1, h2, h3, weight, out):
    member = place[1]
    for rel, rows in enumerate((h0, h1, h2, h3)):
        out[member ^ rel] = jnp.dot(rows[...], weight[...], preferred_element_type=f32)


def kv_partial(place, hiddens, weight):
    tok, depth = hiddens[0].shape
    half = depth // YH
    rows = pl.BlockSpec((tok, half), lambda i, place: (0, place[0]))
    return pl.pallas_call(
        kv_partial_kernel,
        grid_spec=pltpu.PrefetchScalarGridSpec(
            num_scalar_prefetch=1,
            grid=(1,),
            in_specs=[rows] * GROUP + [pl.BlockSpec((half, HD), lambda i, place: (0, 0))],
            out_specs=pl.BlockSpec((GROUP, tok, HD), lambda i, place: (0, 0, 0)),
        ),
        out_shape=jax.ShapeDtypeStruct((GROUP, tok, HD), f32),
        compiler_params=params(),
        name="kv_partial",
    )(place, *hiddens, weight)


def kv_finish_kernel(parts, gain, cosine, sine, keys, values, both):
    key = norm_rope(parts[0] + parts[2], gain[...], cosine[0], sine[0]).astype(bf16)
    value = (parts[1] + parts[3]).astype(bf16)
    keys[...] = key
    values[...] = value
    both[:, :HD] = key
    both[:, HD:] = value


def kv_finish(parts, gain, cosine, sine):
    tok = parts.shape[1]
    return pl.pallas_call(
        kv_finish_kernel,
        out_shape=(
            jax.ShapeDtypeStruct((tok, HD), bf16),
            jax.ShapeDtypeStruct((tok, HD), bf16),
            jax.ShapeDtypeStruct((tok, 2 * HD), bf16),
        ),
        compiler_params=params(),
        name="kv_finish",
    )(parts, gain, cosine, sine)


def q_project_kernel(place, h0, h1, h2, h3, weight, gain, cosine, sine, out):
    member = place[1]
    half = h0.shape[1] // YH
    for rel, rows in enumerate((h0, h1, h2, h3)):
        total = None
        for yh in range(YH):
            part = jnp.dot(
                rows[:, yh * half : (yh + 1) * half],
                weight[:, yh].reshape(half, HD),
                preferred_element_type=f32,
            )
            total = part if total is None else total + part
        out[member ^ rel] = norm_rope(total, gain[...], cosine[rel], sine[rel]).astype(bf16)


def q_project(place, hiddens, weight, gain, cosine, sine):
    tok, depth = hiddens[0].shape

    def whole(shape):
        return pl.BlockSpec(shape, lambda i, place: (0,) * len(shape))

    return pl.pallas_call(
        q_project_kernel,
        grid_spec=pltpu.PrefetchScalarGridSpec(
            num_scalar_prefetch=1,
            grid=(1,),
            in_specs=[whole((tok, depth))] * GROUP
            + [whole(weight.shape), whole(gain.shape), whole(cosine.shape), whole(sine.shape)],
            out_specs=whole((GROUP, tok, HD)),
        ),
        out_shape=jax.ShapeDtypeStruct((GROUP, tok, HD), bf16),
        compiler_params=params(),
        name="q_project",
    )(place, *hiddens, weight, gain, cosine, sine)


CHUNK = 2 * BLOCK
CHUNKS = [
    (0, 0, 0, 0),
    (0, CHUNK, 0, 2),
    (1, 0, 1, 0),
    (1, CHUNK, 1, 2),
    (2, 0, -1, 0),
    (2, CHUNK, -1, 2),
    (3, 0, 2, 0),
    (4, 0, 2, 2),
]


def attend_kernel(place, block_mask, query, kv0, kv1, kv2, kv3, kv4, out, numer, total):
    group = pl.program_id(0)
    yh, zh, zl, core = place[0], place[2], place[3], place[4]
    query_block = (group // CORE) * (NZ * CORE) + (zh * ZL + zl) * CORE + lax.rem(group, CORE)
    rows = query[...].reshape(GQ * BLOCK, HD)
    ahead = lax.broadcasted_iota(jnp.int32, (GQ * BLOCK, BLOCK), 1) - lax.rem(
        lax.broadcasted_iota(jnp.int32, (GQ * BLOCK, BLOCK), 0), BLOCK
    )
    numer[...] = jnp.zeros_like(numer)
    total[...] = jnp.zeros_like(total)
    refs = (kv0, kv1, kv2, kv3, kv4)
    for which, start, offset, zh0 in CHUNKS:
        limits = []
        for i in range(CHUNK // BLOCK):
            z_at = (zh0 + i) * ZL + lax.rem(zl + offset + ZL, ZL)
            key_block = yh * (NZ * CORE) + z_at * CORE + core
            live = (block_mask[query_block, key_block] == 1) & (key_block <= query_block)
            limits.append(
                jnp.where(live, jnp.where(key_block == query_block, 0, 2 * BLOCK), -2 * BLOCK)
            )

        @pl.when(jnp.maximum(limits[0], limits[1]) >= 0)
        def _(which=which, start=start, limits=limits):
            keys = refs[which][start : start + CHUNK, :HD]
            values = refs[which][start : start + CHUNK, HD:]
            scores = lax.dot_general(
                rows, keys, (((1,), (1,)), ((), ())), preferred_element_type=f32
            )
            raised = jnp.exp(scores * (1.0 / math.sqrt(HD)))
            parts = [
                jnp.where(ahead <= limits[i], raised[:, i * BLOCK : (i + 1) * BLOCK], 0.0)
                for i in range(CHUNK // BLOCK)
            ]
            total[...] += parts[0] + parts[1]
            weights = jnp.concatenate([p.astype(bf16) for p in parts], axis=1)
            numer[...] += jnp.dot(weights, values, preferred_element_type=f32)

    denom = jnp.sum(total[...], axis=1, keepdims=True)
    lane = lax.broadcasted_iota(jnp.int32, (BLOCK, HD), 1)
    tail = jnp.zeros((BLOCK, HD), f32)
    for head in range(GQ):
        mine = denom[head * BLOCK : (head + 1) * BLOCK]
        high = mine.astype(bf16).astype(f32)
        tail = jnp.where(lane == 2 * head, high, tail)
        tail = jnp.where(lane == 2 * head + 1, mine - high, tail)
        out[0, :, head * HD : (head + 1) * HD] = numer[
            head * BLOCK : (head + 1) * BLOCK
        ].astype(bf16)
    out[0, :, GQ * HD :] = tail.astype(bf16)


def attend(place, block_mask, query, gathered):
    tok = query.shape[2]
    rows = GQ * tok
    width = (GQ + 1) * HD

    def whole(array):
        return pl.BlockSpec(array.shape, lambda i, *_: (0,) * array.ndim)

    return pl.pallas_call(
        attend_kernel,
        grid_spec=pltpu.PrefetchScalarGridSpec(
            num_scalar_prefetch=2,
            grid=(GROUP,),
            in_specs=[pl.BlockSpec((GQ, 1, tok, HD), lambda i, *_: (0, i, 0, 0))]
            + [whole(a) for a in gathered],
            out_specs=pl.BlockSpec((1, tok, width), lambda i, *_: (i, 0, 0)),
            scratch_shapes=[pltpu.VMEM((rows, HD), f32), pltpu.VMEM((rows, BLOCK), f32)],
        ),
        out_shape=jax.ShapeDtypeStruct((GROUP, tok, width), bf16),
        compiler_params=params(),
        name="attend",
    )(place, block_mask, query, *gathered)


def combine_kernel(parts, out):
    tail = sum(parts[i, :, GQ * HD :].astype(f32) for i in range(GROUP))
    for head in range(GQ):
        at = slice(head * HD, (head + 1) * HD)
        numer = sum(parts[i, :, at].astype(f32) for i in range(GROUP))
        denom = tail[:, 2 * head : 2 * head + 1] + tail[:, 2 * head + 1 : 2 * head + 2]
        out[:, at] = (numer / denom).astype(bf16)


def combine(parts):
    return pl.pallas_call(
        combine_kernel,
        out_shape=jax.ShapeDtypeStruct((parts.shape[1], GQ * HD), bf16),
        compiler_params=params(),
        name="combine",
    )(parts)


def local(hidden, qkv_weight, query_gain, key_gain, positions, block_mask):
    tok, depth = hidden.shape
    share = qkv_weight.shape[0]
    yh, zh, zl, core = (lax.axis_index(a) for a in DP)
    member = yh * CORE + core
    place = jnp.stack([yh, member, zh, zl, core]).astype(jnp.int32)

    near = swap(hidden, "c")

    with jax.named_scope("weights"):
        split = qkv_weight.reshape(share, KV, GQ + 2, HD).transpose(2, 1, 0, 3)
        send = jnp.concatenate(
            [split[:GQ], jnp.concatenate([split[GQ:]] * YH, axis=0)], axis=-1
        ).reshape(GROUP * KV, share, 2 * HD)
        got = lax.all_to_all(send, ("yh", "c", "x", "yl"), 0, 0)
        rows = CORE * KV * share
        got, sent = lax.optimization_barrier((got, hidden))
        far = swap(sent, "yh")
        q_rows = got[:, :, :HD].reshape(YH * rows, HD)
        kv_rows = lax.dynamic_index_in_dim(
            got.reshape(YH, CORE * KV, share, 2 * HD), yh, 0, keepdims=False
        )[:, :, HD:].reshape(rows, HD)
        q_weight = lax.all_gather(q_rows, Z, axis=0, tiled=False)
        q_weight = q_weight.reshape(NZ, YH, rows, HD)
        kv_weight = lax.all_gather(kv_rows, Z, axis=0, tiled=True)

    far, _ = lax.optimization_barrier((far, kv_weight))
    hiddens = (hidden, near, far, swap(far, "c"))

    inverse = 1000000.0 ** (-(jnp.arange(HD // 2, dtype=f32) * 2.0) / HD)
    own = []
    for rel in range(GROUP):
        first = ((yh ^ (rel // CORE)) * NZ + zh * ZL + zl) * CORE + (core ^ (rel % CORE))
        own.append(lax.dynamic_slice_in_dim(positions, first * tok, tok, 0))
    angles = jnp.stack(own).astype(f32)[:, :, None] * inverse
    cosine, sine = jnp.cos(angles), jnp.sin(angles)
    cosine = jnp.concatenate([cosine, cosine], axis=-1)
    sine = jnp.concatenate([-sine, sine], axis=-1)

    with jax.named_scope("keys_values"):
        parts = kv_partial(place, hiddens, kv_weight)
        parts = lax.all_to_all(parts, ("yh", "c"), 0, 0)
        keys, values, both = kv_finish(parts, key_gain.reshape(1, HD), cosine, sine)
        line = lax.all_gather(both, "zh", axis=0, tiled=True)
        half = line.shape[0] // 2
        gathered = (
            line,
            from_z(line, 1),
            from_z(line, -1),
            from_z(line[:half], 2),
            from_z(line[half:], -2),
        )

    with jax.named_scope("queries"):
        q_weight, _ = lax.optimization_barrier((q_weight, line))
        query = q_project(place, hiddens, q_weight, query_gain.reshape(1, HD), cosine, sine)
        query = lax.all_gather(query, ("yh", "c"), axis=0, tiled=False)

    with jax.named_scope("context"):
        partial = attend(place, block_mask, query, gathered)
        partial = lax.all_to_all(partial, ("yh", "c"), 0, 0)
        context = combine(partial)
    return keys, values, context


def solution(mesh):
    fine = Mesh(mesh.devices.reshape(YH, ZH, ZL, CORE, X, YL), DP[:3] + ("c",) + TENSOR)
    return jax.shard_map(
        local,
        mesh=fine,
        in_specs=(P(DP, None), P(DP + TENSOR, None), P(), P(), P(), P()),
        out_specs=(P(DP, TENSOR), P(DP, TENSOR), P(DP, TENSOR)),
        check_vma=False,
    )
```

time: 591 us -> 171 us (0.29)
  waiting for transfers between devices: 526 us -> 7.26 us
  blocking collectives: 0 us -> 98 us
  starting transfers between devices: 0.16 us -> 26.6 us
  matrix products: 24.9 us -> 0 us
  Pallas kernels: 0 us -> 17.5 us
  local copies, waits for them, and re-layouts: 19.7 us -> 5.06 us
    all_gather x3 -> x1, waiting for transfers between devices: 453 us -> 0.01 us  [local(): q_weight = lax.all_gather(q_rows, Z, axis=0, tiled=False)]
    reduce_scatter x1 -> x0, waiting for transfers between devices: 72.3 us -> none  [local(): lax.psum_scatter(partial_sums, 'tensor', scatter_dimension=1, tiled=True)]
    all_gather x0 -> x3, blocking collectives: none -> 65.2 us  [the longest x1 35.8 us: local(): kv_weight = lax.all_gather(kv_rows, Z, axis=0, tiled=True)]
    all_to_all x0 -> x2, blocking collectives: none -> 32.7 us  [the longest x1 18.3 us: local(): got = lax.all_to_all(send, ('yh', 'c', 'x', 'yl'), 0, 0)]
    dot_general x3 -> x0, matrix products: 24.9 us -> none  [the longest x1 9.56 us: local(): jnp.einsum('qgjd,kgd->qgjk', queries, key_part, preferred_element_type=jn...]
    ppermute x0 -> x7, starting transfers between devices: none -> 22.7 us  [the longest x4 11.4 us: from_z(): return lax.ppermute(inputs, Z, [(i, (i - offset) % NZ) for i in range(NZ)])]
    pallas_call x0 -> x5, Pallas kernels: none -> 17.5 us  [the longest x1 8.4 us: attend(): pl.pallas_call(attend_kernel, grid_spec=pltpu.PrefetchScalarGridSpec(num_...]
    unnamed x12 -> x10, local copies, waits for them, and re-layouts: 17.3 us -> 1.33 us
  transfers between devices with their start and end apart: 4 -> 9, of which waited for: 4 -> 2; matrix products, arithmetic and copies ran while one was open for 3% -> 2% of each run, Pallas kernels for 0% -> 5%
where the time goes in v1:
time: 171 us; the launch traced here: 170 us
  blocking collectives  98 us (57%)
  starting transfers between devices  26.6 us (16%)
  Pallas kernels  17.5 us (10%)
  between operations  14.3 us (8%)
  waiting for transfers between devices  7.26 us (4%)
  local copies, waits for them, and re-layouts  5.06 us (3%)
    all_gather x1, blocking collectives, local(): kv_weight = lax.all_gather(kv_rows, Z, axis=0, tiled=True)  35.8 us
    all_gather x1, blocking collectives, local(): line = lax.all_gather(both, 'zh', axis=0, tiled=True)  19.5 us
    all_to_all x1, blocking collectives, local(): got = lax.all_to_all(send, ('yh', 'c', 'x', 'yl'), 0, 0)  18.3 us
    all_to_all x1, blocking collectives, local(): partial = lax.all_to_all(partial, ('yh', 'c'), 0, 0)  14.5 us
    ppermute x4, starting transfers between devices, from_z(): return lax.ppermute(inputs, Z, [(i, (i - offset) % NZ) for i in range(NZ)])  11.4 us
    ppermute x3, starting transfers between devices, swap(): return lax.ppermute(inputs, axis, [(0, 1), (1, 0)])  11.2 us
    all_gather x1, blocking collectives, local(): query = lax.all_gather(query, ('yh', 'c'), axis=0, tiled=False)  9.98 us
    pallas_call x1, Pallas kernels, attend(): pl.pallas_call(attend_kernel, grid_spec=pltpu.PrefetchScalarGridSpec(num_...  8.4 us
  transfers between devices with their start and end apart: 9, of which 2 were waited for; matrix products, arithmetic and copies ran while one was open for 2% of the time, Pallas kernels for 5%

profile of v1, /device:TPU:1, one launch (start us, length us, event | category | flops | bytes accessed | tf_op | source)
XLA Modules:
  0.0 170.0 jit_solution(4503429439902304444)
XLA Ops:
  7.2 0.0 all-gather.3.cloned.1.call-start
  7.2 1.2 reshape.70
  8.5 0.1 maximum_maximum_fusion
  8.7 0.1 copy.14
  8.8 18.3 %all_to_all.15 = bf16[32,10,256]{2,1,0:T(8,128)(2,1)S(1)} all-to-all(bf16[32,10,256]{2,1,0:T(8,128)(2,1)S(1)} %bitcast.28), channel_id=1, replica_groups=mesh['yh'=2,'zh'=4,'zl'=4,'c'=2,'x'=4,'yl'=2] {'yh','c','x','yl'}, dimensions={0} | all-to-all | bytes 327680 | tf_op jit(solution)/shard_map/weights/all_to_all | solution.py:246
  27.0 3.3 %collective-permute-start.1 = (bf16[128,5120]{1,0:T(8,128)(2,1)S(1)}, bf16[128,5120]{1,0:T(8,128)(2,1)S(1)}, u32[]{:S(2)}, u32[]{:S(2)}) collective-permute-start(bf16[128,5120]{1,0:T(8,128)(2,1)S(1)} %copy-done), channel_id=1, source_target_pairs={{0,256},{256,0},{1,257},{257,1},{2,258},{258,2},{3,259},{259,3},{4... | collective-permute-start | bytes 3932168 | tf_op jit(solution)/shard_map/weights/ppermute | solution.py:30
  30.4 0.7 reshape.75
  31.1 0.0 all-gather.3.cloned.1.call-update
  31.1 1.9 %collective-permute-start = (bf16[128,5120]{1,0:T(8,128)(2,1)S(1)}, bf16[128,5120]{1,0:T(8,128)(2,1)}, u32[]{:S(2)}, u32[]{:S(2)}) collective-permute-start(bf16[128,5120]{1,0:T(8,128)(2,1)S(1)} %copy-done), channel_id=1, source_target_pairs={{0,8},{8,0},{1,9},{9,1},{2,10},{10,2},{3,11},{11,3},{4,12},{12,4},... | collective-permute-start | bytes 3932168 | tf_op jit(solution)/shard_map/ppermute | solution.py:30
  33.1 35.8 %all_gather.15.weight = bf16[2560,128]{1,0:T(8,128)(2,1)S(1)} all-gather(bf16[160,128]{1,0:T(8,128)(2,1)S(1)} %reshape.73), channel_id=1, replica_groups=mesh['yh'=2,'zh'=4,'zl'=4,'c'=2,'x'=4,'yl'=2] {'zh','zl'}, dimensions={0}, use_global_device_ids=true | all-gather | bytes 696320 | tf_op jit(solution)/shard_map/weights/all_gather | solution.py:256
  68.9 6.0 %collective-permute-start.2 = (bf16[128,5120]{1,0:T(8,128)(2,1)S(1)}, bf16[128,5120]{1,0:T(8,128)(2,1)}, u32[]{:S(2)}, u32[]{:S(2)}) collective-permute-start(bf16[128,5120]{1,0:T(8,128)(2,1)S(1)} %collective-permute-done.1.h2), channel_id=1, source_target_pairs={{0,8},{8,0},{1,9},{9,1},{2,10},{10,2},{3,11},{11,3},{4,12},{12,4},... | collective-permute-start | bytes 3932168 | tf_op jit(solution)/shard_map/ppermute | solution.py:30
  74.9 0.1 stack.38.place
  75.0 0.9 dynamic-slice_bitcast_fusion.4
  75.9 1.8 %collective-permute-done.2.h3 = bf16[128,5120]{1,0:T(8,128)(2,1)} collective-permute-done((bf16[128,5120]{1,0:T(8,128)(2,1)S(1)}, bf16[128,5120]{1,0:T(8,128)(2,1)}, u32[]{:S(2)}, u32[]{:S(2)}) %collective-permute-start.2) | collective-permute-done | bytes 1310752 | tf_op jit(solution)/shard_map/ppermute | solution.py:30
  77.7 3.4 %kv_partial.1 = f32[4,128,128]{2,1,0:T(8,128)} custom-call(s32[5]{0:T(128)S(1)} %stack.38.place, bf16[128,5120]{1,0:T(8,128)(2,1)S(1)} %copy-done, bf16[128,5120]{1,0:T(8,128)(2,1)} %collective-permute-done.h1, bf16[128,5120]{1,0:T(8,128)(2,1)S(1)} %collective-permute-done.1.h2, bf16[128,5120]{1,0:T(8,128)(2,1)} %collective-permute-done.2.h3, ...), custom_call_target="tpu_custom_call" | custom-call | tf_op jit(solution)/shard_map/keys_values/kv_partial/pallas_call | solution.py:53
  81.1 3.9 %all-to-all-start.1 = ((f32[4,128,128]{2,1,0:T(8,128)}), f32[4,128,128]{2,1,0:T(8,128)S(1)}, u32[]{:S(2)}, u32[]{:S(2)}) async-start(f32[4,128,128]{2,1,0:T(8,128)} %kv_partial.1), calls=%async_computation.1 | async-start | bytes 524288 | tf_op jit(solution)/shard_map/keys_values/all_to_all | solution.py:273
  85.0 1.0 fusion
  86.0 0.2 pad_maximum_fusion
  86.2 5.5 %all-to-all-done.1.parts = f32[4,128,128]{2,1,0:T(8,128)S(1)} async-done(((f32[4,128,128]{2,1,0:T(8,128)}), f32[4,128,128]{2,1,0:T(8,128)S(1)}, u32[]{:S(2)}, u32[]{:S(2)}) %all-to-all-start.1) | async-done | bytes 262176 | tf_op jit(solution)/shard_map/keys_values/all_to_all | solution.py:273
  91.6 0.8 kv_finish.1
  92.4 19.5 %all_gather.17.kv0 = bf16[512,256]{1,0:T(8,128)(2,1)S(1)} all-gather(bf16[128,256]{1,0:T(8,128)(2,1)S(1)} %get-tuple-element.15), channel_id=1, replica_groups=mesh['yh'=2,'zh'=4,'zl'=4,'c'=2,'x'=4,'yl'=2] {'zh'}, dimensions={0}, use_global_device_ids=true | all-gather | bytes 327680 | tf_op jit(solution)/shard_map/keys_values/all_gather | solution.py:275
  111.9 1.9 %collective-permute-start.3 = (bf16[512,256]{1,0:T(8,128)(2,1)S(1)}, bf16[512,256]{1,0:T(8,128)(2,1)}, u32[]{:S(2)}, u32[]{:S(2)}) collective-permute-start(bf16[512,256]{1,0:T(8,128)(2,1)S(1)} %all_gather.17.kv0), channel_id=1, source_target_pairs={{0,240},{16,0},{32,16},{48,32},{64,48},{80,64},{96,80},{112,96},{1... | collective-permute-start | bytes 786440 | tf_op jit(solution)/shard_map/keys_values/ppermute | solution.py:34
  113.8 3.4 %collective-permute-start.4 = (bf16[512,256]{1,0:T(8,128)(2,1)S(1)}, bf16[512,256]{1,0:T(8,128)(2,1)}, u32[]{:S(2)}, u32[]{:S(2)}) collective-permute-start(bf16[512,256]{1,0:T(8,128)(2,1)S(1)} %all_gather.17.kv0), channel_id=1, source_target_pairs={{0,16},{16,32},{32,48},{48,64},{64,80},{80,96},{96,112},{112,128},... | collective-permute-start | bytes 786440 | tf_op jit(solution)/shard_map/keys_values/ppermute | solution.py:34
  117.2 0.7 fusion.1
  117.9 1.9 %collective-permute-start.5 = (bf16[256,256]{1,0:T(8,128)(2,1)}, bf16[256,256]{1,0:T(8,128)(2,1)S(1)}, u32[]{:S(2)}, u32[]{:S(2)}) collective-permute-start(bf16[256,256]{1,0:T(8,128)(2,1)} %get-tuple-element.18), channel_id=1, source_target_pairs={{0,224},{16,240},{32,0},{48,16},{64,32},{80,48},{96,64},{112,80},{... | collective-permute-start | bytes 393224 | tf_op jit(solution)/shard_map/keys_values/ppermute | solution.py:34
  119.8 4.3 %collective-permute-start.6 = (bf16[256,256]{1,0:T(8,128)(2,1)S(1)}, bf16[256,256]{1,0:T(8,128)(2,1)S(1)}, u32[]{:S(2)}, u32[]{:S(2)}) collective-permute-start(bf16[256,256]{1,0:T(8,128)(2,1)S(1)} %get-tuple-element.17), channel_id=1, source_target_pairs={{0,32},{16,48},{32,64},{48,80},{64,96},{80,112},{96,128},{112,144}... | collective-permute-start | bytes 393224 | tf_op jit(solution)/shard_map/keys_values/ppermute | solution.py:34
  124.1 1.3 copy-done.1
  125.4 4.0 %q_project.1 = bf16[4,128,128]{2,1,0:T(8,128)(2,1)S(1)} custom-call(s32[5]{0:T(128)S(1)} %stack.38.place, bf16[128,5120]{1,0:T(8,128)(2,1)S(1)} %copy-done, bf16[128,5120]{1,0:T(8,128)(2,1)} %collective-permute-done.h1, bf16[128,5120]{1,0:T(8,128)(2,1)S(1)} %collective-permute-done.1.h2, bf16[128,5120]{1,0:T(8,128)(2,1)} %collective-permute-done.2.h3, ...), custom_call_target="tpu_custom_call" | custom-call | tf_op jit(solution)/shard_map/queries/q_project/pallas_call | solution.py:111
  129.4 10.0 %all-gather = bf16[16,128,128]{2,1,0:T(8,128)(2,1)S(1)} all-gather(bf16[4,128,128]{2,1,0:T(8,128)(2,1)S(1)} %q_project.1), channel_id=2, replica_groups=mesh['yh'=2,'zh'=4,'zl'=4,'c'=2,'x'=4,'yl'=2] {'yh','c'}, dimensions={0}, use_global_device_ids=true | all-gather | bytes 655360 | tf_op jit(solution)/shard_map/queries/all_gather | solution.py:288
  139.4 8.4 %attend.1 = bf16[4,128,640]{2,1,0:T(8,128)(2,1)S(1)} custom-call(s32[5]{0:T(128)S(1)} %stack.38.place, s32[64,64]{1,0:T(8,128)S(1)} %copy-done.2, bf16[4,4,128,128]{3,2,1,0:T(8,128)(2,1)S(1)} %bitcast.23, bf16[512,256]{1,0:T(8,128)(2,1)S(1)} %all_gather.17.kv0, bf16[512,256]{1,0:T(8,128)(2,1)} %collective-permute-done.3.kv1, ...), custom_call_target="tpu_custom_call" | custom-call | tf_op jit(solution)/shard_map/context/attend/pallas_call | solution.py:198
  147.8 14.5 %all_to_all.16.parts = bf16[4,128,640]{2,1,0:T(8,128)(2,1)S(1)} all-to-all(bf16[4,128,640]{2,1,0:T(8,128)(2,1)S(1)} %attend.1), channel_id=1, replica_groups=mesh['yh'=2,'zh'=4,'zl'=4,'c'=2,'x'=4,'yl'=2] {'yh','c'}, dimensions={0} | all-to-all | bytes 1310720 | tf_op jit(solution)/shard_map/context/all_to_all | solution.py:292
  162.3 0.9 combine.1
  (24 shorter events, 0.2 us)
Async XLA Ops:
  7.2 19.9 %copy-start = (bf16[128,5120]{1,0:T(8,128)(2,1)S(1)}, bf16[128,5120]{1,0:T(8,128)(2,1)}, u32[]{:S(2)}) copy-start(bf16[128,5120]{1,0:T(8,128)(2,1)} %h0.3) | copy-start | bytes 3932164
  7.2 110.7 %all-gather.3.cloned.1.call-start = ((), (), s32[]{:S(2)}) async-start(), calls=%async_computation.3 | async-start | bytes 1392640 | tf_op jit(solution)/shard_map/weights/all_gather | solution.py:254
  27.0 41.9 %collective-permute-start.1 = (bf16[128,5120]{1,0:T(8,128)(2,1)S(1)}, bf16[128,5120]{1,0:T(8,128)(2,1)S(1)}, u32[]{:S(2)}, u32[]{:S(2)}) collective-permute-start(bf16[128,5120]{1,0:T(8,128)(2,1)S(1)} %copy-done), channel_id=1, source_target_pairs={{0,256},{256,0},{1,257},{257,1},{2,258},{258,2},{3,259},{259,3},{4... | collective-permute-start | bytes 3932168 | tf_op jit(solution)/shard_map/weights/ppermute | solution.py:30
  31.1 44.8 %collective-permute-start = (bf16[128,5120]{1,0:T(8,128)(2,1)S(1)}, bf16[128,5120]{1,0:T(8,128)(2,1)}, u32[]{:S(2)}, u32[]{:S(2)}) collective-permute-start(bf16[128,5120]{1,0:T(8,128)(2,1)S(1)} %copy-done), channel_id=1, source_target_pairs={{0,8},{8,0},{1,9},{9,1},{2,10},{10,2},{3,11},{11,3},{4,12},{12,4},... | collective-permute-start | bytes 3932168 | tf_op jit(solution)/shard_map/ppermute | solution.py:30
  68.9 8.8 %collective-permute-start.2 = (bf16[128,5120]{1,0:T(8,128)(2,1)S(1)}, bf16[128,5120]{1,0:T(8,128)(2,1)}, u32[]{:S(2)}, u32[]{:S(2)}) collective-permute-start(bf16[128,5120]{1,0:T(8,128)(2,1)S(1)} %collective-permute-done.1.h2), channel_id=1, source_target_pairs={{0,8},{8,0},{1,9},{9,1},{2,10},{10,2},{3,11},{11,3},{4,12},{12,4},... | collective-permute-start | bytes 3932168 | tf_op jit(solution)/shard_map/ppermute | solution.py:30
  81.1 10.6 %copy-start.3 = (f32[128]{0:T(128)S(1)}, f32[128]{0:T(128)}, u32[]{:S(2)}) copy-start(f32[128]{0:T(128)} %param.9) | copy-start | bytes 1540
  81.1 10.6 %all-to-all-start.1 = ((f32[4,128,128]{2,1,0:T(8,128)}), f32[4,128,128]{2,1,0:T(8,128)S(1)}, u32[]{:S(2)}, u32[]{:S(2)}) async-start(f32[4,128,128]{2,1,0:T(8,128)} %kv_partial.1), calls=%async_computation.1 | async-start | bytes 524288 | tf_op jit(solution)/shard_map/keys_values/all_to_all | solution.py:273
  86.0 38.1 %copy-start.4 = (f32[128]{0:T(128)S(1)}, f32[128]{0:T(128)}, u32[]{:S(2)}) copy-start(f32[128]{0:T(128)} %param.8) | copy-start | bytes 1540
  111.9 27.5 %collective-permute-start.3 = (bf16[512,256]{1,0:T(8,128)(2,1)S(1)}, bf16[512,256]{1,0:T(8,128)(2,1)}, u32[]{:S(2)}, u32[]{:S(2)}) collective-permute-start(bf16[512,256]{1,0:T(8,128)(2,1)S(1)} %all_gather.17.kv0), channel_id=1, source_target_pairs={{0,240},{16,0},{32,16},{48,32},{64,48},{80,64},{96,80},{112,96},{1... | collective-permute-start | bytes 786440 | tf_op jit(solution)/shard_map/keys_values/ppermute | solution.py:34
  113.8 25.6 %collective-permute-start.4 = (bf16[512,256]{1,0:T(8,128)(2,1)S(1)}, bf16[512,256]{1,0:T(8,128)(2,1)}, u32[]{:S(2)}, u32[]{:S(2)}) collective-permute-start(bf16[512,256]{1,0:T(8,128)(2,1)S(1)} %all_gather.17.kv0), channel_id=1, source_target_pairs={{0,16},{16,32},{32,48},{48,64},{64,80},{80,96},{96,112},{112,128},... | collective-permute-start | bytes 786440 | tf_op jit(solution)/shard_map/keys_values/ppermute | solution.py:34
  117.9 21.5 %collective-permute-start.5 = (bf16[256,256]{1,0:T(8,128)(2,1)}, bf16[256,256]{1,0:T(8,128)(2,1)S(1)}, u32[]{:S(2)}, u32[]{:S(2)}) collective-permute-start(bf16[256,256]{1,0:T(8,128)(2,1)} %get-tuple-element.18), channel_id=1, source_target_pairs={{0,224},{16,240},{32,0},{48,16},{64,32},{80,48},{96,64},{112,80},{... | collective-permute-start | bytes 393224 | tf_op jit(solution)/shard_map/keys_values/ppermute | solution.py:34
  119.8 19.6 %collective-permute-start.6 = (bf16[256,256]{1,0:T(8,128)(2,1)S(1)}, bf16[256,256]{1,0:T(8,128)(2,1)S(1)}, u32[]{:S(2)}, u32[]{:S(2)}) collective-permute-start(bf16[256,256]{1,0:T(8,128)(2,1)S(1)} %get-tuple-element.17), channel_id=1, source_target_pairs={{0,32},{16,48},{32,64},{48,80},{64,96},{80,112},{96,128},{112,144}... | collective-permute-start | bytes 393224 | tf_op jit(solution)/shard_map/keys_values/ppermute | solution.py:34
  124.1 1.3 copy-start.1
  125.4 14.0 %copy-start.2 = (s32[64,64]{1,0:T(8,128)S(1)}, s32[64,64]{1,0:T(8,128)}, u32[]{:S(2)}) copy-start(s32[64,64]{1,0:T(8,128)} %block_mask.1) | copy-start | bytes 49156
Sparse Core Ops, SparseCore 0:
  31.2 63.8 all-gather.2

commit v2 on v1

v2 whole, which is shorter than its diff:
```python
import functools
import math

import jax
import jax.numpy as jnp
from jax import lax
from jax.experimental import pallas as pl
from jax.experimental.pallas import tpu as pltpu
from jax.sharding import Mesh, PartitionSpec as P

HD = 128
BLOCK = 128
GQ = 4
KV = 8
YH, ZH, ZL, CORE, X, YL = 2, 4, 4, 2, 4, 2
NZ = ZH * ZL
GROUP = YH * CORE
DP = ("yh", "zh", "zl", "c")
TENSOR = ("x", "yl")
Z = ("zh", "zl")
bf16 = jnp.bfloat16
f32 = jnp.float32


def params():
    return pltpu.CompilerParams(vmem_limit_bytes=24 * 1024 * 1024)


def swap(inputs, axis):
    return lax.ppermute(inputs, axis, [(0, 1), (1, 0)])


def from_z(inputs, offset):
    return lax.ppermute(inputs, Z, [(i, (i - offset) % NZ) for i in range(NZ)])


def from_z_both(inputs, offset):
    pairs = [
        (i * CORE + core, (i - (1 - 2 * core) * offset) % NZ * CORE + core)
        for i in range(NZ)
        for core in range(CORE)
    ]
    return lax.ppermute(inputs, Z + ("c",), pairs)


def norm_rope(inputs, gain, cosine, sine):
    meansq = jnp.mean(inputs * inputs, axis=-1, keepdims=True)
    normed = inputs * lax.rsqrt(meansq + 1e-06) * gain
    return normed * cosine + pltpu.roll(normed, HD // 2, 1) * sine


def kv_partial_kernel(place, h0, h1, h2, h3, weight, out):
    member = place[1]
    half = weight.shape[0]
    columns = pl.ds(pl.multiple_of(place[0] * half, half), half)
    for rel, rows in enumerate((h0, h1, h2, h3)):
        out[member ^ rel] = jnp.dot(rows[:, columns], weight[...], preferred_element_type=f32)


def specs(count):
    scalars = pl.BlockSpec(memory_space=pltpu.SMEM)
    return [scalars] + [pl.BlockSpec(memory_space=pltpu.VMEM)] * count


def kv_partial(place, hiddens, weight):
    tok = hiddens[0].shape[0]
    return pl.pallas_call(
        kv_partial_kernel,
        in_specs=specs(GROUP + 1),
        out_shape=jax.ShapeDtypeStruct((GROUP, tok, HD), f32),
        compiler_params=params(),
        name="kv_partial",
    )(place, *hiddens, weight)


def kv_finish_kernel(parts, gain, cosine, sine, keys, values, both):
    key = norm_rope(parts[0] + parts[2], gain[...], cosine[0], sine[0]).astype(bf16)
    value = (parts[1] + parts[3]).astype(bf16)
    keys[...] = key
    values[...] = value
    both[:, :HD] = key
    both[:, HD:] = value


def kv_finish(parts, gain, cosine, sine):
    tok = parts.shape[1]
    return pl.pallas_call(
        kv_finish_kernel,
        out_shape=(
            jax.ShapeDtypeStruct((tok, HD), bf16),
            jax.ShapeDtypeStruct((tok, HD), bf16),
            jax.ShapeDtypeStruct((tok, 2 * HD), bf16),
        ),
        compiler_params=params(),
        name="kv_finish",
    )(parts, gain, cosine, sine)


def q_project_kernel(place, h0, h1, h2, h3, weight, gain, cosine, sine, out):
    member = place[1]
    half = h0.shape[1] // YH
    for rel, rows in enumerate((h0, h1, h2, h3)):
        total = None
        for yh in range(YH):
            part = jnp.dot(
                rows[:, yh * half : (yh + 1) * half],
                weight[:, yh].reshape(half, HD),
                preferred_element_type=f32,
            )
            total = part if total is None else total + part
        out[member ^ rel] = norm_rope(total, gain[...], cosine[rel], sine[rel]).astype(bf16)


def q_project(place, hiddens, weight, gain, cosine, sine):
    tok = hiddens[0].shape[0]
    return pl.pallas_call(
        q_project_kernel,
        in_specs=specs(GROUP + 4),
        out_shape=jax.ShapeDtypeStruct((GROUP, tok, HD), bf16),
        compiler_params=params(),
        name="q_project",
    )(place, *hiddens, weight, gain, cosine, sine)


OFFSETS = (0, 1, -1, 2)
BATCH = 4
WIDTH = (GQ + 1) * HD
LOW = 64


def query_member(place, remote, i):
    yh = 1 - place[0] if remote else place[0]
    return yh, jnp.where(i == 0, 1 - place[4], place[4])


def attend_kernel(remote, place, block_mask, query, *refs):
    lines = refs[: len(OFFSETS)]
    out, key_value, numer, total, slot_at, limit_at, sems = refs[len(OFFSETS) :]
    step = pl.program_id(0)
    yh, zh, zl, core = place[0], place[2], place[3], place[4]
    line_rows = ZH * BLOCK
    copies = [
        pltpu.make_async_copy(line, key_value.at[pl.ds(i * line_rows, line_rows)], sems.at[i])
        for i, line in enumerate(lines)
    ]

    @pl.when(step == 0)
    def _():
        for copy in copies:
            copy.start()

    query_yh, query_core = query_member(place, remote, step)
    query_block = query_yh * (NZ * CORE) + (zh * ZL + zl) * CORE + query_core
    slots = len(OFFSETS) * ZH
    for i in range(slots + BATCH):
        slot_at[i] = jnp.int32(0)
        limit_at[i] = jnp.int32(-2 * BLOCK)
    count = jnp.int32(0)
    for i in range(slots):
        z_at = (i % ZH) * ZL + lax.rem(zl + (OFFSETS[i // ZH] + ZL), ZL)
        key_block = yh * (NZ * CORE) + z_at * CORE + core
        live = (block_mask[query_block, key_block] == 1) & (key_block <= query_block)
        slot_at[count] = jnp.int32(i)
        limit_at[count] = jnp.where(
            live, jnp.where(key_block == query_block, 0, 2 * BLOCK), -2 * BLOCK
        )
        count = count + live.astype(jnp.int32)

    rows = query[...].reshape(GQ * BLOCK, HD)
    ahead = lax.broadcasted_iota(jnp.int32, (GQ * BLOCK, BLOCK), 1) - lax.rem(
        lax.broadcasted_iota(jnp.int32, (GQ * BLOCK, BLOCK), 0), BLOCK
    )
    numer[...] = jnp.zeros_like(numer)
    total[...] = jnp.zeros_like(total)

    @pl.when(step == 0)
    def _():
        for copy in copies:
            copy.wait()

    def batch(at, carry):
        first = at * BATCH
        starts = [pl.multiple_of(slot_at[first + i] * BLOCK, BLOCK) for i in range(BATCH)]
        limits = [limit_at[first + i] for i in range(BATCH)]
        block = jnp.concatenate([key_value[pl.ds(x, BLOCK), :] for x in starts], axis=0)
        scores = lax.dot_general(
            rows, block[:, :HD], (((1,), (1,)), ((), ())), preferred_element_type=f32
        )
        raised = jnp.exp2(scores * (math.log2(math.e) / math.sqrt(HD)))
        parts = [
            jnp.where(ahead <= limits[i], raised[:, i * BLOCK : (i + 1) * BLOCK], 0.0)
            for i in range(BATCH)
        ]
        total[...] += (parts[0] + parts[1]) + (parts[2] + parts[3])
        weights = jnp.concatenate([p.astype(bf16) for p in parts], axis=1)
        numer[...] += jnp.dot(weights, block[:, HD:], preferred_element_type=f32)
        return carry

    lax.fori_loop(0, (count + BATCH - 1) // BATCH, batch, 0)

    denom = jnp.sum(total[...], axis=1, keepdims=True)
    lane = lax.broadcasted_iota(jnp.int32, (BLOCK, HD), 1)
    tail = jnp.zeros((BLOCK, HD), f32)
    for head in range(GQ):
        mine = denom[head * BLOCK : (head + 1) * BLOCK]
        if remote:
            high = mine.astype(bf16).astype(f32)
            tail = jnp.where(lane == head, high, tail)
            tail = jnp.where(lane == head + LOW, mine - high, tail)
        else:
            tail = jnp.where(lane == head, mine, tail)
        out[0, :, head * HD : (head + 1) * HD] = numer[
            head * BLOCK : (head + 1) * BLOCK
        ].astype(out.dtype)
    out[0, :, GQ * HD :] = tail.astype(out.dtype)


def attend(remote, place, block_mask, query, lines):
    tok = query.shape[2]
    rows = GQ * tok
    keys = sum(line.shape[0] for line in lines)

    def of_query(i, place, block_mask):
        yh, core = query_member(place, remote, i)
        return 0, yh * CORE + core, 0, 0

    slots = len(OFFSETS) * ZH + BATCH
    return pl.pallas_call(
        functools.partial(attend_kernel, remote),
        grid_spec=pltpu.PrefetchScalarGridSpec(
            num_scalar_prefetch=2,
            grid=(CORE,),
            in_specs=[pl.BlockSpec((GQ, 1, tok, HD), of_query)]
            + [pl.BlockSpec(memory_space=pl.ANY)] * len(lines),
            out_specs=pl.BlockSpec((1, tok, WIDTH), lambda i, *_: (i, 0, 0)),
            scratch_shapes=[
                pltpu.VMEM((keys, 2 * HD), bf16),
                pltpu.VMEM((rows, HD), f32),
                pltpu.VMEM((rows, BLOCK), f32),
                pltpu.SMEM((slots,), jnp.int32),
                pltpu.SMEM((slots,), jnp.int32),
                pltpu.SemaphoreType.DMA((len(lines),)),
            ],
        ),
        out_shape=jax.ShapeDtypeStruct((CORE, tok, WIDTH), bf16 if remote else f32),
        compiler_params=params(),
        cost_estimate=pl.CostEstimate(
            flops=4 * CORE * rows * keys * HD,
            bytes_accessed=4 * keys * HD,
            transcendentals=CORE * rows * keys,
        ),
        name="attend_remote" if remote else "attend_local",
    )(place, block_mask, query, *lines)


def fold_kernel(mine, far, out):
    out[...] = mine[0] + far[0].astype(f32)


def fold(mine, far):
    return pl.pallas_call(
        fold_kernel,
        out_shape=jax.ShapeDtypeStruct(mine.shape[1:], f32),
        compiler_params=params(),
        name="fold",
    )(mine, far)


def combine_kernel(mine, far, near, out):
    tail = mine[1, :, GQ * HD :] + far[1, :, GQ * HD :].astype(f32) + near[:, GQ * HD :]
    for head in range(GQ):
        at = slice(head * HD, (head + 1) * HD)
        numer = mine[1, :, at] + far[1, :, at].astype(f32) + near[:, at]
        denom = tail[:, head : head + 1] + tail[:, head + LOW : head + LOW + 1]
        out[:, at] = (numer / denom).astype(bf16)


def combine(mine, far, near):
    return pl.pallas_call(
        combine_kernel,
        out_shape=jax.ShapeDtypeStruct((mine.shape[1], GQ * HD), bf16),
        compiler_params=params(),
        name="combine",
    )(mine, far, near)


def local(hidden, qkv_weight, query_gain, key_gain, positions, block_mask):
    tok, depth = hidden.shape
    share = qkv_weight.shape[0]
    yh, zh, zl, core = (lax.axis_index(a) for a in DP)
    member = yh * CORE + core
    place = jnp.stack([yh, member, zh, zl, core]).astype(jnp.int32)

    near = swap(hidden, "c")

    with jax.named_scope("weights"):
        split = qkv_weight.reshape(share, KV, GQ + 2, HD).transpose(2, 1, 0, 3)
        send = jnp.concatenate(
            [split[:GQ], jnp.concatenate([split[GQ:]] * YH, axis=0)], axis=-1
        ).reshape(GROUP * KV, share, 2 * HD)
        got = lax.all_to_all(send, ("yh", "c", "x", "yl"), 0, 0)
        rows = CORE * KV * share
        got, sent = lax.optimization_barrier((got, hidden))
        far = swap(sent, "yh")
        q_rows = got[:, :, :HD].reshape(YH * rows, HD)
        kv_rows = lax.dynamic_index_in_dim(
            got.reshape(YH, CORE * KV, share, 2 * HD), yh, 0, keepdims=False
        )[:, :, HD:].reshape(rows, HD)
        q_weight = lax.all_gather(q_rows, Z, axis=0, tiled=False)
        q_weight = q_weight.reshape(NZ, YH, rows, HD)
        kv_weight = lax.all_gather(kv_rows, Z, axis=0, tiled=True)

    far, _ = lax.optimization_barrier((far, kv_weight))
    hiddens = (hidden, near, far, swap(far, "c"))

    inverse = 1000000.0 ** (-(jnp.arange(HD // 2, dtype=f32) * 2.0) / HD)
    own = []
    for rel in range(GROUP):
        first = ((yh ^ (rel // CORE)) * NZ + zh * ZL + zl) * CORE + (core ^ (rel % CORE))
        own.append(lax.dynamic_slice_in_dim(positions, first * tok, tok, 0))
    angles = jnp.stack(own).astype(f32)[:, :, None] * inverse
    cosine, sine = jnp.cos(angles), jnp.sin(angles)
    cosine = jnp.concatenate([cosine, cosine], axis=-1)
    sine = jnp.concatenate([-sine, sine], axis=-1)

    with jax.named_scope("keys_values"):
        parts = kv_partial(place, hiddens, kv_weight)
        parts = lax.all_to_all(parts, ("yh", "c"), 0, 0)
        keys, values, both = kv_finish(parts, key_gain.reshape(1, HD), cosine, sine)
        line = lax.all_gather(both, "zh", axis=0, tiled=True)
        across = from_z_both(line, 2)
        gathered = (line, from_z(line, 1), from_z(line, -1), across)

    with jax.named_scope("queries"):
        q_weight, _ = lax.optimization_barrier((q_weight, line))
        query = q_project(place, hiddens, q_weight, query_gain.reshape(1, HD), cosine, sine)
        query = lax.all_gather(query, ("yh", "c"), axis=0, tiled=False)

    with jax.named_scope("context"):
        remote = attend(True, place, block_mask, query, gathered)
        far_part = lax.ppermute(remote, "yh", [(0, 1)])
        mine = attend(False, place, block_mask, query, gathered)
        near_part = swap(fold(mine, far_part), "c")
        context = combine(mine, far_part, near_part)
    return keys, values, context


def solution(mesh):
    fine = Mesh(mesh.devices.reshape(YH, ZH, ZL, CORE, X, YL), DP[:3] + ("c",) + TENSOR)
    return jax.shard_map(
        local,
        mesh=fine,
        in_specs=(P(DP, None), P(DP + TENSOR, None), P(), P(), P(), P()),
        out_specs=(P(DP, TENSOR), P(DP, TENSOR), P(DP, TENSOR)),
        check_vma=False,
    )
```

time: 171 us -> 162 us (0.947)
  blocking collectives: 98 us -> 84.9 us
  waiting for transfers between devices: 7.26 us -> 12.9 us
    all_to_all x1 -> x0, blocking collectives: 14.5 us -> none  [local(): partial = lax.all_to_all(partial, ('yh', 'c'), 0, 0)]
    ppermute x4 -> x2, starting transfers between devices: 11.4 us -> 5.27 us  [from_z(): return lax.ppermute(inputs, Z, [(i, (i - offset) % NZ) for i in range(NZ)])]
    ppermute x0 -> x2, waiting for transfers between devices: none -> 4.14 us  [the longest x1 4.13 us: local(): far_part = lax.ppermute(remote, 'yh', [(0, 1)])]
    ppermute x0 -> x2, starting transfers between devices: none -> 3.23 us  [the longest x1 1.92 us: from_z_both(): return lax.ppermute(inputs, Z + ('c',), pairs)]
    ppermute x3 -> x4, starting transfers between devices: 11.2 us -> 13.3 us  [swap(): return lax.ppermute(inputs, axis, [(0, 1), (1, 0)])]
    pallas_call x4 -> x6, Pallas kernels: 16.7 us -> 16.2 us  [the longest x2 8.5 us: attend(): pl.pallas_call(functools.partial(attend_kernel, remote), grid_spec=pltpu....]
  transfers between devices with their start and end apart: 9 -> 10, of which waited for: 2 -> 4; matrix products, arithmetic and copies ran while one was open for 2% -> 2% of each run, Pallas kernels for 5% -> 7%
where the time goes in v2:
time: 162 us; the launch traced here: 160 us
  blocking collectives  84.9 us (52%)
  starting transfers between devices  25.7 us (16%)
  Pallas kernels  17 us (10%)
  between operations  14.3 us (9%)
  waiting for transfers between devices  12.9 us (8%)
  local copies, waits for them, and re-layouts  4.39 us (3%)
    all_gather x1, blocking collectives, local(): kv_weight = lax.all_gather(kv_rows, Z, axis=0, tiled=True)  35.8 us
    all_gather x1, blocking collectives, local(): line = lax.all_gather(both, 'zh', axis=0, tiled=True)  19.7 us
    all_to_all x1, blocking collectives, local(): got = lax.all_to_all(send, ('yh', 'c', 'x', 'yl'), 0, 0)  18.3 us
    ppermute x4, starting transfers between devices, swap(): return lax.ppermute(inputs, axis, [(0, 1), (1, 0)])  13.3 us
    all_gather x1, blocking collectives, local(): query = lax.all_gather(query, ('yh', 'c'), axis=0, tiled=False)  11.1 us
    pallas_call x2, Pallas kernels, attend(): pl.pallas_call(functools.partial(attend_kernel, remote), grid_spec=pltpu....  8.5 us
    all_to_all x1, waiting for transfers between devices, local(): parts = lax.all_to_all(parts, ('yh', 'c'), 0, 0)  5.46 us
    ppermute x2, starting transfers between devices, from_z(): return lax.ppermute(inputs, Z, [(i, (i - offset) % NZ) for i in range(NZ)])  5.27 us
  transfers between devices with their start and end apart: 10, of which 4 were waited for; matrix products, arithmetic and copies ran while one was open for 2% of the time, Pallas kernels for 7%

profile of v2, /device:TPU:1, one launch (start us, length us, event | category | flops | bytes accessed | tf_op | source)
XLA Modules:
  0.0 160.4 jit_solution(17132305640202799840)
XLA Ops:
  7.2 1.2 reshape.70
  8.5 0.1 maximum_maximum_fusion
  8.7 0.1 copy.14
  8.8 18.3 %all_to_all.10 = bf16[32,10,256]{2,1,0:T(8,128)(2,1)S(1)} all-to-all(bf16[32,10,256]{2,1,0:T(8,128)(2,1)S(1)} %bitcast.29), channel_id=1, replica_groups=mesh['yh'=2,'zh'=4,'zl'=4,'c'=2,'x'=4,'yl'=2] {'yh','c','x','yl'}, dimensions={0} | all-to-all | bytes 327680 | tf_op jit(solution)/shard_map/weights/all_to_all | solution.py:301
  27.0 3.3 %collective-permute-start.1 = (bf16[128,5120]{1,0:T(8,128)(2,1)S(1)}, bf16[128,5120]{1,0:T(8,128)(2,1)S(1)}, u32[]{:S(2)}, u32[]{:S(2)}) collective-permute-start(bf16[128,5120]{1,0:T(8,128)(2,1)S(1)} %copy-done), channel_id=1, source_target_pairs={{0,256},{256,0},{1,257},{257,1},{2,258},{258,2},{3,259},{259,3},{4... | collective-permute-start | bytes 3932168 | tf_op jit(solution)/shard_map/weights/ppermute | solution.py:30
  30.4 0.7 reshape.75
  31.1 1.9 %collective-permute-start = (bf16[128,5120]{1,0:T(8,128)(2,1)S(1)}, bf16[128,5120]{1,0:T(8,128)(2,1)}, u32[]{:S(2)}, u32[]{:S(2)}) collective-permute-start(bf16[128,5120]{1,0:T(8,128)(2,1)S(1)} %copy-done), channel_id=1, source_target_pairs={{0,8},{8,0},{1,9},{9,1},{2,10},{10,2},{3,11},{11,3},{4,12},{12,4},... | collective-permute-start | bytes 3932168 | tf_op jit(solution)/shard_map/ppermute | solution.py:30
  33.1 35.8 %all_gather.15.weight = bf16[2560,128]{1,0:T(8,128)(2,1)S(1)} all-gather(bf16[160,128]{1,0:T(8,128)(2,1)S(1)} %reshape.73), channel_id=1, replica_groups=mesh['yh'=2,'zh'=4,'zl'=4,'c'=2,'x'=4,'yl'=2] {'zh','zl'}, dimensions={0}, use_global_device_ids=true | all-gather | bytes 696320 | tf_op jit(solution)/shard_map/weights/all_gather | solution.py:311
  68.9 6.0 %collective-permute-start.2 = (bf16[128,5120]{1,0:T(8,128)(2,1)S(1)}, bf16[128,5120]{1,0:T(8,128)(2,1)}, u32[]{:S(2)}, u32[]{:S(2)}) collective-permute-start(bf16[128,5120]{1,0:T(8,128)(2,1)S(1)} %collective-permute-done.1.h2), channel_id=1, source_target_pairs={{0,8},{8,0},{1,9},{9,1},{2,10},{10,2},{3,11},{11,3},{4,12},{12,4},... | collective-permute-start | bytes 3932168 | tf_op jit(solution)/shard_map/ppermute | solution.py:30
  75.0 0.1 stack.38.place
  75.0 0.9 dynamic-slice_bitcast_fusion.4
  75.9 1.8 %collective-permute-done.2.h3 = bf16[128,5120]{1,0:T(8,128)(2,1)} collective-permute-done((bf16[128,5120]{1,0:T(8,128)(2,1)S(1)}, bf16[128,5120]{1,0:T(8,128)(2,1)}, u32[]{:S(2)}, u32[]{:S(2)}) %collective-permute-start.2) | collective-permute-done | bytes 1310752 | tf_op jit(solution)/shard_map/ppermute | solution.py:30
  77.7 3.3 %kv_partial.1 = f32[4,128,128]{2,1,0:T(8,128)} custom-call(s32[5]{0:T(128)S(1)} %stack.38.place, bf16[128,5120]{1,0:T(8,128)(2,1)S(1)} %copy-done, bf16[128,5120]{1,0:T(8,128)(2,1)} %collective-permute-done.h1, bf16[128,5120]{1,0:T(8,128)(2,1)S(1)} %collective-permute-done.1.h2, bf16[128,5120]{1,0:T(8,128)(2,1)} %collective-permute-done.2.h3, ...), custom_call_target="tpu_custom_call" | custom-call | tf_op jit(solution)/shard_map/keys_values/kv_partial/pallas_call | solution.py:67
  81.0 3.9 %all-to-all-start.1 = ((f32[4,128,128]{2,1,0:T(8,128)}), f32[4,128,128]{2,1,0:T(8,128)S(1)}, u32[]{:S(2)}, u32[]{:S(2)}) async-start(f32[4,128,128]{2,1,0:T(8,128)} %kv_partial.1), calls=%async_computation.1 | async-start | bytes 524288 | tf_op jit(solution)/shard_map/keys_values/all_to_all | solution.py:328
  84.8 1.0 fusion
  85.8 0.2 pad_maximum_fusion
  86.0 5.5 %all-to-all-done.1.parts = f32[4,128,128]{2,1,0:T(8,128)S(1)} async-done(((f32[4,128,128]{2,1,0:T(8,128)}), f32[4,128,128]{2,1,0:T(8,128)S(1)}, u32[]{:S(2)}, u32[]{:S(2)}) %all-to-all-start.1) | async-done | bytes 262176 | tf_op jit(solution)/shard_map/keys_values/all_to_all | solution.py:328
  91.5 0.8 kv_finish.1
  92.3 19.7 %all_gather.17.refs_0_ = bf16[512,256]{1,0:T(8,128)(2,1)S(1)} all-gather(bf16[128,256]{1,0:T(8,128)(2,1)S(1)} %get-tuple-element.15), channel_id=1, replica_groups=mesh['yh'=2,'zh'=4,'zl'=4,'c'=2,'x'=4,'yl'=2] {'zh'}, dimensions={0}, use_global_device_ids=true | all-gather | bytes 327680 | tf_op jit(solution)/shard_map/keys_values/all_gather | solution.py:330
  112.0 1.9 %collective-permute-start.3 = (bf16[512,256]{1,0:T(8,128)(2,1)S(1)}, bf16[512,256]{1,0:T(8,128)(2,1)}, u32[]{:S(2)}, u32[]{:S(2)}) collective-permute-start(bf16[512,256]{1,0:T(8,128)(2,1)S(1)} %all_gather.17.refs_0_), channel_id=1, source_target_pairs={{0,240},{16,0},{32,16},{48,32},{64,48},{80,64},{96,80},{112,96},{1... | collective-permute-start | bytes 786440 | tf_op jit(solution)/shard_map/keys_values/ppermute | solution.py:34
  114.0 3.4 %collective-permute-start.4 = (bf16[512,256]{1,0:T(8,128)(2,1)S(1)}, bf16[512,256]{1,0:T(8,128)(2,1)}, u32[]{:S(2)}, u32[]{:S(2)}) collective-permute-start(bf16[512,256]{1,0:T(8,128)(2,1)S(1)} %all_gather.17.refs_0_), channel_id=1, source_target_pairs={{0,16},{16,32},{32,48},{48,64},{64,80},{80,96},{96,112},{112,128},... | collective-permute-start | bytes 786440 | tf_op jit(solution)/shard_map/keys_values/ppermute | solution.py:34
  117.3 1.9 %collective-permute-start.5 = (bf16[512,256]{1,0:T(8,128)(2,1)S(1)}, bf16[512,256]{1,0:T(8,128)(2,1)}, u32[]{:S(2)}, u32[]{:S(2)}) collective-permute-start(bf16[512,256]{1,0:T(8,128)(2,1)S(1)} %all_gather.17.refs_0_), channel_id=1, source_target_pairs={{0,224},{8,40},{16,240},{24,56},{32,0},{40,72},{48,16},{56,88},{64... | collective-permute-start | bytes 786440 | tf_op jit(solution)/shard_map/keys_values/ppermute | solution.py:43
  119.3 1.3 copy-done.1
  120.6 3.5 %q_project.1 = bf16[4,128,128]{2,1,0:T(8,128)(2,1)S(1)} custom-call(s32[5]{0:T(128)S(1)} %stack.38.place, bf16[128,5120]{1,0:T(8,128)(2,1)S(1)} %copy-done, bf16[128,5120]{1,0:T(8,128)(2,1)} %collective-permute-done.h1, bf16[128,5120]{1,0:T(8,128)(2,1)S(1)} %collective-permute-done.1.h2, bf16[128,5120]{1,0:T(8,128)(2,1)} %collective-permute-done.2.h3, ...), custom_call_target="tpu_custom_call" | custom-call | tf_op jit(solution)/shard_map/queries/q_project/pallas_call | solution.py:116
  124.1 11.1 %all-gather = bf16[16,128,128]{2,1,0:T(8,128)(2,1)S(1)} all-gather(bf16[4,128,128]{2,1,0:T(8,128)(2,1)S(1)} %q_project.1), channel_id=2, replica_groups=mesh['yh'=2,'zh'=4,'zl'=4,'c'=2,'x'=4,'yl'=2] {'yh','c'}, dimensions={0}, use_global_device_ids=true | all-gather | bytes 655360 | tf_op jit(solution)/shard_map/queries/all_gather | solution.py:337
  135.2 5.2 %attend_remote.1 = bf16[2,128,640]{2,1,0:T(8,128)(2,1)S(1)} custom-call(s32[5]{0:T(128)S(1)} %stack.38.place, s32[64,64]{1,0:T(8,128)S(1)} %copy-done.4, bf16[4,4,128,128]{3,2,1,0:T(8,128)(2,1)S(1)} %bitcast.24, bf16[512,256]{1,0:T(8,128)(2,1)S(1)} %all_gather.17.refs_0_, bf16[512,256]{1,0:T(8,128)(2,1)} %collective-permute-done.3.refs_1_, ...), custom_call_target="tpu_custom_call" | custom-call | flops 1073741824 | bytes 1048576 | tf_op jit(solution)/shard_map/context/attend_remote/pallas_call | solution.py:228
  140.4 1.3 collective-permute-start.6
  141.7 3.3 %attend_local.1.mine = f32[2,128,640]{2,1,0:T(8,128)S(1)} custom-call(s32[5]{0:T(128)S(1)} %stack.38.place, s32[64,64]{1,0:T(8,128)S(1)} %copy-done.4, bf16[4,4,128,128]{3,2,1,0:T(8,128)(2,1)S(1)} %bitcast.25, bf16[512,256]{1,0:T(8,128)(2,1)S(1)} %all_gather.17.refs_0_, bf16[512,256]{1,0:T(8,128)(2,1)} %collective-permute-done.3.refs_1_, ...), custom_call_target="tpu_custom_call" | custom-call | flops 1073741824 | bytes 1048576 | tf_op jit(solution)/shard_map/context/attend_local/pallas_call | solution.py:228
  145.0 4.1 %collective-permute-done.6.far = bf16[2,128,640]{2,1,0:T(8,128)(2,1)S(1)} collective-permute-done((bf16[2,128,640]{2,1,0:T(8,128)(2,1)S(1)}, bf16[2,128,640]{2,1,0:T(8,128)(2,1)S(1)}, u32[]{:S(2)}, u32[]{:S(2)}) %collective-permute-start.6) | collective-permute-done | bytes 327712 | tf_op jit(solution)/shard_map/context/ppermute | solution.py:341
  149.2 2.1 %collective-permute-start.7 = (f32[128,640]{1,0:T(8,128)S(1)}, f32[128,640]{1,0:T(8,128)S(1)}, u32[]{:S(2)}, u32[]{:S(2)}) collective-permute-start(f32[128,640]{1,0:T(8,128)S(1)} %fold.1), channel_id=1, source_target_pairs={{0,8},{8,0},{1,9},{9,1},{2,10},{10,2},{3,11},{11,3},{4,12},{12,4},... | collective-permute-start | bytes 983048 | tf_op jit(solution)/shard_map/context/ppermute | solution.py:30
  151.3 1.4 collective-permute-done.7.near
  152.7 0.9 combine.1
  (26 shorter events, 0.3 us)
Async XLA Ops:
  7.2 19.9 %copy-start = (bf16[128,5120]{1,0:T(8,128)(2,1)S(1)}, bf16[128,5120]{1,0:T(8,128)(2,1)}, u32[]{:S(2)}) copy-start(bf16[128,5120]{1,0:T(8,128)(2,1)} %h0.3) | copy-start | bytes 3932164
  7.2 112.1 %all-gather.3.cloned.1.call-start = ((), (), s32[]{:S(2)}) async-start(), calls=%async_computation.2 | async-start | bytes 1392640 | tf_op jit(solution)/shard_map/weights/all_gather | solution.py:309
  27.0 41.9 %collective-permute-start.1 = (bf16[128,5120]{1,0:T(8,128)(2,1)S(1)}, bf16[128,5120]{1,0:T(8,128)(2,1)S(1)}, u32[]{:S(2)}, u32[]{:S(2)}) collective-permute-start(bf16[128,5120]{1,0:T(8,128)(2,1)S(1)} %copy-done), channel_id=1, source_target_pairs={{0,256},{256,0},{1,257},{257,1},{2,258},{258,2},{3,259},{259,3},{4... | collective-permute-start | bytes 3932168 | tf_op jit(solution)/shard_map/weights/ppermute | solution.py:30
  31.1 44.8 %collective-permute-start = (bf16[128,5120]{1,0:T(8,128)(2,1)S(1)}, bf16[128,5120]{1,0:T(8,128)(2,1)}, u32[]{:S(2)}, u32[]{:S(2)}) collective-permute-start(bf16[128,5120]{1,0:T(8,128)(2,1)S(1)} %copy-done), channel_id=1, source_target_pairs={{0,8},{8,0},{1,9},{9,1},{2,10},{10,2},{3,11},{11,3},{4,12},{12,4},... | collective-permute-start | bytes 3932168 | tf_op jit(solution)/shard_map/ppermute | solution.py:30
  68.9 8.8 %collective-permute-start.2 = (bf16[128,5120]{1,0:T(8,128)(2,1)S(1)}, bf16[128,5120]{1,0:T(8,128)(2,1)}, u32[]{:S(2)}, u32[]{:S(2)}) collective-permute-start(bf16[128,5120]{1,0:T(8,128)(2,1)S(1)} %collective-permute-done.1.h2), channel_id=1, source_target_pairs={{0,8},{8,0},{1,9},{9,1},{2,10},{10,2},{3,11},{11,3},{4,12},{12,4},... | collective-permute-start | bytes 3932168 | tf_op jit(solution)/shard_map/ppermute | solution.py:30
  81.0 10.5 %copy-start.2 = (f32[128]{0:T(128)S(1)}, f32[128]{0:T(128)}, u32[]{:S(2)}) copy-start(f32[128]{0:T(128)} %param.9) | copy-start | bytes 1540
  81.0 10.5 %all-to-all-start.1 = ((f32[4,128,128]{2,1,0:T(8,128)}), f32[4,128,128]{2,1,0:T(8,128)S(1)}, u32[]{:S(2)}, u32[]{:S(2)}) async-start(f32[4,128,128]{2,1,0:T(8,128)} %kv_partial.1), calls=%async_computation.1 | async-start | bytes 524288 | tf_op jit(solution)/shard_map/keys_values/all_to_all | solution.py:328
  85.8 33.5 %copy-start.3 = (f32[128]{0:T(128)S(1)}, f32[128]{0:T(128)}, u32[]{:S(2)}) copy-start(f32[128]{0:T(128)} %param.8) | copy-start | bytes 1540
  112.0 23.1 %collective-permute-start.3 = (bf16[512,256]{1,0:T(8,128)(2,1)S(1)}, bf16[512,256]{1,0:T(8,128)(2,1)}, u32[]{:S(2)}, u32[]{:S(2)}) collective-permute-start(bf16[512,256]{1,0:T(8,128)(2,1)S(1)} %all_gather.17.refs_0_), channel_id=1, source_target_pairs={{0,240},{16,0},{32,16},{48,32},{64,48},{80,64},{96,80},{112,96},{1... | collective-permute-start | bytes 786440 | tf_op jit(solution)/shard_map/keys_values/ppermute | solution.py:34
  114.0 21.2 %collective-permute-start.4 = (bf16[512,256]{1,0:T(8,128)(2,1)S(1)}, bf16[512,256]{1,0:T(8,128)(2,1)}, u32[]{:S(2)}, u32[]{:S(2)}) collective-permute-start(bf16[512,256]{1,0:T(8,128)(2,1)S(1)} %all_gather.17.refs_0_), channel_id=1, source_target_pairs={{0,16},{16,32},{32,48},{48,64},{64,80},{80,96},{96,112},{112,128},... | collective-permute-start | bytes 786440 | tf_op jit(solution)/shard_map/keys_values/ppermute | solution.py:34
  117.3 17.8 %collective-permute-start.5 = (bf16[512,256]{1,0:T(8,128)(2,1)S(1)}, bf16[512,256]{1,0:T(8,128)(2,1)}, u32[]{:S(2)}, u32[]{:S(2)}) collective-permute-start(bf16[512,256]{1,0:T(8,128)(2,1)S(1)} %all_gather.17.refs_0_), channel_id=1, source_target_pairs={{0,224},{8,40},{16,240},{24,56},{32,0},{40,72},{48,16},{56,88},{64... | collective-permute-start | bytes 786440 | tf_op jit(solution)/shard_map/keys_values/ppermute | solution.py:43
  119.3 1.3 copy-start.1
  120.6 14.6 %copy-start.4 = (s32[64,64]{1,0:T(8,128)S(1)}, s32[64,64]{1,0:T(8,128)}, u32[]{:S(2)}) copy-start(s32[64,64]{1,0:T(8,128)} %block_mask.3) | copy-start | bytes 49156
  140.4 8.7 %collective-permute-start.6 = (bf16[2,128,640]{2,1,0:T(8,128)(2,1)S(1)}, bf16[2,128,640]{2,1,0:T(8,128)(2,1)S(1)}, u32[]{:S(2)}, u32[]{:S(2)}) collective-permute-start(bf16[2,128,640]{2,1,0:T(8,128)(2,1)S(1)} %attend_remote.1), channel_id=1, source_target_pairs={{0,256},{1,257},{2,258},{3,259},{4,260},{5,261},{6,262},{7,263},{8... | collective-permute-start | bytes 983048 | tf_op jit(solution)/shard_map/context/ppermute | solution.py:341
  149.2 3.5 %collective-permute-start.7 = (f32[128,640]{1,0:T(8,128)S(1)}, f32[128,640]{1,0:T(8,128)S(1)}, u32[]{:S(2)}, u32[]{:S(2)}) collective-permute-start(f32[128,640]{1,0:T(8,128)S(1)} %fold.1), channel_id=1, source_target_pairs={{0,8},{8,0},{1,9},{9,1},{2,10},{10,2},{3,11},{11,3},{4,12},{12,4},... | collective-permute-start | bytes 983048 | tf_op jit(solution)/shard_map/context/ppermute | solution.py:30
Sparse Core Ops, SparseCore 0:
  31.2 63.8 all-gather.2

commit v3 on v2

v3 whole, which is shorter than its diff:
```python
import functools
import math

import jax
import jax.numpy as jnp
from jax import lax
from jax.experimental import pallas as pl
from jax.experimental.pallas import tpu as pltpu
from jax.sharding import Mesh, PartitionSpec as P

HD = 128
BLOCK = 128
GQ = 4
PAIR = 2
KV = 8
YH, ZH, ZL, CORE, X, YL = 2, 4, 4, 2, 4, 2
NZ = ZH * ZL
GROUP = YH * CORE
DP = ("yh", "zh", "zl", "c")
TENSOR = ("x", "yl")
Z = ("zh", "zl")
bf16 = jnp.bfloat16
f32 = jnp.float32


def params():
    return pltpu.CompilerParams(vmem_limit_bytes=24 * 1024 * 1024)


def swap(inputs, axis):
    return lax.ppermute(inputs, axis, [(0, 1), (1, 0)])


def from_z(inputs, offset):
    return lax.ppermute(inputs, Z, [(i, (i - offset) % NZ) for i in range(NZ)])


def from_z_both(inputs, offset):
    pairs = [
        (i * CORE + core, (i - (1 - 2 * core) * offset) % NZ * CORE + core)
        for i in range(NZ)
        for core in range(CORE)
    ]
    return lax.ppermute(inputs, Z + ("c",), pairs)


def norm_rope(inputs, gain, cosine, sine):
    meansq = jnp.mean(inputs * inputs, axis=-1, keepdims=True)
    normed = inputs * lax.rsqrt(meansq + 1e-06) * gain
    return normed * cosine + pltpu.roll(normed, HD // 2, 1) * sine


def specs(count):
    scalars = pl.BlockSpec(memory_space=pltpu.SMEM)
    return [scalars] + [pl.BlockSpec(memory_space=pltpu.VMEM)] * count


def pack_kernel(weight, out):
    for yh in range(YH):
        for core in range(CORE):
            for head in range(KV):
                first = head * (GQ + 2)
                slots = [first + yh * PAIR + core, first + GQ + core]
                for i, slot in enumerate(slots):
                    out[(yh * CORE + core) * KV + head, :, i * HD : (i + 1) * HD] = weight[
                        :, slot * HD : (slot + 1) * HD
                    ]


def pack(weight):
    return pl.pallas_call(
        pack_kernel,
        out_shape=jax.ShapeDtypeStruct(
            (GROUP * KV, weight.shape[0], 2 * HD), weight.dtype
        ),
        compiler_params=params(),
        name="pack",
    )(weight)


def half_dots(place, h0, h1, weight):
    half = weight.shape[0]
    columns = pl.ds(pl.multiple_of(place[0] * half, half), half)
    return [
        jnp.dot(rows[:, columns], weight[...], preferred_element_type=f32) for rows in (h0, h1)
    ]


def kv_first_kernel(place, h0, h1, weight, out):
    out[0], out[1] = half_dots(place, h0, h1, weight)


def kv_first(place, hiddens, weight):
    tok = hiddens[0].shape[0]
    return pl.pallas_call(
        kv_first_kernel,
        in_specs=specs(YH + 1),
        out_shape=jax.ShapeDtypeStruct((YH, tok, HD), f32),
        compiler_params=params(),
        name="kv_first",
    )(place, *hiddens, weight)


def kv_second_kernel(place, h0, h1, weight, first, keep, send):
    core = place[4]
    mine = pl.ds(pl.multiple_of(core * HD, HD), HD)
    other = pl.ds(pl.multiple_of((1 - core) * HD, HD), HD)
    dots = half_dots(place, h0, h1, weight)
    for rel, out in enumerate((keep, send)):
        out[:, mine] = first[rel]
        out[:, other] = dots[rel]


def kv_second(place, hiddens, weight, first):
    tok = hiddens[0].shape[0]
    shape = jax.ShapeDtypeStruct((tok, 2 * HD), f32)
    return pl.pallas_call(
        kv_second_kernel,
        in_specs=specs(YH + 2),
        out_shape=(shape, shape),
        compiler_params=params(),
        name="kv_second",
    )(place, *hiddens, weight, first)


def kv_finish_kernel(place, keep, sent, gain, cosine, sine, keys, values, both):
    total = keep[...] + sent[1 - place[0]]
    key = norm_rope(total[:, :HD], gain[...], cosine[0], sine[0]).astype(bf16)
    value = total[:, HD:].astype(bf16)
    keys[...] = key
    values[...] = value
    both[:, :HD] = key
    both[:, HD:] = value


def kv_finish(place, keep, sent, gain, cosine, sine):
    tok = keep.shape[0]
    return pl.pallas_call(
        kv_finish_kernel,
        in_specs=specs(5),
        out_shape=(
            jax.ShapeDtypeStruct((tok, HD), bf16),
            jax.ShapeDtypeStruct((tok, HD), bf16),
            jax.ShapeDtypeStruct((tok, 2 * HD), bf16),
        ),
        compiler_params=params(),
        name="kv_finish",
    )(place, keep, sent, gain, cosine, sine)


def q_project_kernel(place, h0, h1, mine, other, gain, cosine, sine, out):
    yh, core = place[0], place[4]
    half = h0.shape[1] // YH
    for flip, weight in enumerate((mine, other)):
        for rel, rows in enumerate((h0, h1)):
            total = None
            for i in range(YH):
                part = jnp.dot(
                    rows[:, i * half : (i + 1) * half],
                    weight[:, i].reshape(half, HD),
                    preferred_element_type=f32,
                )
                total = part if total is None else total + part
            out[core ^ flip, yh ^ rel] = norm_rope(
                total, gain[...], cosine[rel], sine[rel]
            ).astype(bf16)


def q_project(place, hiddens, weights, gain, cosine, sine):
    tok = hiddens[0].shape[0]
    return pl.pallas_call(
        q_project_kernel,
        in_specs=specs(YH + CORE + 3),
        out_shape=jax.ShapeDtypeStruct((PAIR, YH, tok, HD), bf16),
        compiler_params=params(),
        name="q_project",
    )(place, *hiddens, *weights, gain, cosine, sine)


OFFSETS = (0, 1, -1, 2)
BATCH = 4
WIDTH = (GQ + 1) * HD
LOW = 64


def query_member(place, remote, i):
    yh = 1 - place[0] if remote else place[0]
    return yh, jnp.where(i == 0, 1 - place[4], place[4])


def attend_kernel(remote, place, block_mask, query, *refs):
    lines = refs[: len(OFFSETS)]
    peer, own, key_value, numer, total, slot_at, limit_at, sems = refs[-8:]
    step = pl.program_id(0)
    yh, zh, zl, core = place[0], place[2], place[3], place[4]
    line_rows = ZH * BLOCK
    copies = [
        pltpu.make_async_copy(line, key_value.at[pl.ds(i * line_rows, line_rows)], sems.at[i])
        for i, line in enumerate(lines)
    ]

    @pl.when(step == 0)
    def _():
        for copy in copies:
            copy.start()

    query_yh, query_core = query_member(place, remote, step)
    query_block = query_yh * (NZ * CORE) + (zh * ZL + zl) * CORE + query_core
    slots = len(OFFSETS) * ZH
    for i in range(slots + BATCH):
        slot_at[i] = jnp.int32(0)
        limit_at[i] = jnp.int32(-2 * BLOCK)
    count = jnp.int32(0)
    for i in range(slots):
        z_at = (i % ZH) * ZL + lax.rem(zl + (OFFSETS[i // ZH] + ZL), ZL)
        key_block = yh * (NZ * CORE) + z_at * CORE + core
        live = (block_mask[query_block, key_block] == 1) & (key_block <= query_block)
        slot_at[count] = jnp.int32(i)
        limit_at[count] = jnp.where(
            live, jnp.where(key_block == query_block, 0, 2 * BLOCK), -2 * BLOCK
        )
        count = count + live.astype(jnp.int32)

    rows = query[...].reshape(GQ * BLOCK, HD)
    ahead = lax.broadcasted_iota(jnp.int32, (GQ * BLOCK, BLOCK), 1) - lax.rem(
        lax.broadcasted_iota(jnp.int32, (GQ * BLOCK, BLOCK), 0), BLOCK
    )
    numer[...] = jnp.zeros_like(numer)
    total[...] = jnp.zeros_like(total)

    @pl.when(step == 0)
    def _():
        for copy in copies:
            copy.wait()

    def batch(at, carry):
        first = at * BATCH
        starts = [pl.multiple_of(slot_at[first + i] * BLOCK, BLOCK) for i in range(BATCH)]
        limits = [limit_at[first + i] for i in range(BATCH)]
        block = jnp.concatenate([key_value[pl.ds(x, BLOCK), :] for x in starts], axis=0)
        scores = lax.dot_general(
            rows, block[:, :HD], (((1,), (1,)), ((), ())), preferred_element_type=f32
        )
        raised = jnp.exp2(scores * (math.log2(math.e) / math.sqrt(HD)))
        parts = [
            jnp.where(ahead <= limits[i], raised[:, i * BLOCK : (i + 1) * BLOCK], 0.0)
            for i in range(BATCH)
        ]
        total[...] += (parts[0] + parts[1]) + (parts[2] + parts[3])
        weights = jnp.concatenate([p.astype(bf16) for p in parts], axis=1)
        numer[...] += jnp.dot(weights, block[:, HD:], preferred_element_type=f32)
        return carry

    lax.fori_loop(0, (count + BATCH - 1) // BATCH, batch, 0)

    denom = jnp.sum(total[...], axis=1, keepdims=True)
    lane = lax.broadcasted_iota(jnp.int32, (BLOCK, HD), 1)
    tail = jnp.zeros((BLOCK, HD), f32)
    for head in range(GQ):
        tail = jnp.where(lane == head, denom[head * BLOCK : (head + 1) * BLOCK], tail)
    for at, out in enumerate((peer, own)):

        @pl.when(step == at)
        def _(out=out):
            for head in range(GQ):
                out[:, head * HD : (head + 1) * HD] = numer[
                    head * BLOCK : (head + 1) * BLOCK
                ].astype(out.dtype)
            out[:, GQ * HD :] = tail if out.dtype == f32 else two_words(tail)


def two_words(denom):
    high = denom.astype(bf16).astype(f32)
    return (high + pltpu.roll(denom - high, LOW, 1)).astype(bf16)


def attend(remote, place, block_mask, query, lines, after=()):
    tok = query.shape[-2]
    rows = GQ * tok
    keys = sum(line.shape[0] for line in lines)

    def of_query(i, place, block_mask):
        yh, core = query_member(place, remote, i)
        return 0, core, 0, yh, 0, 0

    slots = len(OFFSETS) * ZH + BATCH
    return pl.pallas_call(
        functools.partial(attend_kernel, remote),
        grid_spec=pltpu.PrefetchScalarGridSpec(
            num_scalar_prefetch=2,
            grid=(CORE,),
            in_specs=[pl.BlockSpec((YH, 1, PAIR, 1, tok, HD), of_query)]
            + [pl.BlockSpec(memory_space=pl.ANY)] * (len(lines) + len(after)),
            out_specs=(pl.BlockSpec((tok, WIDTH), lambda i, *_: (0, 0)),) * CORE,
            scratch_shapes=[
                pltpu.VMEM((keys, 2 * HD), bf16),
                pltpu.VMEM((rows, HD), f32),
                pltpu.VMEM((rows, BLOCK), f32),
                pltpu.SMEM((slots,), jnp.int32),
                pltpu.SMEM((slots,), jnp.int32),
                pltpu.SemaphoreType.DMA((len(lines),)),
            ],
        ),
        out_shape=(
            jax.ShapeDtypeStruct((tok, WIDTH), f32 if remote else bf16),
            jax.ShapeDtypeStruct((tok, WIDTH), f32),
        ),
        compiler_params=params(),
        cost_estimate=pl.CostEstimate(
            flops=4 * CORE * rows * keys * HD,
            bytes_accessed=4 * keys * HD,
            transcendentals=CORE * rows * keys,
        ),
        name="attend_remote" if remote else "attend_local",
    )(place, block_mask, query, *lines, *after)


def fold_kernel(place, own, both, out):
    got = both.at[1 - place[4]]
    out[:, : GQ * HD] = (own[:, : GQ * HD] + got[:, : GQ * HD]).astype(bf16)
    out[:, GQ * HD :] = two_words(own[:, GQ * HD :] + got[:, GQ * HD :])


def fold(place, own, both):
    return pl.pallas_call(
        fold_kernel,
        in_specs=specs(2),
        out_shape=jax.ShapeDtypeStruct(own.shape, bf16),
        compiler_params=params(),
        name="fold",
    )(place, own, both)


def combine_kernel(place, own, both, far, out):
    got = both.at[1 - place[4]]
    tail = own[:, GQ * HD :] + got[:, GQ * HD :].astype(f32) + far[:, GQ * HD :].astype(f32)
    for head in range(GQ):
        at = slice(head * HD, (head + 1) * HD)
        numer = own[:, at] + got[:, at].astype(f32) + far[:, at].astype(f32)
        denom = tail[:, head : head + 1] + tail[:, head + LOW : head + LOW + 1]
        out[:, at] = (numer / denom).astype(bf16)


def combine(place, own, both, far):
    return pl.pallas_call(
        combine_kernel,
        in_specs=specs(3),
        out_shape=jax.ShapeDtypeStruct((own.shape[0], GQ * HD), bf16),
        compiler_params=params(),
        name="combine",
    )(place, own, both, far)


def local(hidden, qkv_weight, query_gain, key_gain, positions, block_mask):
    tok, depth = hidden.shape
    share = qkv_weight.shape[0]
    yh, zh, zl, core = (lax.axis_index(a) for a in DP)
    place = jnp.stack([yh, yh * CORE + core, zh, zl, core]).astype(jnp.int32)

    with jax.named_scope("weights"):
        got = lax.all_to_all(pack(qkv_weight), ("yh", "c", "x", "yl"), 0, 0)
        got, sent = lax.optimization_barrier((got, hidden))
        far = swap(sent, "yh")
        rows = CORE * KV * share
        q_rows = got[:, :, :HD].reshape(YH * rows, HD)
        kv_rows = lax.dynamic_index_in_dim(
            got.reshape(YH, CORE * KV, share, 2 * HD), yh, 0, keepdims=False
        )[:, :, HD:].reshape(rows, HD)
        q_weight = lax.all_gather(q_rows, Z, axis=0, tiled=False)
        q_weight = q_weight.reshape(NZ, YH, rows, HD)
        kv_weight = lax.all_gather(kv_rows, Z, axis=0, tiled=True)

    hiddens = (hidden, far)

    inverse = 1000000.0 ** (-(jnp.arange(HD // 2, dtype=f32) * 2.0) / HD)
    own = []
    for rel in range(YH):
        first = ((yh ^ rel) * NZ + zh * ZL + zl) * CORE + core
        own.append(lax.dynamic_slice_in_dim(positions, first * tok, tok, 0))
    angles = jnp.stack(own).astype(f32)[:, :, None] * inverse
    cosine, sine = jnp.cos(angles), jnp.sin(angles)
    cosine = jnp.concatenate([cosine, cosine], axis=-1)
    sine = jnp.concatenate([-sine, sine], axis=-1)

    with jax.named_scope("keys_values"):
        other = swap(kv_weight, "c")
        first = kv_first(place, hiddens, kv_weight)
        keep, send = kv_second(place, hiddens, other, first)
        sent = lax.all_gather(send, "yh", axis=0, tiled=False)
        keys, values, both = kv_finish(
            place, keep, sent, key_gain.reshape(1, HD), cosine, sine
        )
        line = lax.all_gather(both, "zh", axis=0, tiled=True)
        line, q_weight = lax.optimization_barrier((line, q_weight))
        q_other = swap(q_weight, "c")
        across = from_z_both(line, 2)
        gathered = (line, from_z(line, 1), from_z(line, -1), across)

    with jax.named_scope("queries"):
        query = q_project(place, hiddens, (q_weight, q_other), query_gain.reshape(1, HD), cosine, sine)
        query = lax.all_gather(query, ("yh", "c"), axis=0, tiled=False)
        query = query.reshape(YH, CORE, PAIR, YH, tok, HD)

    with jax.named_scope("context"):
        peer, own = attend(True, place, block_mask, query, gathered)
        both = lax.all_gather(peer, "c", axis=0, tiled=False)
        folded = fold(place, own, both)
        far_part = lax.ppermute(folded, "yh", [(0, 1)])
        peer, own = attend(False, place, block_mask, query, gathered, (folded,))
        both = lax.all_gather(peer, "c", axis=0, tiled=False)
        context = combine(place, own, both, far_part)
    return keys, values, context


def solution(mesh):
    fine = Mesh(mesh.devices.reshape(YH, ZH, ZL, CORE, X, YL), DP[:3] + ("c",) + TENSOR)
    return jax.shard_map(
        local,
        mesh=fine,
        in_specs=(P(DP, None), P(DP + TENSOR, None), P(), P(), P(), P()),
        out_specs=(P(DP, TENSOR), P(DP, TENSOR), P(DP, TENSOR)),
        check_vma=False,
    )
```

time: 162 us -> 151 us (0.932)
  waiting for transfers between devices: 12.9 us -> 0.04 us
  blocking collectives: 84.9 us -> 91.2 us
  Pallas kernels: 17 us -> 14.1 us
    all_gather x0 -> x3, blocking collectives: none -> 12.4 us  [the longest x1 7.3 us: local(): sent = lax.all_gather(send, 'yh', axis=0, tiled=False)]
    all_to_all x1 -> x0, waiting for transfers between devices: 5.46 us -> none  [local(): parts = lax.all_to_all(parts, ('yh', 'c'), 0, 0)]
    ppermute x1, waiting for transfers between devices: 4.13 us -> 0.01 us  [local(): far_part = lax.ppermute(folded, 'yh', [(0, 1)])]
    all_to_all x1 -> x0, starting transfers between devices: 3.86 us -> none  [local(): parts = lax.all_to_all(parts, ('yh', 'c'), 0, 0)]
    ppermute x4 -> x3, waiting for transfers between devices: 3.22 us -> 0.01 us  [swap(): return lax.ppermute(inputs, axis, [(0, 1), (1, 0)])]
    all_gather x1, blocking collectives: 19.7 us -> 16.8 us  [local(): line = lax.all_gather(both, 'zh', axis=0, tiled=True)]
    pallas_call x2, Pallas kernels: 8.5 us -> 6.31 us  [attend(): pl.pallas_call(functools.partial(attend_kernel, remote), grid_spec=pltpu....]
    ppermute x2, starting transfers between devices: 5.27 us -> 7.36 us  [from_z(): return lax.ppermute(inputs, Z, [(i, (i - offset) % NZ) for i in range(NZ)])]
  transfers between devices with their start and end apart: 10 -> 8, of which waited for: 4 -> 0; matrix products, arithmetic and copies ran while one was open for 2% -> 1% of each run, Pallas kernels for 7% -> 5%
where the time goes in v3:
time: 151 us; the launch traced here: 150 us
  blocking collectives  91.2 us (60%)
  starting transfers between devices  25.2 us (17%)
  between operations  14.3 us (9%)
  Pallas kernels  14.1 us (9%)
  local copies, waits for them, and re-layouts  3.95 us (3%)
    all_gather x1, blocking collectives, local(): kv_weight = lax.all_gather(kv_rows, Z, axis=0, tiled=True)  34.2 us
    all_to_all x1, blocking collectives, local(): got = lax.all_to_all(pack(qkv_weight), ('yh', 'c', 'x', 'yl'), 0, 0)  18.3 us
    all_gather x1, blocking collectives, local(): line = lax.all_gather(both, 'zh', axis=0, tiled=True)  16.8 us
    ppermute x3, starting transfers between devices, swap(): return lax.ppermute(inputs, axis, [(0, 1), (1, 0)])  14.6 us
    all_gather x1, blocking collectives, local(): query = lax.all_gather(query, ('yh', 'c'), axis=0, tiled=False)  9.58 us
    ppermute x2, starting transfers between devices, from_z(): return lax.ppermute(inputs, Z, [(i, (i - offset) % NZ) for i in range(NZ)])  7.36 us
    all_gather x1, blocking collectives, local(): sent = lax.all_gather(send, 'yh', axis=0, tiled=False)  7.3 us
    pallas_call x2, Pallas kernels, attend(): pl.pallas_call(functools.partial(attend_kernel, remote), grid_spec=pltpu....  6.31 us
  transfers between devices with their start and end apart: 8, of which 0 were waited for; matrix products, arithmetic and copies ran while one was open for 1% of the time, Pallas kernels for 5%

profile of v3, /device:TPU:1, one launch (start us, length us, event | category | flops | bytes accessed | tf_op | source)
XLA Modules:
  0.0 149.6 jit_solution(7499011611380631636)
XLA Ops:
  7.2 0.0 all-gather.6.cloned.1.call-start
  7.2 1.0 copy-done.2
  8.3 18.3 %all_to_all.5 = bf16[32,10,256]{2,1,0:T(8,128)(2,1)S(1)} all-to-all(bf16[32,10,256]{2,1,0:T(8,128)(2,1)S(1)} %pack.1), channel_id=1, replica_groups=mesh['yh'=2,'zh'=4,'zl'=4,'c'=2,'x'=4,'yl'=2] {'yh','c','x','yl'}, dimensions={0} | all-to-all | bytes 327680 | tf_op jit(solution)/shard_map/weights/all_to_all | solution.py:361
  26.6 0.7 reshape.54
  27.3 0.0 all-gather.6.cloned.1.call-update
  27.3 3.3 %collective-permute-start = (bf16[128,5120]{1,0:T(8,128)(2,1)S(1)}, bf16[128,5120]{1,0:T(8,128)(2,1)S(1)}, u32[]{:S(2)}, u32[]{:S(2)}) collective-permute-start(bf16[128,5120]{1,0:T(8,128)(2,1)S(1)} %copy-done), channel_id=1, source_target_pairs={{0,256},{256,0},{1,257},{257,1},{2,258},{258,2},{3,259},{259,3},{4... | collective-permute-start | bytes 3932168 | tf_op jit(solution)/shard_map/weights/ppermute | solution.py:31
  30.7 0.1 stack.32.place
  30.8 34.2 %all_gather.33.weight = bf16[2560,128]{1,0:T(8,128)(2,1)S(1)} all-gather(bf16[160,128]{1,0:T(8,128)(2,1)S(1)} %reshape.52), channel_id=1, replica_groups=mesh['yh'=2,'zh'=4,'zl'=4,'c'=2,'x'=4,'yl'=2] {'zh','zl'}, dimensions={0}, use_global_device_ids=true | all-gather | bytes 696320 | tf_op jit(solution)/shard_map/weights/all_gather | solution.py:371
  65.0 6.3 %collective-permute-start.1 = (bf16[2560,128]{1,0:T(8,128)(2,1)S(1)}, bf16[2560,128]{1,0:T(8,128)(2,1)S(1)}, u32[]{:S(2)}, u32[]{:S(2)}) collective-permute-start(bf16[2560,128]{1,0:T(8,128)(2,1)S(1)} %all_gather.33.weight), channel_id=1, source_target_pairs={{0,8},{8,0},{1,9},{9,1},{2,10},{10,2},{3,11},{11,3},{4,12},{12,4},... | collective-permute-start | bytes 1966088 | tf_op jit(solution)/shard_map/keys_values/ppermute | solution.py:31
  71.3 0.8 dynamic-slice_bitcast_fusion.2
  72.1 0.5 fusion
  72.7 0.1 pad_maximum_fusion
  72.8 1.0 kv_first.1.first
  73.9 1.0 kv_second.1
  74.9 0.0 copy-start.4
  74.9 7.3 %all-gather = f32[256,256]{1,0:T(8,128)S(1)} all-gather(f32[128,256]{1,0:T(8,128)S(1)} %get-tuple-element.19), channel_id=2, replica_groups=mesh['yh'=2,'zh'=4,'zl'=4,'c'=2,'x'=4,'yl'=2] {'yh'}, dimensions={0}, use_global_device_ids=true | all-gather | bytes 393216 | tf_op jit(solution)/shard_map/keys_values/all_gather | solution.py:389
  82.2 1.3 kv_finish.1
  83.6 16.8 %all_gather.36.refs_0_ = bf16[512,256]{1,0:T(8,128)(2,1)S(1)} all-gather(bf16[128,256]{1,0:T(8,128)(2,1)S(1)} %get-tuple-element.22), channel_id=1, replica_groups=mesh['yh'=2,'zh'=4,'zl'=4,'c'=2,'x'=4,'yl'=2] {'zh'}, dimensions={0}, use_global_device_ids=true | all-gather | bytes 327680 | tf_op jit(solution)/shard_map/keys_values/all_gather | solution.py:393
  100.4 5.0 %collective-permute-start.2 = (bf16[16,2,160,128]{3,2,1,0:T(8,128)(2,1)}, bf16[16,2,160,128]{3,2,1,0:T(8,128)(2,1)S(1)}, u32[]{:S(2)}, u32[]{:S(2)}) collective-permute-start(bf16[16,2,160,128]{3,2,1,0:T(8,128)(2,1)} %bitcast.21), channel_id=1, source_target_pairs={{0,8},{8,0},{1,9},{9,1},{2,10},{10,2},{3,11},{11,3},{4,12},{12,4},... | collective-permute-start | bytes 3932168 | tf_op jit(solution)/shard_map/keys_values/ppermute | solution.py:31
  105.4 5.4 %collective-permute-start.3 = (bf16[512,256]{1,0:T(8,128)(2,1)S(1)}, bf16[512,256]{1,0:T(8,128)(2,1)S(1)}, u32[]{:S(2)}, u32[]{:S(2)}) collective-permute-start(bf16[512,256]{1,0:T(8,128)(2,1)S(1)} %all_gather.36.refs_0_), channel_id=1, source_target_pairs={{0,240},{16,0},{32,16},{48,32},{64,48},{80,64},{96,80},{112,96},{1... | collective-permute-start | bytes 786440 | tf_op jit(solution)/shard_map/keys_values/ppermute | solution.py:35
  110.8 1.9 %collective-permute-start.4 = (bf16[512,256]{1,0:T(8,128)(2,1)S(1)}, bf16[512,256]{1,0:T(8,128)(2,1)S(1)}, u32[]{:S(2)}, u32[]{:S(2)}) collective-permute-start(bf16[512,256]{1,0:T(8,128)(2,1)S(1)} %all_gather.36.refs_0_), channel_id=1, source_target_pairs={{0,16},{16,32},{32,48},{48,64},{64,80},{80,96},{96,112},{112,128},... | collective-permute-start | bytes 786440 | tf_op jit(solution)/shard_map/keys_values/ppermute | solution.py:35
  112.8 1.9 %collective-permute-start.5 = (bf16[512,256]{1,0:T(8,128)(2,1)S(1)}, bf16[512,256]{1,0:T(8,128)(2,1)S(1)}, u32[]{:S(2)}, u32[]{:S(2)}) collective-permute-start(bf16[512,256]{1,0:T(8,128)(2,1)S(1)} %all_gather.36.refs_0_), channel_id=1, source_target_pairs={{0,224},{8,40},{16,240},{24,56},{32,0},{40,72},{48,16},{56,88},{64... | collective-permute-start | bytes 786440 | tf_op jit(solution)/shard_map/keys_values/ppermute | solution.py:44
  114.7 1.3 copy-done.1
  116.0 2.3 %q_project.1 = bf16[2,2,128,128]{3,2,1,0:T(8,128)(2,1)S(1)} custom-call(s32[5]{0:T(128)S(1)} %stack.32.place, bf16[128,5120]{1,0:T(8,128)(2,1)S(1)} %copy-done, bf16[128,5120]{1,0:T(8,128)(2,1)S(1)} %collective-permute-done.h1, bf16[16,2,160,128]{3,2,1,0:T(8,128)(2,1)S(1)} %bitcast.22, bf16[16,2,160,128]{3,2,1,0:T(8,128)(2,1)S(1)} %collective-permute-done.2.other, ...), custom_call_target="tpu_custom_call" | custom-call | tf_op jit(solution)/shard_map/queries/q_project/pallas_call | solution.py:171
  118.3 9.6 %all-gather.1 = bf16[8,2,128,128]{3,2,1,0:T(8,128)(2,1)S(1)} all-gather(bf16[2,2,128,128]{3,2,1,0:T(8,128)(2,1)S(1)} %q_project.1), channel_id=3, replica_groups=mesh['yh'=2,'zh'=4,'zl'=4,'c'=2,'x'=4,'yl'=2] {'yh','c'}, dimensions={0}, use_global_device_ids=true | all-gather | bytes 655360 | tf_op jit(solution)/shard_map/queries/all_gather | solution.py:401
  127.9 3.9 %attend_remote.1 = (f32[128,640]{1,0:T(8,128)S(1)}, f32[128,640]{1,0:T(8,128)S(1)}) custom-call(s32[5]{0:T(128)S(1)} %stack.32.place, s32[64,64]{1,0:T(8,128)S(1)} %copy-done.5, bf16[2,2,2,2,128,128]{5,4,3,2,1,0:T(8,128)(2,1)S(1)} %bitcast.24, bf16[512,256]{1,0:T(8,128)(2,1)S(1)} %all_gather.36.refs_0_, bf16[512,256]{1,0:T(8,128)(2,1)S(1)} %collective-permute-done.3.refs_1_, ...), custom_call_target="tpu_custom_call" | custom-call | flops 1073741824 | bytes 1048576 | tf_op jit(solution)/shard_map/context/attend_remote/pallas_call | solution.py:287
  131.8 3.0 %all-gather.2 = f32[256,640]{1,0:T(8,128)S(1)} all-gather(f32[128,640]{1,0:T(8,128)S(1)} %get-tuple-element.26), channel_id=4, replica_groups=mesh['yh'=2,'zh'=4,'zl'=4,'c'=2,'x'=4,'yl'=2] {'c'}, dimensions={0}, use_global_device_ids=true | all-gather | bytes 983040 | tf_op jit(solution)/shard_map/context/all_gather | solution.py:406
  134.8 0.7 fold.1.refs_4_
  135.5 1.3 collective-permute-start.6
  136.8 2.5 %attend_local.1 = (bf16[128,640]{1,0:T(8,128)(2,1)S(1)}, f32[128,640]{1,0:T(8,128)S(1)}) custom-call(s32[5]{0:T(128)S(1)} %stack.32.place, s32[64,64]{1,0:T(8,128)S(1)} %copy-done.5, bf16[2,2,2,2,128,128]{5,4,3,2,1,0:T(8,128)(2,1)S(1)} %bitcast.25, bf16[512,256]{1,0:T(8,128)(2,1)S(1)} %all_gather.36.refs_0_, ...), custom_call_target="tpu_custom_call" | custom-call | flops 1073741824 | bytes 1048576 | tf_op jit(solution)/shard_map/context/attend_local/pallas_call | solution.py:287
  139.2 2.0 %all-gather.3 = bf16[256,640]{1,0:T(8,128)(2,1)S(1)} all-gather(bf16[128,640]{1,0:T(8,128)(2,1)S(1)} %get-tuple-element.28), channel_id=5, replica_groups=mesh['yh'=2,'zh'=4,'zl'=4,'c'=2,'x'=4,'yl'=2] {'c'}, dimensions={0}, use_global_device_ids=true | all-gather | bytes 491520 | tf_op jit(solution)/shard_map/context/all_gather | solution.py:410
  141.3 1.4 combine.1
  (24 shorter events, 0.2 us)
Async XLA Ops:
  7.2 20.1 %copy-start = (bf16[128,5120]{1,0:T(8,128)(2,1)S(1)}, bf16[128,5120]{1,0:T(8,128)(2,1)}, u32[]{:S(2)}) copy-start(bf16[128,5120]{1,0:T(8,128)(2,1)} %h0.5) | copy-start | bytes 3932164
  7.2 93.2 %all-gather.6.cloned.1.call-start = ((), (), s32[]{:S(2)}) async-start(), calls=%async_computation.1 | async-start | bytes 1392640 | tf_op jit(solution)/shard_map/weights/all_gather | solution.py:369
  7.2 1.0 copy-start.2
  27.3 45.5 %collective-permute-start = (bf16[128,5120]{1,0:T(8,128)(2,1)S(1)}, bf16[128,5120]{1,0:T(8,128)(2,1)S(1)}, u32[]{:S(2)}, u32[]{:S(2)}) collective-permute-start(bf16[128,5120]{1,0:T(8,128)(2,1)S(1)} %copy-done), channel_id=1, source_target_pairs={{0,256},{256,0},{1,257},{257,1},{2,258},{258,2},{3,259},{259,3},{4... | collective-permute-start | bytes 3932168 | tf_op jit(solution)/shard_map/weights/ppermute | solution.py:31
  65.0 8.9 %collective-permute-start.1 = (bf16[2560,128]{1,0:T(8,128)(2,1)S(1)}, bf16[2560,128]{1,0:T(8,128)(2,1)S(1)}, u32[]{:S(2)}, u32[]{:S(2)}) collective-permute-start(bf16[2560,128]{1,0:T(8,128)(2,1)S(1)} %all_gather.33.weight), channel_id=1, source_target_pairs={{0,8},{8,0},{1,9},{9,1},{2,10},{10,2},{3,11},{11,3},{4,12},{12,4},... | collective-permute-start | bytes 1966088 | tf_op jit(solution)/shard_map/keys_values/ppermute | solution.py:31
  73.9 8.4 %copy-start.3 = (f32[128]{0:T(128)S(1)}, f32[128]{0:T(128)}, u32[]{:S(2)}) copy-start(f32[128]{0:T(128)} %param.9) | copy-start | bytes 1540
  74.9 39.8 %copy-start.4 = (f32[128]{0:T(128)S(1)}, f32[128]{0:T(128)}, u32[]{:S(2)}) copy-start(f32[128]{0:T(128)} %param.8) | copy-start | bytes 1540
  100.4 14.3 %collective-permute-start.2 = (bf16[16,2,160,128]{3,2,1,0:T(8,128)(2,1)}, bf16[16,2,160,128]{3,2,1,0:T(8,128)(2,1)S(1)}, u32[]{:S(2)}, u32[]{:S(2)}) collective-permute-start(bf16[16,2,160,128]{3,2,1,0:T(8,128)(2,1)} %bitcast.21), channel_id=1, source_target_pairs={{0,8},{8,0},{1,9},{9,1},{2,10},{10,2},{3,11},{11,3},{4,12},{12,4},... | collective-permute-start | bytes 3932168 | tf_op jit(solution)/shard_map/keys_values/ppermute | solution.py:31
  105.4 22.5 %collective-permute-start.3 = (bf16[512,256]{1,0:T(8,128)(2,1)S(1)}, bf16[512,256]{1,0:T(8,128)(2,1)S(1)}, u32[]{:S(2)}, u32[]{:S(2)}) collective-permute-start(bf16[512,256]{1,0:T(8,128)(2,1)S(1)} %all_gather.36.refs_0_), channel_id=1, source_target_pairs={{0,240},{16,0},{32,16},{48,32},{64,48},{80,64},{96,80},{112,96},{1... | collective-permute-start | bytes 786440 | tf_op jit(solution)/shard_map/keys_values/ppermute | solution.py:35
  110.8 17.1 %collective-permute-start.4 = (bf16[512,256]{1,0:T(8,128)(2,1)S(1)}, bf16[512,256]{1,0:T(8,128)(2,1)S(1)}, u32[]{:S(2)}, u32[]{:S(2)}) collective-permute-start(bf16[512,256]{1,0:T(8,128)(2,1)S(1)} %all_gather.36.refs_0_), channel_id=1, source_target_pairs={{0,16},{16,32},{32,48},{48,64},{64,80},{80,96},{96,112},{112,128},... | collective-permute-start | bytes 786440 | tf_op jit(solution)/shard_map/keys_values/ppermute | solution.py:35
  112.8 15.1 %collective-permute-start.5 = (bf16[512,256]{1,0:T(8,128)(2,1)S(1)}, bf16[512,256]{1,0:T(8,128)(2,1)S(1)}, u32[]{:S(2)}, u32[]{:S(2)}) collective-permute-start(bf16[512,256]{1,0:T(8,128)(2,1)S(1)} %all_gather.36.refs_0_), channel_id=1, source_target_pairs={{0,224},{8,40},{16,240},{24,56},{32,0},{40,72},{48,16},{56,88},{64... | collective-permute-start | bytes 786440 | tf_op jit(solution)/shard_map/keys_values/ppermute | solution.py:44
  114.7 1.3 copy-start.1
  116.0 11.9 %copy-start.5 = (s32[64,64]{1,0:T(8,128)S(1)}, s32[64,64]{1,0:T(8,128)}, u32[]{:S(2)}) copy-start(s32[64,64]{1,0:T(8,128)} %block_mask.3) | copy-start | bytes 49156
  135.5 5.8 %collective-permute-start.6 = (bf16[128,640]{1,0:T(8,128)(2,1)S(1)}, bf16[128,640]{1,0:T(8,128)(2,1)S(1)}, u32[]{:S(2)}, u32[]{:S(2)}) collective-permute-start(bf16[128,640]{1,0:T(8,128)(2,1)S(1)} %fold.1.refs_4_), channel_id=1, source_target_pairs={{0,256},{1,257},{2,258},{3,259},{4,260},{5,261},{6,262},{7,263},{8... | collective-permute-start | bytes 491528 | tf_op jit(solution)/shard_map/context/ppermute | solution.py:408
Sparse Core Ops, SparseCore 0:
  27.4 62.7 all-gather.5

commit v4 on v3

v4 whole, which is shorter than its diff:
```python
import functools
import math

import jax
import jax.numpy as jnp
from jax import lax
from jax.experimental import pallas as pl
from jax.experimental.pallas import tpu as pltpu
from jax.sharding import Mesh, PartitionSpec as P

HD = 128
BLOCK = 128
GQ = 4
PAIR = 2
KV = 8
YH, ZH, ZL, CORE, X, YL = 2, 4, 4, 2, 4, 2
NZ = ZH * ZL
GROUP = YH * CORE
DP = ("yh", "zh", "zl", "c")
TENSOR = ("x", "yl")
Z = ("zh", "zl")
bf16 = jnp.bfloat16
f32 = jnp.float32


def params():
    return pltpu.CompilerParams(vmem_limit_bytes=24 * 1024 * 1024)


def swap(inputs, axis):
    return lax.ppermute(inputs, axis, [(0, 1), (1, 0)])


def from_z(inputs, offset):
    return lax.ppermute(inputs, Z, [(i, (i - offset) % NZ) for i in range(NZ)])


def from_z_both(inputs, offset):
    pairs = [
        (i * CORE + core, (i - (1 - 2 * core) * offset) % NZ * CORE + core)
        for i in range(NZ)
        for core in range(CORE)
    ]
    return lax.ppermute(inputs, Z + ("c",), pairs)


def norm_rope(inputs, gain, cosine, sine):
    meansq = jnp.mean(inputs * inputs, axis=-1, keepdims=True)
    normed = inputs * lax.rsqrt(meansq + 1e-06) * gain
    return normed * cosine + pltpu.roll(normed, HD // 2, 1) * sine


def pack_kernel(weight, out):
    for yh in range(YH):
        for head in range(KV):
            first = head * (GQ + 2)
            for i, slot in enumerate((first + yh * PAIR, first + GQ)):
                out[yh * KV + head, :, i * PAIR * HD : (i + 1) * PAIR * HD] = weight[
                    :, slot * HD : (slot + PAIR) * HD
                ]


def pack(weight):
    return pl.pallas_call(
        pack_kernel,
        out_shape=jax.ShapeDtypeStruct(
            (YH * KV, weight.shape[0], 2 * PAIR * HD), weight.dtype
        ),
        compiler_params=params(),
        name="pack",
    )(weight)


def kv_partial_kernel(h0, h1, mine, other, keep, send, weight):
    core = lax.axis_index("c")
    nz, _, share, wide = weight.shape
    half = nz * CORE * share
    weight[:, core] = mine[...].reshape(nz, share, wide)
    weight[:, 1 - core] = other[...].reshape(nz, share, wide)
    columns = pl.ds(pl.multiple_of(lax.axis_index("yh") * half, half), half)
    whole = weight[...].reshape(half, wide)
    for rows, out in ((h0, keep), (h1, send)):
        out[...] = jnp.dot(rows[:, columns], whole, preferred_element_type=f32)


def kv_partial(hiddens, mine, other):
    tok = hiddens[0].shape[0]
    shape = jax.ShapeDtypeStruct((tok, 2 * HD), f32)
    return pl.pallas_call(
        kv_partial_kernel,
        out_shape=(shape, shape),
        scratch_shapes=[pltpu.VMEM((NZ, CORE, mine.shape[0] // NZ, mine.shape[1]), bf16)],
        compiler_params=params(),
        name="kv_partial",
    )(*hiddens, mine, other)


def kv_finish_kernel(keep, sent, gain, cosine, sine, keys, values, both):
    total = keep[...] + sent[1 - lax.axis_index("yh")]
    key = norm_rope(total[:, :HD], gain[...], cosine[0], sine[0]).astype(bf16)
    value = total[:, HD:].astype(bf16)
    keys[...] = key
    values[...] = value
    both[:, :HD] = key
    both[:, HD:] = value


def kv_finish(keep, sent, gain, cosine, sine):
    tok = keep.shape[0]
    return pl.pallas_call(
        kv_finish_kernel,
        out_shape=(
            jax.ShapeDtypeStruct((tok, HD), bf16),
            jax.ShapeDtypeStruct((tok, HD), bf16),
            jax.ShapeDtypeStruct((tok, 2 * HD), bf16),
        ),
        compiler_params=params(),
        name="kv_finish",
    )(keep, sent, gain, cosine, sine)


def q_project_kernel(h0, h1, gain, cosine, sine, mine, other, out, weight, sem):
    yh, core = lax.axis_index("yh"), lax.axis_index("c")
    half = h0.shape[1] // YH
    copies = [
        pltpu.make_async_copy(source.at[:, i], weight.at[i, :, owner], sem.at[i, flip])
        for i in range(YH)
        for flip, (source, owner) in enumerate(((mine, core), (other, 1 - core)))
    ]
    for copy in copies:
        copy.start()
    totals = [None] * YH
    for i in range(YH):
        for copy in copies[i * CORE : (i + 1) * CORE]:
            copy.wait()
        columns = weight[i].reshape(half, PAIR * HD)
        for rel, rows in enumerate((h0, h1)):
            part = jnp.dot(
                rows[:, i * half : (i + 1) * half], columns, preferred_element_type=f32
            )
            totals[rel] = part if i == 0 else totals[rel] + part
    for rel, total in enumerate(totals):
        for head in range(PAIR):
            out[head, yh ^ rel] = norm_rope(
                total[:, head * HD : (head + 1) * HD], gain[...], cosine[rel], sine[rel]
            ).astype(bf16)


def q_project(hiddens, weights, gain, cosine, sine):
    tok = hiddens[0].shape[0]
    nz, halves, share, wide = weights[0].shape
    return pl.pallas_call(
        q_project_kernel,
        in_specs=[pl.BlockSpec(memory_space=pltpu.VMEM)] * (YH + 3)
        + [pl.BlockSpec(memory_space=pl.ANY)] * CORE,
        out_shape=jax.ShapeDtypeStruct((PAIR, YH, tok, HD), bf16),
        scratch_shapes=[
            pltpu.VMEM((halves, nz, CORE, share, wide), bf16),
            pltpu.SemaphoreType.DMA((halves, CORE)),
        ],
        compiler_params=params(),
        name="q_project",
    )(*hiddens, gain, cosine, sine, *weights)


OFFSETS = (0, 1, -1, 2)
BATCH = 4
WIDTH = (GQ + 1) * HD
LOW = 64


def attend_kernel(remote, masks, query, *refs):
    lines = refs[: len(OFFSETS)]
    peer, own, key_value, numer, total, limit_at = refs[-6:]
    yh, zh, zl, core = (lax.axis_index(a) for a in DP)
    query_yh = 1 - yh if remote else yh
    ahead = lax.broadcasted_iota(jnp.int32, (GQ * BLOCK, BLOCK), 1) - lax.rem(
        lax.broadcasted_iota(jnp.int32, (GQ * BLOCK, BLOCK), 0), BLOCK
    )
    lane = lax.broadcasted_iota(jnp.int32, (BLOCK, HD), 1)
    for query_core, out in ((1 - core, peer), (core, own)):
        query_block = query_yh * (NZ * CORE) + (zh * ZL + zl) * CORE + query_core
        count = jnp.int32(0)
        for i, offset in enumerate(OFFSETS):
            for j in range(ZH):
                z_at = j * ZL + lax.rem(zl + (offset + ZL), ZL)
                key_block = yh * (NZ * CORE) + z_at * CORE + core
                live = (masks[query_core, key_block] == 1) & (key_block <= query_block)

                @pl.when(live)
                def _(i=i, j=j, count=count, key_block=key_block, query_block=query_block):
                    there = pl.ds(pl.multiple_of(count * BLOCK, BLOCK), BLOCK)
                    key_value[there, :] = lines[i][j * BLOCK : (j + 1) * BLOCK, :]
                    limit_at[count] = jnp.where(key_block == query_block, 0, 2 * BLOCK)

                count = count + live.astype(jnp.int32)
        for i in range(BATCH - 1):
            there = pl.ds(pl.multiple_of((count + i) * BLOCK, BLOCK), BLOCK)
            key_value[there, :] = lines[0][:BLOCK, :]
            limit_at[count + i] = jnp.int32(-2 * BLOCK)

        rows = query[:, query_core, :, query_yh].reshape(GQ * BLOCK, HD)
        numer[...] = jnp.zeros_like(numer)
        total[...] = jnp.zeros_like(total)

        def batch(at, carry):
            first = at * BATCH
            limits = [limit_at[first + i] for i in range(BATCH)]
            there = pl.ds(pl.multiple_of(first * BLOCK, BATCH * BLOCK), BATCH * BLOCK)
            scores = lax.dot_general(
                rows,
                key_value[there, :HD],
                (((1,), (1,)), ((), ())),
                preferred_element_type=f32,
            )
            raised = jnp.exp2(scores * (math.log2(math.e) / math.sqrt(HD)))
            parts = [
                jnp.where(ahead <= limits[i], raised[:, i * BLOCK : (i + 1) * BLOCK], 0.0)
                for i in range(BATCH)
            ]
            total[...] += (parts[0] + parts[1]) + (parts[2] + parts[3])
            weights = jnp.concatenate([p.astype(bf16) for p in parts], axis=1)
            numer[...] += jnp.dot(weights, key_value[there, HD:], preferred_element_type=f32)
            return carry

        lax.fori_loop(0, (count + BATCH - 1) // BATCH, batch, 0)

        denom = jnp.sum(total[...], axis=1, keepdims=True)
        tail = jnp.zeros((BLOCK, HD), f32)
        for head in range(GQ):
            at = slice(head * BLOCK, (head + 1) * BLOCK)
            tail = jnp.where(lane == head, denom[at], tail)
            out[:, head * HD : (head + 1) * HD] = numer[at].astype(out.dtype)
        out[:, GQ * HD :] = tail if out.dtype == f32 else two_words(tail)


def two_words(denom):
    high = denom.astype(bf16).astype(f32)
    return (high + pltpu.roll(denom - high, LOW, 1)).astype(bf16)


def attend(remote, masks, query, lines, after=()):
    tok = query.shape[-2]
    rows = GQ * tok
    blocks = len(OFFSETS) * ZH + BATCH - 1
    in_vmem = pl.BlockSpec(memory_space=pltpu.VMEM)
    return pl.pallas_call(
        functools.partial(attend_kernel, remote),
        in_specs=[pl.BlockSpec(memory_space=pltpu.SMEM)]
        + [in_vmem] * (1 + len(lines))
        + [pl.BlockSpec(memory_space=pl.ANY)] * len(after),
        scratch_shapes=[
            pltpu.VMEM((blocks * BLOCK, 2 * HD), bf16),
            pltpu.VMEM((rows, HD), f32),
            pltpu.VMEM((rows, BLOCK), f32),
            pltpu.SMEM((blocks,), jnp.int32),
        ],
        out_shape=(
            jax.ShapeDtypeStruct((tok, WIDTH), f32 if remote else bf16),
            jax.ShapeDtypeStruct((tok, WIDTH), f32),
        ),
        compiler_params=params(),
        cost_estimate=pl.CostEstimate(
            flops=4 * CORE * rows * blocks * BLOCK * HD,
            bytes_accessed=4 * blocks * BLOCK * HD,
            transcendentals=CORE * rows * blocks * BLOCK,
        ),
        name="attend_remote" if remote else "attend_local",
    )(masks, query, *lines, *after)


def fold_kernel(own, both, out):
    got = both.at[1 - lax.axis_index("c")]
    out[:, : GQ * HD] = (own[:, : GQ * HD] + got[:, : GQ * HD]).astype(bf16)
    out[:, GQ * HD :] = two_words(own[:, GQ * HD :] + got[:, GQ * HD :])


def fold(own, both):
    return pl.pallas_call(
        fold_kernel,
        out_shape=jax.ShapeDtypeStruct(own.shape, bf16),
        compiler_params=params(),
        name="fold",
    )(own, both)


def combine_kernel(own, both, far, out):
    got = both.at[1 - lax.axis_index("c")]
    tail = own[:, GQ * HD :] + got[:, GQ * HD :].astype(f32) + far[:, GQ * HD :].astype(f32)
    for head in range(GQ):
        at = slice(head * HD, (head + 1) * HD)
        numer = own[:, at] + got[:, at].astype(f32) + far[:, at].astype(f32)
        denom = tail[:, head : head + 1] + tail[:, head + LOW : head + LOW + 1]
        out[:, at] = (numer / denom).astype(bf16)


def combine(own, both, far):
    return pl.pallas_call(
        combine_kernel,
        out_shape=jax.ShapeDtypeStruct((own.shape[0], GQ * HD), bf16),
        compiler_params=params(),
        name="combine",
    )(own, both, far)


def local(hidden, qkv_weight, query_gain, key_gain, positions, block_mask):
    tok, depth = hidden.shape
    share = qkv_weight.shape[0]
    yh, zh, zl, core = (lax.axis_index(a) for a in DP)
    with jax.named_scope("weights"):
        got = lax.all_to_all(pack(qkv_weight), ("yh", "x", "yl"), 0, 0)
        got, sent = lax.optimization_barrier((got, hidden))
        far = swap(sent, "yh")
        rows, wide = KV * share, PAIR * HD
        q_rows = got[:, :, :wide].reshape(YH * rows, wide)
        kv_rows = lax.dynamic_index_in_dim(
            got.reshape(YH, KV, share, 2 * wide), yh, 0, keepdims=False
        )[:, :, wide:].reshape(rows, wide)
        q_weight = lax.all_gather(q_rows, Z, axis=0, tiled=False)
        q_weight = q_weight.reshape(NZ, YH, rows, wide)
        kv_weight = lax.all_gather(kv_rows, Z, axis=0, tiled=True)

    hiddens = (hidden, far)

    inverse = 1000000.0 ** (-(jnp.arange(HD // 2, dtype=f32) * 2.0) / HD)
    own = []
    for rel in range(YH):
        first = ((yh ^ rel) * NZ + zh * ZL + zl) * CORE + core
        own.append(lax.dynamic_slice_in_dim(positions, first * tok, tok, 0))
    angles = jnp.stack(own).astype(f32)[:, :, None] * inverse
    cosine, sine = jnp.cos(angles), jnp.sin(angles)
    cosine = jnp.concatenate([cosine, cosine], axis=-1)
    sine = jnp.concatenate([-sine, sine], axis=-1)

    with jax.named_scope("keys_values"):
        keep, send = kv_partial(hiddens, kv_weight, swap(kv_weight, "c"))
        sent = lax.all_gather(send, "yh", axis=0, tiled=False)
        keys, values, both = kv_finish(
            keep, sent, key_gain.reshape(1, HD), cosine, sine
        )
        line = lax.all_gather(both, "zh", axis=0, tiled=True)
        line, q_weight = lax.optimization_barrier((line, q_weight))
        q_other = swap(q_weight, "c")
        across = from_z_both(line, 2)
        gathered = (line, from_z(line, 1), from_z(line, -1), across)

    with jax.named_scope("queries"):
        query = q_project(hiddens, (q_weight, q_other), query_gain.reshape(1, HD), cosine, sine)
        query = lax.all_gather(query, ("yh", "c"), axis=0, tiled=False)
        query = query.reshape(YH, CORE, PAIR, YH, tok, HD)

    def masks(query_yh):
        first = (query_yh * NZ + zh * ZL + zl) * CORE
        return lax.dynamic_slice_in_dim(block_mask, first, CORE, 0)

    with jax.named_scope("context"):
        peer, own = attend(True, masks(1 - yh), query, gathered)
        both = lax.all_gather(peer, "c", axis=0, tiled=False)
        folded = fold(own, both)
        far_part = lax.ppermute(folded, "yh", [(0, 1)])
        peer, own = attend(False, masks(yh), query, gathered, (folded,))
        both = lax.all_gather(peer, "c", axis=0, tiled=False)
        context = combine(own, both, far_part)
    return keys, values, context


def solution(mesh):
    fine = Mesh(mesh.devices.reshape(YH, ZH, ZL, CORE, X, YL), DP[:3] + ("c",) + TENSOR)
    return jax.shard_map(
        local,
        mesh=fine,
        in_specs=(P(DP, None), P(DP + TENSOR, None), P(), P(), P(), P()),
        out_specs=(P(DP, TENSOR), P(DP, TENSOR), P(DP, TENSOR)),
        check_vma=False,
    )
```

time: 151 us -> 147 us (0.974)
  Pallas kernels: 14.1 us -> 10.7 us
  blocking collectives: 91.2 us -> 88.7 us
  starting transfers between devices: 25.2 us -> 27.1 us
    all_to_all x1, blocking collectives: 18.3 us -> 14.8 us  [local(): got = lax.all_to_all(pack(qkv_weight), ('yh', 'x', 'yl'), 0, 0)]
    pallas_call x9 -> x8, Pallas kernels: 14.1 us -> 10.7 us  [the longest x2 5.8 us: attend(): pl.pallas_call(functools.partial(attend_kernel, remote), in_specs=[pl.Blo...]
    ppermute x3, starting transfers between devices: 14.6 us -> 17.3 us  [swap(): return lax.ppermute(inputs, axis, [(0, 1), (1, 0)])]
    ppermute x2, starting transfers between devices: 7.36 us -> 5.42 us  [from_z(): return lax.ppermute(inputs, Z, [(i, (i - offset) % NZ) for i in range(NZ)])]
    all_gather x1, blocking collectives: 16.8 us -> 18.4 us  [local(): line = lax.all_gather(both, 'zh', axis=0, tiled=True)]
  transfers between devices with their start and end apart: 8 -> 8, of which waited for: 0 -> 1; matrix products, arithmetic and copies ran while one was open for 1% -> 2% of each run, Pallas kernels for 5% -> 4%
where the time goes in v4:
time: 147 us; the launch traced here: 146 us
  blocking collectives  88.7 us (60%)
  starting transfers between devices  27.1 us (18%)
  between operations  14.3 us (10%)
  Pallas kernels  10.7 us (7%)
  local copies, waits for them, and re-layouts  4.57 us (3%)
    all_gather x1, blocking collectives, local(): kv_weight = lax.all_gather(kv_rows, Z, axis=0, tiled=True)  35 us
    all_gather x1, blocking collectives, local(): line = lax.all_gather(both, 'zh', axis=0, tiled=True)  18.4 us
    ppermute x3, starting transfers between devices, swap(): return lax.ppermute(inputs, axis, [(0, 1), (1, 0)])  17.3 us
    all_to_all x1, blocking collectives, local(): got = lax.all_to_all(pack(qkv_weight), ('yh', 'x', 'yl'), 0, 0)  14.8 us
    all_gather x1, blocking collectives, local(): query = lax.all_gather(query, ('yh', 'c'), axis=0, tiled=False)  9.19 us
    all_gather x1, blocking collectives, local(): sent = lax.all_gather(send, 'yh', axis=0, tiled=False)  6.89 us
    pallas_call x2, Pallas kernels, attend(): pl.pallas_call(functools.partial(attend_kernel, remote), in_specs=[pl.Blo...  5.8 us
    ppermute x2, starting transfers between devices, from_z(): return lax.ppermute(inputs, Z, [(i, (i - offset) % NZ) for i in range(NZ)])  5.42 us
  transfers between devices with their start and end apart: 8, of which 1 were waited for; matrix products, arithmetic and copies ran while one was open for 2% of the time, Pallas kernels for 4%

profile of v4, /device:TPU:1, one launch (start us, length us, event | category | flops | bytes accessed | tf_op | source)
XLA Modules:
  0.0 146.2 jit_solution(7528803654851811169)
XLA Ops:
  7.2 0.0 all-gather.6.cloned.1.call-start
  7.2 1.0 copy-done.2
  8.3 14.8 %all_to_all.5 = bf16[16,10,512]{2,1,0:T(8,128)(2,1)S(1)} all-to-all(bf16[16,10,512]{2,1,0:T(8,128)(2,1)S(1)} %pack.1), channel_id=1, replica_groups=mesh['yh'=2,'zh'=4,'zl'=4,'c'=2,'x'=4,'yl'=2] {'yh','x','yl'}, dimensions={0} | all-to-all | bytes 327680 | tf_op jit(solution)/shard_map/weights/all_to_all | solution.py:311
  23.0 0.7 reshape.55
  23.7 0.0 all-gather.6.cloned.1.call-update
  23.7 3.1 %collective-permute-start = (bf16[128,5120]{1,0:T(8,128)(2,1)S(1)}, bf16[128,5120]{1,0:T(8,128)(2,1)S(1)}, u32[]{:S(2)}, u32[]{:S(2)}) collective-permute-start(bf16[128,5120]{1,0:T(8,128)(2,1)S(1)} %copy-done), channel_id=1, source_target_pairs={{0,256},{256,0},{1,257},{257,1},{2,258},{258,2},{3,259},{259,3},{4... | collective-permute-start | bytes 3932168 | tf_op jit(solution)/shard_map/weights/ppermute | solution.py:31
  26.9 35.0 %all_gather.33.mine = bf16[1280,256]{1,0:T(8,128)(2,1)S(1)} all-gather(bf16[80,256]{1,0:T(8,128)(2,1)S(1)} %reshape.52), channel_id=1, replica_groups=mesh['yh'=2,'zh'=4,'zl'=4,'c'=2,'x'=4,'yl'=2] {'zh','zl'}, dimensions={0}, use_global_device_ids=true | all-gather | bytes 696320 | tf_op jit(solution)/shard_map/weights/all_gather | solution.py:321
  62.0 8.8 %collective-permute-start.1 = (bf16[1280,256]{1,0:T(8,128)(2,1)S(1)}, bf16[1280,256]{1,0:T(8,128)(2,1)S(1)}, u32[]{:S(2)}, u32[]{:S(2)}) collective-permute-start(bf16[1280,256]{1,0:T(8,128)(2,1)S(1)} %all_gather.33.mine), channel_id=1, source_target_pairs={{0,8},{8,0},{1,9},{9,1},{2,10},{10,2},{3,11},{11,3},{4,12},{12,4},... | collective-permute-start | bytes 1966088 | tf_op jit(solution)/shard_map/keys_values/ppermute | solution.py:31
  70.8 0.8 dynamic-slice_bitcast_fusion.2
  71.6 0.5 fusion
  72.1 0.1 pad_maximum_fusion
  72.3 0.0 copy-start.4
  72.3 0.2 collective-permute-done.1.other
  72.5 0.7 kv_partial.1
  73.2 6.9 %all-gather = f32[256,256]{1,0:T(8,128)S(1)} all-gather(f32[128,256]{1,0:T(8,128)S(1)} %get-tuple-element.19), channel_id=2, replica_groups=mesh['yh'=2,'zh'=4,'zl'=4,'c'=2,'x'=4,'yl'=2] {'yh'}, dimensions={0}, use_global_device_ids=true | all-gather | bytes 393216 | tf_op jit(solution)/shard_map/keys_values/all_gather | solution.py:337
  80.0 0.8 kv_finish.1
  80.8 18.4 %all_gather.36.refs_0_ = bf16[512,256]{1,0:T(8,128)(2,1)S(1)} all-gather(bf16[128,256]{1,0:T(8,128)(2,1)S(1)} %get-tuple-element.22), channel_id=1, replica_groups=mesh['yh'=2,'zh'=4,'zl'=4,'c'=2,'x'=4,'yl'=2] {'zh'}, dimensions={0}, use_global_device_ids=true | all-gather | bytes 327680 | tf_op jit(solution)/shard_map/keys_values/all_gather | solution.py:341
  99.3 5.4 %collective-permute-start.2 = (bf16[16,2,80,256]{3,2,1,0:T(8,128)(2,1)}, bf16[16,2,80,256]{3,2,1,0:T(8,128)(2,1)}, u32[]{:S(2)}, u32[]{:S(2)}) collective-permute-start(bf16[16,2,80,256]{3,2,1,0:T(8,128)(2,1)} %bitcast.15), channel_id=1, source_target_pairs={{0,8},{8,0},{1,9},{9,1},{2,10},{10,2},{3,11},{11,3},{4,12},{12,4},... | collective-permute-start | bytes 3932168 | tf_op jit(solution)/shard_map/keys_values/ppermute | solution.py:31
  104.7 3.5 %collective-permute-start.3 = (bf16[512,256]{1,0:T(8,128)(2,1)S(1)}, bf16[512,256]{1,0:T(8,128)(2,1)S(1)}, u32[]{:S(2)}, u32[]{:S(2)}) collective-permute-start(bf16[512,256]{1,0:T(8,128)(2,1)S(1)} %all_gather.36.refs_0_), channel_id=1, source_target_pairs={{0,240},{16,0},{32,16},{48,32},{64,48},{80,64},{96,80},{112,96},{1... | collective-permute-start | bytes 786440 | tf_op jit(solution)/shard_map/keys_values/ppermute | solution.py:35
  108.2 1.9 %collective-permute-start.4 = (bf16[512,256]{1,0:T(8,128)(2,1)S(1)}, bf16[512,256]{1,0:T(8,128)(2,1)S(1)}, u32[]{:S(2)}, u32[]{:S(2)}) collective-permute-start(bf16[512,256]{1,0:T(8,128)(2,1)S(1)} %all_gather.36.refs_0_), channel_id=1, source_target_pairs={{0,16},{16,32},{32,48},{48,64},{64,80},{80,96},{96,112},{112,128},... | collective-permute-start | bytes 786440 | tf_op jit(solution)/shard_map/keys_values/ppermute | solution.py:35
  110.1 2.5 %collective-permute-start.5 = (bf16[512,256]{1,0:T(8,128)(2,1)S(1)}, bf16[512,256]{1,0:T(8,128)(2,1)S(1)}, u32[]{:S(2)}, u32[]{:S(2)}) collective-permute-start(bf16[512,256]{1,0:T(8,128)(2,1)S(1)} %all_gather.36.refs_0_), channel_id=1, source_target_pairs={{0,224},{8,40},{16,240},{24,56},{32,0},{40,72},{48,16},{56,88},{64... | collective-permute-start | bytes 786440 | tf_op jit(solution)/shard_map/keys_values/ppermute | solution.py:44
  112.6 0.7 constant_dynamic-slice_fusion
  113.4 1.3 copy-done.1
  114.7 2.4 %q_project.1 = bf16[2,2,128,128]{3,2,1,0:T(8,128)(2,1)S(1)} custom-call(bf16[128,5120]{1,0:T(8,128)(2,1)S(1)} %copy-done, bf16[128,5120]{1,0:T(8,128)(2,1)S(1)} %collective-permute-done.h1, f32[1,128]{1,0:T(1,128)S(1)} %bitcast.21, f32[2,128,128]{2,1,0:T(8,128)S(1)} %get-tuple-element.36.cosine, f32[2,128,128]{2,1,0:T(8,128)S(1)} %get-tuple-element.37.sine, ...), custom_call_target="tpu_custom_call" | custom-call | tf_op jit(solution)/shard_map/queries/q_project/pallas_call | solution.py:152
  117.1 9.2 %all-gather.1 = bf16[8,2,128,128]{3,2,1,0:T(8,128)(2,1)S(1)} all-gather(bf16[2,2,128,128]{3,2,1,0:T(8,128)(2,1)S(1)} %q_project.1), channel_id=3, replica_groups=mesh['yh'=2,'zh'=4,'zl'=4,'c'=2,'x'=4,'yl'=2] {'yh','c'}, dimensions={0}, use_global_device_ids=true | all-gather | bytes 655360 | tf_op jit(solution)/shard_map/queries/all_gather | solution.py:349
  126.3 3.8 %attend_remote.1 = (f32[128,640]{1,0:T(8,128)S(1)}, f32[128,640]{1,0:T(8,128)S(1)}) custom-call(s32[2,64]{1,0:T(2,128)S(1)} %get-tuple-element.29.masks, bf16[2,2,2,2,128,128]{5,4,3,2,1,0:T(8,128)(2,1)S(1)} %bitcast.19, bf16[512,256]{1,0:T(8,128)(2,1)S(1)} %all_gather.36.refs_0_, bf16[512,256]{1,0:T(8,128)(2,1)S(1)} %collective-permute-done.3.refs_1_, ...), custom_call_target="tpu_custom_call" | custom-call | flops 1275068416 | bytes 1245184 | tf_op jit(solution)/shard_map/context/attend_remote/pallas_call | solution.py:247
  130.2 2.3 %all-gather.2 = f32[256,640]{1,0:T(8,128)S(1)} all-gather(f32[128,640]{1,0:T(8,128)S(1)} %get-tuple-element.26), channel_id=4, replica_groups=mesh['yh'=2,'zh'=4,'zl'=4,'c'=2,'x'=4,'yl'=2] {'c'}, dimensions={0}, use_global_device_ids=true | all-gather | bytes 983040 | tf_op jit(solution)/shard_map/context/all_gather | solution.py:358
  132.4 0.1 fold.1.refs_4_
  132.6 1.8 %collective-permute-start.6 = (bf16[128,640]{1,0:T(8,128)(2,1)S(1)}, bf16[128,640]{1,0:T(8,128)(2,1)S(1)}, u32[]{:S(2)}, u32[]{:S(2)}) collective-permute-start(bf16[128,640]{1,0:T(8,128)(2,1)S(1)} %fold.1.refs_4_), channel_id=1, source_target_pairs={{0,256},{1,257},{2,258},{3,259},{4,260},{5,261},{6,262},{7,263},{8... | collective-permute-start | bytes 491528 | tf_op jit(solution)/shard_map/context/ppermute | solution.py:360
  134.4 2.0 %attend_local.1 = (bf16[128,640]{1,0:T(8,128)(2,1)S(1)}, f32[128,640]{1,0:T(8,128)S(1)}) custom-call(s32[2,64]{1,0:T(2,128)S(1)} %get-tuple-element.30.masks, bf16[2,2,2,2,128,128]{5,4,3,2,1,0:T(8,128)(2,1)S(1)} %bitcast.20, bf16[512,256]{1,0:T(8,128)(2,1)S(1)} %all_gather.36.refs_0_, bf16[512,256]{1,0:T(8,128)(2,1)S(1)} %collective-permute-done.3.refs_1_, ...), custom_call_target="tpu_custom_call" | custom-call | flops 1275068416 | bytes 1245184 | tf_op jit(solution)/shard_map/context/attend_local/pallas_call | solution.py:247
  136.3 2.1 %all-gather.3 = bf16[256,640]{1,0:T(8,128)(2,1)S(1)} all-gather(bf16[128,640]{1,0:T(8,128)(2,1)S(1)} %get-tuple-element.28), channel_id=5, replica_groups=mesh['yh'=2,'zh'=4,'zl'=4,'c'=2,'x'=4,'yl'=2] {'c'}, dimensions={0}, use_global_device_ids=true | all-gather | bytes 491520 | tf_op jit(solution)/shard_map/context/all_gather | solution.py:362
  138.5 0.9 combine.1
  (21 shorter events, 0.1 us)
Async XLA Ops:
  7.2 16.6 %copy-start = (bf16[128,5120]{1,0:T(8,128)(2,1)S(1)}, bf16[128,5120]{1,0:T(8,128)(2,1)}, u32[]{:S(2)}) copy-start(bf16[128,5120]{1,0:T(8,128)(2,1)} %h0.3) | copy-start | bytes 3932164
  7.2 92.1 %all-gather.6.cloned.1.call-start = ((), (), s32[]{:S(2)}) async-start(), calls=%async_computation.1 | async-start | bytes 1392640 | tf_op jit(solution)/shard_map/weights/all_gather | solution.py:319
  7.2 1.0 copy-start.2
  23.7 48.7 %collective-permute-start = (bf16[128,5120]{1,0:T(8,128)(2,1)S(1)}, bf16[128,5120]{1,0:T(8,128)(2,1)S(1)}, u32[]{:S(2)}, u32[]{:S(2)}) collective-permute-start(bf16[128,5120]{1,0:T(8,128)(2,1)S(1)} %copy-done), channel_id=1, source_target_pairs={{0,256},{256,0},{1,257},{257,1},{2,258},{258,2},{3,259},{259,3},{4... | collective-permute-start | bytes 3932168 | tf_op jit(solution)/shard_map/weights/ppermute | solution.py:31
  62.0 10.5 %collective-permute-start.1 = (bf16[1280,256]{1,0:T(8,128)(2,1)S(1)}, bf16[1280,256]{1,0:T(8,128)(2,1)S(1)}, u32[]{:S(2)}, u32[]{:S(2)}) collective-permute-start(bf16[1280,256]{1,0:T(8,128)(2,1)S(1)} %all_gather.33.mine), channel_id=1, source_target_pairs={{0,8},{8,0},{1,9},{9,1},{2,10},{10,2},{3,11},{11,3},{4,12},{12,4},... | collective-permute-start | bytes 1966088 | tf_op jit(solution)/shard_map/keys_values/ppermute | solution.py:31
  72.3 7.8 %copy-start.4 = (f32[128]{0:T(128)S(1)}, f32[128]{0:T(128)}, u32[]{:S(2)}) copy-start(f32[128]{0:T(128)} %param.9) | copy-start | bytes 1540
  73.1 40.2 %copy-start.3 = (f32[128]{0:T(128)S(1)}, f32[128]{0:T(128)}, u32[]{:S(2)}) copy-start(f32[128]{0:T(128)} %param.8) | copy-start | bytes 1540
  99.3 14.1 %collective-permute-start.2 = (bf16[16,2,80,256]{3,2,1,0:T(8,128)(2,1)}, bf16[16,2,80,256]{3,2,1,0:T(8,128)(2,1)}, u32[]{:S(2)}, u32[]{:S(2)}) collective-permute-start(bf16[16,2,80,256]{3,2,1,0:T(8,128)(2,1)} %bitcast.15), channel_id=1, source_target_pairs={{0,8},{8,0},{1,9},{9,1},{2,10},{10,2},{3,11},{11,3},{4,12},{12,4},... | collective-permute-start | bytes 3932168 | tf_op jit(solution)/shard_map/keys_values/ppermute | solution.py:31
  104.7 21.7 %collective-permute-start.3 = (bf16[512,256]{1,0:T(8,128)(2,1)S(1)}, bf16[512,256]{1,0:T(8,128)(2,1)S(1)}, u32[]{:S(2)}, u32[]{:S(2)}) collective-permute-start(bf16[512,256]{1,0:T(8,128)(2,1)S(1)} %all_gather.36.refs_0_), channel_id=1, source_target_pairs={{0,240},{16,0},{32,16},{48,32},{64,48},{80,64},{96,80},{112,96},{1... | collective-permute-start | bytes 786440 | tf_op jit(solution)/shard_map/keys_values/ppermute | solution.py:35
  108.2 18.2 %collective-permute-start.4 = (bf16[512,256]{1,0:T(8,128)(2,1)S(1)}, bf16[512,256]{1,0:T(8,128)(2,1)S(1)}, u32[]{:S(2)}, u32[]{:S(2)}) collective-permute-start(bf16[512,256]{1,0:T(8,128)(2,1)S(1)} %all_gather.36.refs_0_), channel_id=1, source_target_pairs={{0,16},{16,32},{32,48},{48,64},{64,80},{80,96},{96,112},{112,128},... | collective-permute-start | bytes 786440 | tf_op jit(solution)/shard_map/keys_values/ppermute | solution.py:35
  110.1 16.2 %collective-permute-start.5 = (bf16[512,256]{1,0:T(8,128)(2,1)S(1)}, bf16[512,256]{1,0:T(8,128)(2,1)S(1)}, u32[]{:S(2)}, u32[]{:S(2)}) collective-permute-start(bf16[512,256]{1,0:T(8,128)(2,1)S(1)} %all_gather.36.refs_0_), channel_id=1, source_target_pairs={{0,224},{8,40},{16,240},{24,56},{32,0},{40,72},{48,16},{56,88},{64... | collective-permute-start | bytes 786440 | tf_op jit(solution)/shard_map/keys_values/ppermute | solution.py:44
  113.4 1.3 copy-start.1
  132.6 5.9 %collective-permute-start.6 = (bf16[128,640]{1,0:T(8,128)(2,1)S(1)}, bf16[128,640]{1,0:T(8,128)(2,1)S(1)}, u32[]{:S(2)}, u32[]{:S(2)}) collective-permute-start(bf16[128,640]{1,0:T(8,128)(2,1)S(1)} %fold.1.refs_4_), channel_id=1, source_target_pairs={{0,256},{1,257},{2,258},{3,259},{4,260},{5,261},{6,262},{7,263},{8... | collective-permute-start | bytes 491528 | tf_op jit(solution)/shard_map/context/ppermute | solution.py:360
Sparse Core Ops, SparseCore 0:
  23.8 66.5 all-gather.5

commit v5 on v4

--- a/solution.py
+++ b/solution.py
@@ -23,6 +23,9 @@
 f32 = jnp.float32
 
 
+ALTERNATE = [[z * CORE + (z + first) % CORE for z in range(NZ)] for first in range(CORE)]
+
+
 def params():
     return pltpu.CompilerParams(vmem_limit_bytes=24 * 1024 * 1024)
 
@@ -73,10 +76,14 @@
 
 def kv_partial_kernel(h0, h1, mine, other, keep, send, weight):
     core = lax.axis_index("c")
-    nz, _, share, wide = weight.shape
+    pairs, _, _, share, wide = weight.shape
+    nz = 2 * pairs
     half = nz * CORE * share
-    weight[:, core] = mine[...].reshape(nz, share, wide)
-    weight[:, 1 - core] = other[...].reshape(nz, share, wide)
+    even = lax.rem(core + lax.axis_index("zl"), 2)
+    for source, first in ((mine, even), (other, 1 - even)):
+        chunks = source[...].reshape(nz // 2, 2, share, wide)
+        weight[:, 0, first] = chunks[:, 0]
+        weight[:, 1, 1 - first] = chunks[:, 1]
     columns = pl.ds(pl.multiple_of(lax.axis_index("yh") * half, half), half)
     whole = weight[...].reshape(half, wide)
     for rows, out in ((h0, keep), (h1, send)):
@@ -89,7 +96,7 @@
     return pl.pallas_call(
         kv_partial_kernel,
         out_shape=(shape, shape),
-        scratch_shapes=[pltpu.VMEM((NZ, CORE, mine.shape[0] // NZ, mine.shape[1]), bf16)],
+        scratch_shapes=[pltpu.VMEM((NZ // 2, 2, CORE, mine.shape[0] // NZ, mine.shape[1]), bf16)],
         compiler_params=params(),
         name="kv_partial",
     )(*hiddens, mine, other)
@@ -119,21 +126,12 @@
     )(keep, sent, gain, cosine, sine)
 
 
-def q_project_kernel(h0, h1, gain, cosine, sine, mine, other, out, weight, sem):
-    yh, core = lax.axis_index("yh"), lax.axis_index("c")
+def q_project_kernel(h0, h1, gain, cosine, sine, weight, out):
+    yh = lax.axis_index("yh")
     half = h0.shape[1] // YH
-    copies = [
-        pltpu.make_async_copy(source.at[:, i], weight.at[i, :, owner], sem.at[i, flip])
-        for i in range(YH)
-        for flip, (source, owner) in enumerate(((mine, core), (other, 1 - core)))
-    ]
-    for copy in copies:
-        copy.start()
     totals = [None] * YH
     for i in range(YH):
-        for copy in copies[i * CORE : (i + 1) * CORE]:
-            copy.wait()
-        columns = weight[i].reshape(half, PAIR * HD)
+        columns = weight[:, :, i].reshape(half, PAIR * HD)
         for rel, rows in enumerate((h0, h1)):
             part = jnp.dot(
                 rows[:, i * half : (i + 1) * half], columns, preferred_element_type=f32
@@ -146,21 +144,14 @@
             ).astype(bf16)
 
 
-def q_project(hiddens, weights, gain, cosine, sine):
+def q_project(hiddens, weight, gain, cosine, sine):
     tok = hiddens[0].shape[0]
-    nz, halves, share, wide = weights[0].shape
     return pl.pallas_call(
         q_project_kernel,
-        in_specs=[pl.BlockSpec(memory_space=pltpu.VMEM)] * (YH + 3)
-        + [pl.BlockSpec(memory_space=pl.ANY)] * CORE,
         out_shape=jax.ShapeDtypeStruct((PAIR, YH, tok, HD), bf16),
-        scratch_shapes=[
-            pltpu.VMEM((halves, nz, CORE, share, wide), bf16),
-            pltpu.SemaphoreType.DMA((halves, CORE)),
-        ],
         compiler_params=params(),
         name="q_project",
-    )(*hiddens, gain, cosine, sine, *weights)
+    )(*hiddens, gain, cosine, sine, weight)
 
 
 OFFSETS = (0, 1, -1, 2)
@@ -185,7 +176,7 @@
             for j in range(ZH):
                 z_at = j * ZL + lax.rem(zl + (offset + ZL), ZL)
                 key_block = yh * (NZ * CORE) + z_at * CORE + core
-                live = (masks[query_core, key_block] == 1) & (key_block <= query_block)
+                live = (masks[query_yh * CORE + query_core, key_block] == 1) & (key_block <= query_block)
 
                 @pl.when(live)
                 def _(i=i, j=j, count=count, key_block=key_block, query_block=query_block):
@@ -316,9 +307,11 @@
         kv_rows = lax.dynamic_index_in_dim(
             got.reshape(YH, KV, share, 2 * wide), yh, 0, keepdims=False
         )[:, :, wide:].reshape(rows, wide)
-        q_weight = lax.all_gather(q_rows, Z, axis=0, tiled=False)
-        q_weight = q_weight.reshape(NZ, YH, rows, wide)
-        kv_weight = lax.all_gather(kv_rows, Z, axis=0, tiled=True)
+        q_weight = lax.all_gather(q_rows, Z + ("c",), axis=0, tiled=False)
+        q_weight = q_weight.reshape(NZ, CORE, YH, rows, wide)
+        kv_weight = lax.all_gather(
+            kv_rows, Z + ("c",), axis=0, tiled=True, axis_index_groups=ALTERNATE
+        )
 
     hiddens = (hidden, far)
 
@@ -340,25 +333,24 @@
         )
         line = lax.all_gather(both, "zh", axis=0, tiled=True)
         line, q_weight = lax.optimization_barrier((line, q_weight))
-        q_other = swap(q_weight, "c")
         across = from_z_both(line, 2)
         gathered = (line, from_z(line, 1), from_z(line, -1), across)
 
     with jax.named_scope("queries"):
-        query = q_project(hiddens, (q_weight, q_other), query_gain.reshape(1, HD), cosine, sine)
+        query = q_project(hiddens, q_weight, query_gain.reshape(1, HD), cosine, sine)
         query = lax.all_gather(query, ("yh", "c"), axis=0, tiled=False)
         query = query.reshape(YH, CORE, PAIR, YH, tok, HD)
 
-    def masks(query_yh):
-        first = (query_yh * NZ + zh * ZL + zl) * CORE
-        return lax.dynamic_slice_in_dim(block_mask, first, CORE, 0)
+    masks = block_mask.reshape(YH, NZ, CORE, block_mask.shape[1])
+    masks = lax.dynamic_index_in_dim(masks, zh * ZL + zl, 1, keepdims=False)
+    masks = masks.reshape(GROUP, block_mask.shape[1])
 
     with jax.named_scope("context"):
-        peer, own = attend(True, masks(1 - yh), query, gathered)
+        peer, own = attend(True, masks, query, gathered)
         both = lax.all_gather(peer, "c", axis=0, tiled=False)
         folded = fold(own, both)
         far_part = lax.ppermute(folded, "yh", [(0, 1)])
-        peer, own = attend(False, masks(yh), query, gathered, (folded,))
+        peer, own = attend(False, masks, query, gathered, (folded,))
         both = lax.all_gather(peer, "c", axis=0, tiled=False)
         context = combine(own, both, far_part)
     return keys, values, context

time: 147 us -> 144 us (0.980)
  starting transfers between devices: 27.1 us -> 15.5 us
  waiting for transfers between devices: 0.22 us -> 5.49 us
  blocking collectives: 88.7 us -> 93.9 us
  Pallas kernels: 10.7 us -> 8.91 us
    ppermute x3 -> x2, starting transfers between devices: 17.3 us -> 5.02 us  [swap(): return lax.ppermute(inputs, axis, [(0, 1), (1, 0)])]
    all_gather x1, blocking collectives: 35 us -> 40.1 us  [local(): lax.all_gather(kv_rows, Z + ('c',), axis=0, tiled=True, axis_index_groups...]
    all_gather x1, waiting for transfers between devices: 0.01 us -> 4.91 us  [local(): q_weight = lax.all_gather(q_rows, Z + ('c',), axis=0, tiled=False)]
    all_gather x1, blocking collectives: 18.4 us -> 16.3 us  [local(): line = lax.all_gather(both, 'zh', axis=0, tiled=True)]
    all_gather x1, blocking collectives: 9.19 us -> 11.3 us  [local(): query = lax.all_gather(query, ('yh', 'c'), axis=0, tiled=False)]
  transfers between devices with their start and end apart: 8 -> 7, of which waited for: 1 -> 2; matrix products, arithmetic and copies ran while one was open for 2% -> 1% of each run, Pallas kernels for 4% -> 3%
where the time goes in v5:
time: 144 us; the launch traced here: 143 us
  blocking collectives  93.9 us (65%)
  starting transfers between devices  15.5 us (11%)
  between operations  14.3 us (10%)
  Pallas kernels  8.91 us (6%)
  waiting for transfers between devices  5.49 us (4%)
  local copies, waits for them, and re-layouts  4.3 us (3%)
    all_gather x1, blocking collectives, local(): lax.all_gather(kv_rows, Z + ('c',), axis=0, tiled=True, axis_index_groups...  40.1 us
    all_gather x1, blocking collectives, local(): line = lax.all_gather(both, 'zh', axis=0, tiled=True)  16.3 us
    all_to_all x1, blocking collectives, local(): got = lax.all_to_all(pack(qkv_weight), ('yh', 'x', 'yl'), 0, 0)  14.8 us
    all_gather x1, blocking collectives, local(): query = lax.all_gather(query, ('yh', 'c'), axis=0, tiled=False)  11.3 us
    all_gather x1, blocking collectives, local(): sent = lax.all_gather(send, 'yh', axis=0, tiled=False)  7.14 us
    ppermute x2, starting transfers between devices, from_z(): return lax.ppermute(inputs, Z, [(i, (i - offset) % NZ) for i in range(NZ)])  6.07 us
    pallas_call x2, Pallas kernels, attend(): pl.pallas_call(functools.partial(attend_kernel, remote), in_specs=[pl.Blo...  5.35 us
    ppermute x2, starting transfers between devices, swap(): return lax.ppermute(inputs, axis, [(0, 1), (1, 0)])  5.02 us
  transfers between devices with their start and end apart: 7, of which 2 were waited for; matrix products, arithmetic and copies ran while one was open for 1% of the time, Pallas kernels for 3%

profile of v5, /device:TPU:1, one launch (start us, length us, event | category | flops | bytes accessed | tf_op | source)
XLA Modules:
  0.0 143.1 jit_solution(11303318154510886082)
XLA Ops:
  7.2 0.0 copy-start
  7.2 0.0 all-gather.6.cloned.1.call-start
  7.2 1.0 copy-done.3
  8.3 14.8 %all_to_all.5 = bf16[16,10,512]{2,1,0:T(8,128)(2,1)S(1)} all-to-all(bf16[16,10,512]{2,1,0:T(8,128)(2,1)S(1)} %pack.1), channel_id=1, replica_groups=mesh['yh'=2,'zh'=4,'zl'=4,'c'=2,'x'=4,'yl'=2] {'yh','x','yl'}, dimensions={0} | all-to-all | bytes 327680 | tf_op jit(solution)/shard_map/weights/all_to_all | solution.py:302
  23.0 0.7 reshape.64
  23.7 0.0 all-gather.6.cloned.1.call-update
  23.8 3.1 %collective-permute-start = (bf16[128,5120]{1,0:T(8,128)(2,1)S(1)}, bf16[128,5120]{1,0:T(8,128)(2,1)S(1)}, u32[]{:S(2)}, u32[]{:S(2)}) collective-permute-start(bf16[128,5120]{1,0:T(8,128)(2,1)S(1)} %copy-done.1), channel_id=1, source_target_pairs={{0,256},{256,0},{1,257},{257,1},{2,258},{258,2},{3,259},{259,3},{4... | collective-permute-start | bytes 3932168 | tf_op jit(solution)/shard_map/weights/ppermute | solution.py:34
  27.0 40.1 %all_gather.33.mine = bf16[1280,256]{1,0:T(8,128)(2,1)S(1)} all-gather(bf16[80,256]{1,0:T(8,128)(2,1)S(1)} %reshape.59), channel_id=1, replica_groups={{0,24,32,56,64,88,96,120,128,152,160,184,192,216,224,248},{8,16,40,48,7..., dimensions={0}, use_global_device_ids=true | all-gather | bytes 696320 | tf_op jit(solution)/shard_map/weights/all_gather | solution.py:312
  67.1 1.9 %collective-permute-start.1 = (bf16[1280,256]{1,0:T(8,128)(2,1)S(1)}, bf16[1280,256]{1,0:T(8,128)(2,1)S(1)}, u32[]{:S(2)}, u32[]{:S(2)}) collective-permute-start(bf16[1280,256]{1,0:T(8,128)(2,1)S(1)} %all_gather.33.mine), channel_id=1, source_target_pairs={{0,8},{8,0},{1,9},{9,1},{2,10},{10,2},{3,11},{11,3},{4,12},{12,4},... | collective-permute-start | bytes 1966088 | tf_op jit(solution)/shard_map/keys_values/ppermute | solution.py:34
  69.0 0.8 dynamic-slice_bitcast_fusion.2
  69.8 0.5 fusion
  70.4 0.1 pad_maximum_fusion
  70.5 0.0 copy-start.5
  70.5 0.6 collective-permute-done.1.other
  71.1 0.7 kv_partial.1
  71.8 7.1 %all-gather = f32[256,256]{1,0:T(8,128)S(1)} all-gather(f32[128,256]{1,0:T(8,128)S(1)} %get-tuple-element.19), channel_id=2, replica_groups=mesh['yh'=2,'zh'=4,'zl'=4,'c'=2,'x'=4,'yl'=2] {'yh'}, dimensions={0}, use_global_device_ids=true | all-gather | bytes 393216 | tf_op jit(solution)/shard_map/keys_values/all_gather | solution.py:330
  78.9 0.8 kv_finish.1
  79.7 16.3 %all_gather.36.refs_0_ = bf16[512,256]{1,0:T(8,128)(2,1)S(1)} all-gather(bf16[128,256]{1,0:T(8,128)(2,1)S(1)} %get-tuple-element.22), channel_id=1, replica_groups=mesh['yh'=2,'zh'=4,'zl'=4,'c'=2,'x'=4,'yl'=2] {'zh'}, dimensions={0}, use_global_device_ids=true | all-gather | bytes 327680 | tf_op jit(solution)/shard_map/keys_values/all_gather | solution.py:334
  96.0 4.9 %all-gather.6.cloned.1.call-done = bf16[32,160,256]{2,1,0:T(8,128)(2,1)} async-done(((bf16[1,160,256]{2,1,0:T(8,128)(2,1)}), bf16[32,160,256]{2,1,0:T(8,128)(2,1)}) %all-gather.6.cloned.1.call-update) | async-done | bytes 2621456 | tf_op jit(solution)/shard_map/weights/all_gather | solution.py:310
  100.9 4.2 %collective-permute-start.2 = (bf16[512,256]{1,0:T(8,128)(2,1)S(1)}, bf16[512,256]{1,0:T(8,128)(2,1)S(1)}, u32[]{:S(2)}, u32[]{:S(2)}) collective-permute-start(bf16[512,256]{1,0:T(8,128)(2,1)S(1)} %all_gather.36.refs_0_), channel_id=1, source_target_pairs={{0,240},{16,0},{32,16},{48,32},{64,48},{80,64},{96,80},{112,96},{1... | collective-permute-start | bytes 786440 | tf_op jit(solution)/shard_map/keys_values/ppermute | solution.py:38
  105.1 1.9 %collective-permute-start.3 = (bf16[512,256]{1,0:T(8,128)(2,1)S(1)}, bf16[512,256]{1,0:T(8,128)(2,1)S(1)}, u32[]{:S(2)}, u32[]{:S(2)}) collective-permute-start(bf16[512,256]{1,0:T(8,128)(2,1)S(1)} %all_gather.36.refs_0_), channel_id=1, source_target_pairs={{0,16},{16,32},{32,48},{48,64},{64,80},{80,96},{96,112},{112,128},... | collective-permute-start | bytes 786440 | tf_op jit(solution)/shard_map/keys_values/ppermute | solution.py:38
  107.0 2.3 %collective-permute-start.4 = (bf16[512,256]{1,0:T(8,128)(2,1)S(1)}, bf16[512,256]{1,0:T(8,128)(2,1)S(1)}, u32[]{:S(2)}, u32[]{:S(2)}) collective-permute-start(bf16[512,256]{1,0:T(8,128)(2,1)S(1)} %all_gather.36.refs_0_), channel_id=1, source_target_pairs={{0,224},{8,40},{16,240},{24,56},{32,0},{40,72},{48,16},{56,88},{64... | collective-permute-start | bytes 786440 | tf_op jit(solution)/shard_map/keys_values/ppermute | solution.py:47
  109.4 1.7 %copy-done.2 = bf16[32,160,256]{2,1,0:T(8,128)(2,1)S(1)} copy-done((bf16[32,160,256]{2,1,0:T(8,128)(2,1)S(1)}, bf16[32,160,256]{2,1,0:T(8,128)(2,1)}, u32[]{:S(2)}) %copy-start.2) | copy-done | bytes 2621464
  111.1 1.1 q_project.1
  112.2 11.3 %all-gather.1 = bf16[8,2,128,128]{3,2,1,0:T(8,128)(2,1)S(1)} all-gather(bf16[2,2,128,128]{3,2,1,0:T(8,128)(2,1)S(1)} %q_project.1), channel_id=3, replica_groups=mesh['yh'=2,'zh'=4,'zl'=4,'c'=2,'x'=4,'yl'=2] {'yh','c'}, dimensions={0}, use_global_device_ids=true | all-gather | bytes 655360 | tf_op jit(solution)/shard_map/queries/all_gather | solution.py:341
  123.5 3.4 %attend_remote.1 = (f32[128,640]{1,0:T(8,128)S(1)}, f32[128,640]{1,0:T(8,128)S(1)}) custom-call(s32[4,64]{1,0:T(4,128)S(1)} %bitcast.25, bf16[2,2,2,2,128,128]{5,4,3,2,1,0:T(8,128)(2,1)S(1)} %bitcast.23, bf16[512,256]{1,0:T(8,128)(2,1)S(1)} %all_gather.36.refs_0_, bf16[512,256]{1,0:T(8,128)(2,1)S(1)} %collective-permute-done.2.refs_1_, ...), custom_call_target="tpu_custom_call" | custom-call | flops 1275068416 | bytes 1245184 | tf_op jit(solution)/shard_map/context/attend_remote/pallas_call | solution.py:238
  126.9 2.3 %all-gather.2 = f32[256,640]{1,0:T(8,128)S(1)} all-gather(f32[128,640]{1,0:T(8,128)S(1)} %get-tuple-element.26), channel_id=4, replica_groups=mesh['yh'=2,'zh'=4,'zl'=4,'c'=2,'x'=4,'yl'=2] {'c'}, dimensions={0}, use_global_device_ids=true | all-gather | bytes 983040 | tf_op jit(solution)/shard_map/context/all_gather | solution.py:350
  129.1 0.1 fold.1.refs_4_
  129.2 2.0 %collective-permute-start.5 = (bf16[128,640]{1,0:T(8,128)(2,1)S(1)}, bf16[128,640]{1,0:T(8,128)(2,1)S(1)}, u32[]{:S(2)}, u32[]{:S(2)}) collective-permute-start(bf16[128,640]{1,0:T(8,128)(2,1)S(1)} %fold.1.refs_4_), channel_id=1, source_target_pairs={{0,256},{1,257},{2,258},{3,259},{4,260},{5,261},{6,262},{7,263},{8... | collective-permute-start | bytes 491528 | tf_op jit(solution)/shard_map/context/ppermute | solution.py:352
  131.3 2.0 %attend_local.1 = (bf16[128,640]{1,0:T(8,128)(2,1)S(1)}, f32[128,640]{1,0:T(8,128)S(1)}) custom-call(s32[4,64]{1,0:T(4,128)S(1)} %bitcast.26, bf16[2,2,2,2,128,128]{5,4,3,2,1,0:T(8,128)(2,1)S(1)} %bitcast.24, bf16[512,256]{1,0:T(8,128)(2,1)S(1)} %all_gather.36.refs_0_, bf16[512,256]{1,0:T(8,128)(2,1)S(1)} %collective-permute-done.2.refs_1_, ...), custom_call_target="tpu_custom_call" | custom-call | flops 1275068416 | bytes 1245184 | tf_op jit(solution)/shard_map/context/attend_local/pallas_call | solution.py:238
  133.2 2.1 %all-gather.3 = bf16[256,640]{1,0:T(8,128)(2,1)S(1)} all-gather(bf16[128,640]{1,0:T(8,128)(2,1)S(1)} %get-tuple-element.28), channel_id=5, replica_groups=mesh['yh'=2,'zh'=4,'zl'=4,'c'=2,'x'=4,'yl'=2] {'c'}, dimensions={0}, use_global_device_ids=true | all-gather | bytes 491520 | tf_op jit(solution)/shard_map/context/all_gather | solution.py:354
  135.4 0.9 combine.1
  (21 shorter events, 0.1 us)
Async XLA Ops:
  7.2 102.2 %copy-start = (s32[64,64]{1,0:T(8,128)S(1)}, s32[64,64]{1,0:T(8,128)}, u32[]{:S(2)}) copy-start(s32[64,64]{1,0:T(8,128)} %param.11) | copy-start | bytes 49156
  7.2 16.6 %copy-start.1 = (bf16[128,5120]{1,0:T(8,128)(2,1)S(1)}, bf16[128,5120]{1,0:T(8,128)(2,1)}, u32[]{:S(2)}) copy-start(bf16[128,5120]{1,0:T(8,128)(2,1)} %h0.3) | copy-start | bytes 3932164
  7.2 93.7 %all-gather.6.cloned.1.call-start = ((), (), s32[]{:S(2)}) async-start(), calls=%async_computation.1 | async-start | bytes 2703360 | tf_op jit(solution)/shard_map/weights/all_gather | solution.py:310
  7.2 1.0 copy-start.3
  23.8 47.3 %collective-permute-start = (bf16[128,5120]{1,0:T(8,128)(2,1)S(1)}, bf16[128,5120]{1,0:T(8,128)(2,1)S(1)}, u32[]{:S(2)}, u32[]{:S(2)}) collective-permute-start(bf16[128,5120]{1,0:T(8,128)(2,1)S(1)} %copy-done.1), channel_id=1, source_target_pairs={{0,256},{256,0},{1,257},{257,1},{2,258},{258,2},{3,259},{259,3},{4... | collective-permute-start | bytes 3932168 | tf_op jit(solution)/shard_map/weights/ppermute | solution.py:34
  67.1 4.0 %collective-permute-start.1 = (bf16[1280,256]{1,0:T(8,128)(2,1)S(1)}, bf16[1280,256]{1,0:T(8,128)(2,1)S(1)}, u32[]{:S(2)}, u32[]{:S(2)}) collective-permute-start(bf16[1280,256]{1,0:T(8,128)(2,1)S(1)} %all_gather.33.mine), channel_id=1, source_target_pairs={{0,8},{8,0},{1,9},{9,1},{2,10},{10,2},{3,11},{11,3},{4,12},{12,4},... | collective-permute-start | bytes 1966088 | tf_op jit(solution)/shard_map/keys_values/ppermute | solution.py:34
  70.5 8.4 %copy-start.5 = (f32[128]{0:T(128)S(1)}, f32[128]{0:T(128)}, u32[]{:S(2)}) copy-start(f32[128]{0:T(128)} %param.9) | copy-start | bytes 1540
  71.8 37.6 %copy-start.4 = (f32[128]{0:T(128)S(1)}, f32[128]{0:T(128)}, u32[]{:S(2)}) copy-start(f32[128]{0:T(128)} %param.8) | copy-start | bytes 1540
  100.9 22.6 %collective-permute-start.2 = (bf16[512,256]{1,0:T(8,128)(2,1)S(1)}, bf16[512,256]{1,0:T(8,128)(2,1)S(1)}, u32[]{:S(2)}, u32[]{:S(2)}) collective-permute-start(bf16[512,256]{1,0:T(8,128)(2,1)S(1)} %all_gather.36.refs_0_), channel_id=1, source_target_pairs={{0,240},{16,0},{32,16},{48,32},{64,48},{80,64},{96,80},{112,96},{1... | collective-permute-start | bytes 786440 | tf_op jit(solution)/shard_map/keys_values/ppermute | solution.py:38
  105.1 18.4 %collective-permute-start.3 = (bf16[512,256]{1,0:T(8,128)(2,1)S(1)}, bf16[512,256]{1,0:T(8,128)(2,1)S(1)}, u32[]{:S(2)}, u32[]{:S(2)}) collective-permute-start(bf16[512,256]{1,0:T(8,128)(2,1)S(1)} %all_gather.36.refs_0_), channel_id=1, source_target_pairs={{0,16},{16,32},{32,48},{48,64},{64,80},{80,96},{96,112},{112,128},... | collective-permute-start | bytes 786440 | tf_op jit(solution)/shard_map/keys_values/ppermute | solution.py:38
  107.0 16.5 %collective-permute-start.4 = (bf16[512,256]{1,0:T(8,128)(2,1)S(1)}, bf16[512,256]{1,0:T(8,128)(2,1)S(1)}, u32[]{:S(2)}, u32[]{:S(2)}) collective-permute-start(bf16[512,256]{1,0:T(8,128)(2,1)S(1)} %all_gather.36.refs_0_), channel_id=1, source_target_pairs={{0,224},{8,40},{16,240},{24,56},{32,0},{40,72},{48,16},{56,88},{64... | collective-permute-start | bytes 786440 | tf_op jit(solution)/shard_map/keys_values/ppermute | solution.py:47
  109.4 1.7 %copy-start.2 = (bf16[32,160,256]{2,1,0:T(8,128)(2,1)S(1)}, bf16[32,160,256]{2,1,0:T(8,128)(2,1)}, u32[]{:S(2)}) copy-start(bf16[32,160,256]{2,1,0:T(8,128)(2,1)} %all-gather.6.cloned.1.call-done) | copy-start | bytes 7864324
  129.2 6.1 %collective-permute-start.5 = (bf16[128,640]{1,0:T(8,128)(2,1)S(1)}, bf16[128,640]{1,0:T(8,128)(2,1)S(1)}, u32[]{:S(2)}, u32[]{:S(2)}) collective-permute-start(bf16[128,640]{1,0:T(8,128)(2,1)S(1)} %fold.1.refs_4_), channel_id=1, source_target_pairs={{0,256},{1,257},{2,258},{3,259},{4,260},{5,261},{6,262},{7,263},{8... | collective-permute-start | bytes 491528 | tf_op jit(solution)/shard_map/context/ppermute | solution.py:352
Sparse Core Ops, SparseCore 0:
  23.9 77.0 all-gather.5

commit v6 on v5

--- a/solution.py
+++ b/solution.py
@@ -87,15 +87,16 @@
     columns = pl.ds(pl.multiple_of(lax.axis_index("yh") * half, half), half)
     whole = weight[...].reshape(half, wide)
     for rows, out in ((h0, keep), (h1, send)):
-        out[...] = jnp.dot(rows[:, columns], whole, preferred_element_type=f32)
+        total = jnp.dot(rows[:, columns], whole, preferred_element_type=f32)
+        out[...] = total.astype(out.dtype)
 
 
 def kv_partial(hiddens, mine, other):
     tok = hiddens[0].shape[0]
-    shape = jax.ShapeDtypeStruct((tok, 2 * HD), f32)
+    shape = (tok, 2 * HD)
     return pl.pallas_call(
         kv_partial_kernel,
-        out_shape=(shape, shape),
+        out_shape=(jax.ShapeDtypeStruct(shape, f32), jax.ShapeDtypeStruct(shape, bf16)),
         scratch_shapes=[pltpu.VMEM((NZ // 2, 2, CORE, mine.shape[0] // NZ, mine.shape[1]), bf16)],
         compiler_params=params(),
         name="kv_partial",
@@ -103,7 +104,7 @@
 
 
 def kv_finish_kernel(keep, sent, gain, cosine, sine, keys, values, both):
-    total = keep[...] + sent[1 - lax.axis_index("yh")]
+    total = keep[...] + sent[1 - lax.axis_index("yh")].astype(f32)
     key = norm_rope(total[:, :HD], gain[...], cosine[0], sine[0]).astype(bf16)
     value = total[:, HD:].astype(bf16)
     keys[...] = key

time: 144 us -> 144 us (level)
  blocking collectives: 93.9 us -> 91.4 us
where the time goes in v6:
time: 144 us; the launch traced here: 143 us
  blocking collectives  91.4 us (63%)
  starting transfers between devices  15.9 us (11%)
  between operations  14.3 us (10%)
  Pallas kernels  9.4 us (7%)
  waiting for transfers between devices  6.75 us (5%)
  local copies, waits for them, and re-layouts  4.3 us (3%)
    all_gather x1, blocking collectives, local(): lax.all_gather(kv_rows, Z + ('c',), axis=0, tiled=True, axis_index_groups...  40.1 us
    all_gather x1, blocking collectives, local(): line = lax.all_gather(both, 'zh', axis=0, tiled=True)  16.4 us
    all_to_all x1, blocking collectives, local(): got = lax.all_to_all(pack(qkv_weight), ('yh', 'x', 'yl'), 0, 0)  14.8 us
    all_gather x1, blocking collectives, local(): query = lax.all_gather(query, ('yh', 'c'), axis=0, tiled=False)  9.98 us
    ppermute x2, starting transfers between devices, from_z(): return lax.ppermute(inputs, Z, [(i, (i - offset) % NZ) for i in range(NZ)])  6.4 us
    all_gather x1, waiting for transfers between devices, local(): q_weight = lax.all_gather(q_rows, Z + ('c',), axis=0, tiled=False)  6.18 us
    pallas_call x2, Pallas kernels, attend(): pl.pallas_call(functools.partial(attend_kernel, remote), in_specs=[pl.Blo...  5.84 us
    all_gather x1, blocking collectives, local(): sent = lax.all_gather(send, 'yh', axis=0, tiled=False)  5.73 us
  transfers between devices with their start and end apart: 7, of which 2 were waited for; matrix products, arithmetic and copies ran while one was open for 1% of the time, Pallas kernels for 3%

profile of v6, /device:TPU:1, one launch (start us, length us, event | category | flops | bytes accessed | tf_op | source)
XLA Modules:
  0.0 142.7 jit_solution(8850241259148364385)
XLA Ops:
  7.2 0.0 copy-start
  7.2 0.0 all-gather.6.cloned.1.call-start
  7.2 1.0 copy-done.3
  8.3 14.8 %all_to_all.5 = bf16[16,10,512]{2,1,0:T(8,128)(2,1)S(1)} all-to-all(bf16[16,10,512]{2,1,0:T(8,128)(2,1)S(1)} %pack.1), channel_id=1, replica_groups=mesh['yh'=2,'zh'=4,'zl'=4,'c'=2,'x'=4,'yl'=2] {'yh','x','yl'}, dimensions={0} | all-to-all | bytes 327680 | tf_op jit(solution)/shard_map/weights/all_to_all | solution.py:303
  23.0 0.7 reshape.64
  23.7 0.0 all-gather.6.cloned.1.call-update
  23.8 3.1 %collective-permute-start = (bf16[128,5120]{1,0:T(8,128)(2,1)S(1)}, bf16[128,5120]{1,0:T(8,128)(2,1)S(1)}, u32[]{:S(2)}, u32[]{:S(2)}) collective-permute-start(bf16[128,5120]{1,0:T(8,128)(2,1)S(1)} %copy-done.1), channel_id=1, source_target_pairs={{0,256},{256,0},{1,257},{257,1},{2,258},{258,2},{3,259},{259,3},{4... | collective-permute-start | bytes 3932168 | tf_op jit(solution)/shard_map/weights/ppermute | solution.py:34
  27.0 40.1 %all_gather.33.mine = bf16[1280,256]{1,0:T(8,128)(2,1)S(1)} all-gather(bf16[80,256]{1,0:T(8,128)(2,1)S(1)} %reshape.59), channel_id=1, replica_groups={{0,24,32,56,64,88,96,120,128,152,160,184,192,216,224,248},{8,16,40,48,7..., dimensions={0}, use_global_device_ids=true | all-gather | bytes 696320 | tf_op jit(solution)/shard_map/weights/all_gather | solution.py:313
  67.1 1.9 %collective-permute-start.1 = (bf16[1280,256]{1,0:T(8,128)(2,1)S(1)}, bf16[1280,256]{1,0:T(8,128)(2,1)S(1)}, u32[]{:S(2)}, u32[]{:S(2)}) collective-permute-start(bf16[1280,256]{1,0:T(8,128)(2,1)S(1)} %all_gather.33.mine), channel_id=1, source_target_pairs={{0,8},{8,0},{1,9},{9,1},{2,10},{10,2},{3,11},{11,3},{4,12},{12,4},... | collective-permute-start | bytes 1966088 | tf_op jit(solution)/shard_map/keys_values/ppermute | solution.py:34
  69.0 0.8 dynamic-slice_bitcast_fusion.2
  69.8 0.5 fusion
  70.4 0.1 pad_maximum_fusion
  70.5 0.0 copy-start.4
  70.5 0.5 collective-permute-done.1.other
  71.1 0.7 kv_partial.1
  71.8 5.7 %all-gather = bf16[256,256]{1,0:T(8,128)(2,1)S(1)} all-gather(bf16[128,256]{1,0:T(8,128)(2,1)S(1)} %get-tuple-element.19), channel_id=2, replica_groups=mesh['yh'=2,'zh'=4,'zl'=4,'c'=2,'x'=4,'yl'=2] {'yh'}, dimensions={0}, use_global_device_ids=true | all-gather | bytes 196608 | tf_op jit(solution)/shard_map/keys_values/all_gather | solution.py:331
  77.5 0.8 kv_finish.1
  78.3 16.4 %all_gather.36.refs_0_ = bf16[512,256]{1,0:T(8,128)(2,1)S(1)} all-gather(bf16[128,256]{1,0:T(8,128)(2,1)S(1)} %get-tuple-element.22), channel_id=1, replica_groups=mesh['yh'=2,'zh'=4,'zl'=4,'c'=2,'x'=4,'yl'=2] {'zh'}, dimensions={0}, use_global_device_ids=true | all-gather | bytes 327680 | tf_op jit(solution)/shard_map/keys_values/all_gather | solution.py:335
  94.8 6.2 %all-gather.6.cloned.1.call-done = bf16[32,160,256]{2,1,0:T(8,128)(2,1)} async-done(((bf16[1,160,256]{2,1,0:T(8,128)(2,1)}), bf16[32,160,256]{2,1,0:T(8,128)(2,1)}) %all-gather.6.cloned.1.call-update) | async-done | bytes 2621456 | tf_op jit(solution)/shard_map/weights/all_gather | solution.py:311
  100.9 4.5 %collective-permute-start.2 = (bf16[512,256]{1,0:T(8,128)(2,1)S(1)}, bf16[512,256]{1,0:T(8,128)(2,1)S(1)}, u32[]{:S(2)}, u32[]{:S(2)}) collective-permute-start(bf16[512,256]{1,0:T(8,128)(2,1)S(1)} %all_gather.36.refs_0_), channel_id=1, source_target_pairs={{0,240},{16,0},{32,16},{48,32},{64,48},{80,64},{96,80},{112,96},{1... | collective-permute-start | bytes 786440 | tf_op jit(solution)/shard_map/keys_values/ppermute | solution.py:38
  105.4 1.9 %collective-permute-start.3 = (bf16[512,256]{1,0:T(8,128)(2,1)S(1)}, bf16[512,256]{1,0:T(8,128)(2,1)S(1)}, u32[]{:S(2)}, u32[]{:S(2)}) collective-permute-start(bf16[512,256]{1,0:T(8,128)(2,1)S(1)} %all_gather.36.refs_0_), channel_id=1, source_target_pairs={{0,16},{16,32},{32,48},{48,64},{64,80},{80,96},{96,112},{112,128},... | collective-permute-start | bytes 786440 | tf_op jit(solution)/shard_map/keys_values/ppermute | solution.py:38
  107.4 2.9 %collective-permute-start.4 = (bf16[512,256]{1,0:T(8,128)(2,1)S(1)}, bf16[512,256]{1,0:T(8,128)(2,1)S(1)}, u32[]{:S(2)}, u32[]{:S(2)}) collective-permute-start(bf16[512,256]{1,0:T(8,128)(2,1)S(1)} %all_gather.36.refs_0_), channel_id=1, source_target_pairs={{0,224},{8,40},{16,240},{24,56},{32,0},{40,72},{48,16},{56,88},{64... | collective-permute-start | bytes 786440 | tf_op jit(solution)/shard_map/keys_values/ppermute | solution.py:47
  110.3 1.7 %copy-done.2 = bf16[32,160,256]{2,1,0:T(8,128)(2,1)S(1)} copy-done((bf16[32,160,256]{2,1,0:T(8,128)(2,1)S(1)}, bf16[32,160,256]{2,1,0:T(8,128)(2,1)}, u32[]{:S(2)}) %copy-start.2) | copy-done | bytes 2621464
  112.0 1.1 q_project.1
  113.1 10.0 %all-gather.1 = bf16[8,2,128,128]{3,2,1,0:T(8,128)(2,1)S(1)} all-gather(bf16[2,2,128,128]{3,2,1,0:T(8,128)(2,1)S(1)} %q_project.1), channel_id=3, replica_groups=mesh['yh'=2,'zh'=4,'zl'=4,'c'=2,'x'=4,'yl'=2] {'yh','c'}, dimensions={0}, use_global_device_ids=true | all-gather | bytes 655360 | tf_op jit(solution)/shard_map/queries/all_gather | solution.py:342
  123.1 3.9 %attend_remote.1 = (f32[128,640]{1,0:T(8,128)S(1)}, f32[128,640]{1,0:T(8,128)S(1)}) custom-call(s32[4,64]{1,0:T(4,128)S(1)} %bitcast.25, bf16[2,2,2,2,128,128]{5,4,3,2,1,0:T(8,128)(2,1)S(1)} %bitcast.22, bf16[512,256]{1,0:T(8,128)(2,1)S(1)} %all_gather.36.refs_0_, bf16[512,256]{1,0:T(8,128)(2,1)S(1)} %collective-permute-done.2.refs_1_, ...), custom_call_target="tpu_custom_call" | custom-call | flops 1275068416 | bytes 1245184 | tf_op jit(solution)/shard_map/context/attend_remote/pallas_call | solution.py:239
  127.0 2.3 %all-gather.2 = f32[256,640]{1,0:T(8,128)S(1)} all-gather(f32[128,640]{1,0:T(8,128)S(1)} %get-tuple-element.26), channel_id=4, replica_groups=mesh['yh'=2,'zh'=4,'zl'=4,'c'=2,'x'=4,'yl'=2] {'c'}, dimensions={0}, use_global_device_ids=true | all-gather | bytes 983040 | tf_op jit(solution)/shard_map/context/all_gather | solution.py:351
  129.3 0.1 fold.1.refs_4_
  129.4 1.5 %collective-permute-start.5 = (bf16[128,640]{1,0:T(8,128)(2,1)S(1)}, bf16[128,640]{1,0:T(8,128)(2,1)S(1)}, u32[]{:S(2)}, u32[]{:S(2)}) collective-permute-start(bf16[128,640]{1,0:T(8,128)(2,1)S(1)} %fold.1.refs_4_), channel_id=1, source_target_pairs={{0,256},{1,257},{2,258},{3,259},{4,260},{5,261},{6,262},{7,263},{8... | collective-permute-start | bytes 491528 | tf_op jit(solution)/shard_map/context/ppermute | solution.py:353
  130.9 2.0 %attend_local.1 = (bf16[128,640]{1,0:T(8,128)(2,1)S(1)}, f32[128,640]{1,0:T(8,128)S(1)}) custom-call(s32[4,64]{1,0:T(4,128)S(1)} %bitcast.26, bf16[2,2,2,2,128,128]{5,4,3,2,1,0:T(8,128)(2,1)S(1)} %bitcast.23, bf16[512,256]{1,0:T(8,128)(2,1)S(1)} %all_gather.36.refs_0_, bf16[512,256]{1,0:T(8,128)(2,1)S(1)} %collective-permute-done.2.refs_1_, ...), custom_call_target="tpu_custom_call" | custom-call | flops 1275068416 | bytes 1245184 | tf_op jit(solution)/shard_map/context/attend_local/pallas_call | solution.py:239
  132.9 2.1 %all-gather.3 = bf16[256,640]{1,0:T(8,128)(2,1)S(1)} all-gather(bf16[128,640]{1,0:T(8,128)(2,1)S(1)} %get-tuple-element.28), channel_id=5, replica_groups=mesh['yh'=2,'zh'=4,'zl'=4,'c'=2,'x'=4,'yl'=2] {'c'}, dimensions={0}, use_global_device_ids=true | all-gather | bytes 491520 | tf_op jit(solution)/shard_map/context/all_gather | solution.py:355
  135.0 0.9 combine.1
  (21 shorter events, 0.1 us)
Async XLA Ops:
  7.2 103.1 %copy-start = (s32[64,64]{1,0:T(8,128)S(1)}, s32[64,64]{1,0:T(8,128)}, u32[]{:S(2)}) copy-start(s32[64,64]{1,0:T(8,128)} %param.11) | copy-start | bytes 49156
  7.2 16.6 %copy-start.1 = (bf16[128,5120]{1,0:T(8,128)(2,1)S(1)}, bf16[128,5120]{1,0:T(8,128)(2,1)}, u32[]{:S(2)}) copy-start(bf16[128,5120]{1,0:T(8,128)(2,1)} %h0.3) | copy-start | bytes 3932164
  7.2 93.8 %all-gather.6.cloned.1.call-start = ((), (), s32[]{:S(2)}) async-start(), calls=%async_computation.1 | async-start | bytes 2703360 | tf_op jit(solution)/shard_map/weights/all_gather | solution.py:311
  7.2 1.0 copy-start.3
  23.8 47.3 %collective-permute-start = (bf16[128,5120]{1,0:T(8,128)(2,1)S(1)}, bf16[128,5120]{1,0:T(8,128)(2,1)S(1)}, u32[]{:S(2)}, u32[]{:S(2)}) collective-permute-start(bf16[128,5120]{1,0:T(8,128)(2,1)S(1)} %copy-done.1), channel_id=1, source_target_pairs={{0,256},{256,0},{1,257},{257,1},{2,258},{258,2},{3,259},{259,3},{4... | collective-permute-start | bytes 3932168 | tf_op jit(solution)/shard_map/weights/ppermute | solution.py:34
  67.1 4.0 %collective-permute-start.1 = (bf16[1280,256]{1,0:T(8,128)(2,1)S(1)}, bf16[1280,256]{1,0:T(8,128)(2,1)S(1)}, u32[]{:S(2)}, u32[]{:S(2)}) collective-permute-start(bf16[1280,256]{1,0:T(8,128)(2,1)S(1)} %all_gather.33.mine), channel_id=1, source_target_pairs={{0,8},{8,0},{1,9},{9,1},{2,10},{10,2},{3,11},{11,3},{4,12},{12,4},... | collective-permute-start | bytes 1966088 | tf_op jit(solution)/shard_map/keys_values/ppermute | solution.py:34
  70.5 7.0 %copy-start.4 = (f32[128]{0:T(128)S(1)}, f32[128]{0:T(128)}, u32[]{:S(2)}) copy-start(f32[128]{0:T(128)} %param.9) | copy-start | bytes 1540
  70.5 39.8 %copy-start.5 = (f32[128]{0:T(128)S(1)}, f32[128]{0:T(128)}, u32[]{:S(2)}) copy-start(f32[128]{0:T(128)} %param.8) | copy-start | bytes 1540
  100.9 22.2 %collective-permute-start.2 = (bf16[512,256]{1,0:T(8,128)(2,1)S(1)}, bf16[512,256]{1,0:T(8,128)(2,1)S(1)}, u32[]{:S(2)}, u32[]{:S(2)}) collective-permute-start(bf16[512,256]{1,0:T(8,128)(2,1)S(1)} %all_gather.36.refs_0_), channel_id=1, source_target_pairs={{0,240},{16,0},{32,16},{48,32},{64,48},{80,64},{96,80},{112,96},{1... | collective-permute-start | bytes 786440 | tf_op jit(solution)/shard_map/keys_values/ppermute | solution.py:38
  105.4 17.7 %collective-permute-start.3 = (bf16[512,256]{1,0:T(8,128)(2,1)S(1)}, bf16[512,256]{1,0:T(8,128)(2,1)S(1)}, u32[]{:S(2)}, u32[]{:S(2)}) collective-permute-start(bf16[512,256]{1,0:T(8,128)(2,1)S(1)} %all_gather.36.refs_0_), channel_id=1, source_target_pairs={{0,16},{16,32},{32,48},{48,64},{64,80},{80,96},{96,112},{112,128},... | collective-permute-start | bytes 786440 | tf_op jit(solution)/shard_map/keys_values/ppermute | solution.py:38
  107.4 15.8 %collective-permute-start.4 = (bf16[512,256]{1,0:T(8,128)(2,1)S(1)}, bf16[512,256]{1,0:T(8,128)(2,1)S(1)}, u32[]{:S(2)}, u32[]{:S(2)}) collective-permute-start(bf16[512,256]{1,0:T(8,128)(2,1)S(1)} %all_gather.36.refs_0_), channel_id=1, source_target_pairs={{0,224},{8,40},{16,240},{24,56},{32,0},{40,72},{48,16},{56,88},{64... | collective-permute-start | bytes 786440 | tf_op jit(solution)/shard_map/keys_values/ppermute | solution.py:47
  110.3 1.7 %copy-start.2 = (bf16[32,160,256]{2,1,0:T(8,128)(2,1)S(1)}, bf16[32,160,256]{2,1,0:T(8,128)(2,1)}, u32[]{:S(2)}) copy-start(bf16[32,160,256]{2,1,0:T(8,128)(2,1)} %all-gather.6.cloned.1.call-done) | copy-start | bytes 7864324
  129.4 5.6 %collective-permute-start.5 = (bf16[128,640]{1,0:T(8,128)(2,1)S(1)}, bf16[128,640]{1,0:T(8,128)(2,1)S(1)}, u32[]{:S(2)}, u32[]{:S(2)}) collective-permute-start(bf16[128,640]{1,0:T(8,128)(2,1)S(1)} %fold.1.refs_4_), channel_id=1, source_target_pairs={{0,256},{1,257},{2,258},{3,259},{4,260},{5,261},{6,262},{7,263},{8... | collective-permute-start | bytes 491528 | tf_op jit(solution)/shard_map/context/ppermute | solution.py:353
Sparse Core Ops, SparseCore 0:
  23.9 77.0 all-gather.5
